TPU v7x, 512 devices: a whole 4x4x16 slice. The times are simulated.
512 devices in a mesh: modes: 32 (over z, core), dom: 16 (over y, x).
Axes of the slice: x: 4, y: 4, z: 16, core: 2. Of those that a mesh axis runs over, the one named last changes fastest.
Arguments:
- plane_load: float32 [512, 512, 256], P('modes', 'dom'), may hold values from -5 to 5, as said below
- iterate: float32 [256, 2, 512, 256], P('modes', None, 'dom'), may hold values from -0.5 to 0.5, as said below
- helmholtz: float32 [256], P('modes'), may hold values from 0.02 to 0.5
- coarse_factor: float32 [256, 2640, 264], P('modes', 'dom'), as said below
Outputs:
- residual: float32 [256, 2, 512, 256], P('modes', None, 'dom')
- correction: float32 [256, 2, 512, 256], P('modes', None, 'dom')
Inputs may be any that keep to these rules, and one draw needn't show every extreme that they name: `plane_load`: copies of one node in element-local storage are equal. `iterate`: copies of one node in element-local storage are equal. `coarse_factor`: the row of a vertex of a separator line of level L is zero in the columns of lower levels; line 4 of partition p repeats line 0 of partition p + 1 (mod the partitions) on the columns the two share.
All inputs are finite; a program needn't handle non-finite values.
Results may differ from a plain program's by a relative error of at most 0.0001.
Values sent between devices are 32-bit elements; how exact they have to be, the bound alone decides.
No kernel may reach another device: no remote copies, remote signals or barrier semaphores. Data moves between devices by JAX's collectives and lax.ppermute only.
A program may use at most 64 MiB of HBM per device.

v0:
```python
import math

import jax
import jax.numpy as jnp
import numpy as np
from jax import lax
from jax.sharding import PartitionSpec as P

NODES = 8
OV = 1


PRECISE = lax.Precision.HIGHEST


def extended(array, sides, width):
    for axis, dim in sides:
        count, length = (lax.axis_size(axis), array.shape[dim])
        up = [(i, (i + 1) % count) for i in range(count)]
        down = [(j, i) for i, j in up]
        last = lax.slice_in_dim(array, length - width, length, axis=dim)
        leading = lax.slice_in_dim(array, 0, width, axis=dim)
        before = lax.ppermute(last, axis, up)
        after = lax.ppermute(leading, axis, down)
        array = jnp.concatenate([before, array, after], axis=dim)
    return array


def partner_2(array, axis, bit):
    return lax.ppermute(array, axis, [(i, i ^ 1 << bit) for i in range(lax.axis_size(axis))])


def legendre_pair(degree, points):
    p_prev = np.ones(points.shape)
    p_now = points * 1.0
    for order in range(2, degree + 1):
        p_next = ((2 * order - 1) * points * p_now - (order - 1) * p_prev) / order
        p_prev = p_now
        p_now = p_next
    return (p_now, p_prev)


def gll_tables(node_count):
    degree = node_count - 1
    grid = np.cos(np.pi * np.arange(node_count) / degree)
    for sweep in range(80):
        p_now, p_prev = legendre_pair(degree, grid)
        grid = grid - (grid * p_now - p_prev) / (node_count * p_now)
    points = grid[::-1] * 1.0
    values = legendre_pair(degree, points)[0]
    weights = 2.0 / (degree * (degree + 1) * values**2)
    identity = np.eye(node_count)
    differ = points[:, None] - points[None, :] + identity
    derivative = (1.0 - identity) * values[:, None] / (values[None, :] * differ)
    corner_value = degree * (degree + 1) / 4.0
    derivative = (
        derivative
        - corner_value * np.outer(identity[0], identity[0])
        + corner_value * np.outer(identity[degree], identity[degree])
    )
    stiffness = derivative.T @ (weights[:, None] * derivative)
    return (points, weights, stiffness)


def jacobi_eigen(matrix):
    order_n = matrix.shape[0]
    current = matrix * 1.0
    vectors = np.eye(order_n)
    for sweep in range(30):
        for first in range(order_n):
            for second in range(first + 1, order_n):
                angle = 0.5 * math.atan2(
                    2.0 * float(current[first, second]),
                    float(current[second, second] - current[first, first]),
                )
                rotation = np.eye(order_n)
                rotation[first, first] = math.cos(angle)
                rotation[second, second] = math.cos(angle)
                rotation[first, second] = math.sin(angle)
                rotation[second, first] = -math.sin(angle)
                current = rotation.T @ current @ rotation
                vectors = vectors @ rotation
    return (np.array([current[place, place] for place in range(order_n)]), vectors)


def assemble(element_count, weights, stiffness):
    node_total = (NODES - 1) * element_count + 1
    stiff_global = np.zeros((node_total, node_total))
    mass_global = np.zeros(node_total)
    for element in range(element_count):
        offset = (NODES - 1) * element
        stiff_global[offset : offset + NODES, offset : offset + NODES] += stiffness
        mass_global[offset : offset + NODES] += weights
    return (stiff_global, mass_global)


def patch_tables(has_left, has_right, weights, stiffness):
    stiff_global, mass_global = assemble(1 + has_left + has_right, weights, stiffness)
    own_start = (NODES - 1) * has_left
    indices = np.arange(own_start - OV * has_left, own_start + NODES + OV * has_right)
    patch_len = NODES + 2 * OV
    front_pad = OV * (1 - has_left)
    span = indices.shape[0]
    kpatch = np.zeros((patch_len, patch_len))
    kpatch[front_pad : front_pad + span, front_pad : front_pad + span] = stiff_global[indices][
        :, indices
    ]
    mpatch = np.ones(patch_len)
    mpatch[front_pad : front_pad + span] = mass_global[indices]
    scaling = 1.0 / np.sqrt(mpatch)
    eigval, eigvec = jacobi_eigen(scaling[:, None] * kpatch * scaling[None, :])
    return (np.maximum(eigval, 0.0), scaling[:, None] * eigvec)


def x_tables(element_count, weights, stiffness):
    eigval, eigvec = patch_tables(1, 1, weights, stiffness)
    patch_len = NODES + 2 * OV
    forward = np.zeros((element_count * patch_len, element_count * NODES + 2 * OV + 2))
    backward = np.zeros((element_count * NODES, element_count * patch_len))
    node_place = np.arange(NODES)
    halves = np.where((node_place == 0) | (node_place == NODES - 1), 0.5, 1.0)
    for element in range(element_count):
        rows_here = slice(element * patch_len, (element + 1) * patch_len)
        for position in range(patch_len):
            column = NODES * element + position + int(position >= OV) + int(position >= OV + NODES)
            forward[rows_here, column] = eigvec[position]
        backward[NODES * element : NODES * (element + 1), rows_here] = (
            halves[:, None] * eigvec[OV : OV + NODES]
        )
    return (forward, backward, np.tile(eigval, element_count))


def y_tables(element_count, weights, stiffness):
    patch_len = NODES + 2 * OV
    forward = np.zeros((element_count * patch_len, element_count * NODES))
    backward = np.zeros((element_count * NODES, element_count * patch_len))
    eigen_parts = []
    for element in range(element_count):
        has_left = int(element > 0)
        has_right = int(element < element_count - 1)
        eigval, eigvec = patch_tables(has_left, has_right, weights, stiffness)
        rows_here = slice(element * patch_len, (element + 1) * patch_len)
        for position in range(patch_len):
            outside = position < OV and has_left == 0 or (position >= OV + NODES and has_right == 0)
            if not outside:
                column = (
                    NODES * element
                    + position
                    - OV
                    - 1
                    + int(position >= OV)
                    + int(position >= OV + NODES)
                )
                forward[rows_here, column] = eigvec[position]
        node_place = np.arange(NODES)
        halves = np.where(
            node_place == 0,
            1.0 - 0.5 * has_left,
            np.where(node_place == NODES - 1, 1.0 - 0.5 * has_right, 1.0),
        )
        backward[NODES * element : NODES * (element + 1), rows_here] = (
            halves[:, None] * eigvec[OV : OV + NODES]
        )
        eigen_parts.append(eigval)
    return (forward, backward, np.concatenate(eigen_parts))


def multiplicity(element_count, periodic):
    positions = np.arange(element_count * NODES)
    node_place = positions % NODES
    factors = np.where((node_place == 0) | (node_place == NODES - 1), 0.5, 1.0)
    if not periodic:
        factors = np.where(
            (positions == 0) | (positions == element_count * NODES - 1), 1.0, factors
        )
    return factors


def hat_tables(element_count, points, periodic):
    prolong = np.zeros((element_count + 1, element_count * NODES))
    for element in range(element_count):
        prolong[element, NODES * element : NODES * (element + 1)] = (1.0 - points) / 2.0
        prolong[element + 1, NODES * element : NODES * (element + 1)] = (1.0 + points) / 2.0
    return (prolong, prolong * multiplicity(element_count, periodic)[None, :])


def as_table(values):
    return jnp.asarray(values, jnp.float32)


def fourier_table(planes_total):
    wavenumber = np.arange(planes_total // 2)[:, None]
    plane_index = np.arange(planes_total)[None, :]
    phase_angle = 2.0 * np.pi * (wavenumber * plane_index % planes_total) / planes_total
    dft_rows = np.stack([np.cos(phase_angle), -np.sin(phase_angle)], axis=1) / math.sqrt(
        planes_total
    )
    return as_table(dft_rows.reshape(planes_total, planes_total))


def spectra(block_piece, dft_matrix):
    mixed_modes = jnp.matmul(
        dft_matrix, block_piece.reshape(block_piece.shape[0], -1), precision=PRECISE
    )
    return mixed_modes.reshape((block_piece.shape[0] // 2, 2) + block_piece.shape[1:])


def element_apply(nodal_field, coefficient, weights, stiffness):
    row_count = nodal_field.shape[-2]
    columns = nodal_field.shape[-1]
    blocks = nodal_field.reshape(nodal_field.shape[:-2] + (row_count // NODES, NODES, columns))
    along_x = jnp.einsum(
        "ip,...eph->...eih", as_table(stiffness), blocks, precision=PRECISE
    ).reshape(nodal_field.shape)
    along_y = jnp.matmul(
        nodal_field, as_table(np.kron(np.eye(columns // NODES), stiffness)), precision=PRECISE
    )
    weight_x = as_table(np.tile(weights, row_count // NODES))[:, None]
    weight_y = as_table(np.tile(weights, columns // NODES))[None, :]
    return along_x * weight_y + weight_x * along_y + coefficient * weight_x * weight_y * nodal_field


def pair_rows(nodal_field, before, following):
    node_place = jnp.arange(nodal_field.shape[2]) % NODES
    return (
        nodal_field
        + jnp.where((node_place == 0)[:, None], before, 0.0)
        + jnp.where((node_place == NODES - 1)[:, None], following, 0.0)
    )


def pair_columns(nodal_field):
    count_y = nodal_field.shape[-1]
    column_id = jnp.arange(count_y)
    zeros_col = jnp.zeros(nodal_field.shape[:-1] + (1,), nodal_field.dtype)
    before = jnp.concatenate([zeros_col, nodal_field[..., :-1]], axis=-1)
    following = jnp.concatenate([nodal_field[..., 1:], zeros_col], axis=-1)
    first_node = (column_id % NODES == 0) & (column_id > 0)
    last_node = (column_id % NODES == NODES - 1) & (column_id < count_y - 1)
    return nodal_field + jnp.where(first_node, before, 0.0) + jnp.where(last_node, following, 0.0)


def copy_sum(nodal_field):
    widened = extended(nodal_field, (("dom", 2),), 1)
    return pair_columns(pair_rows(nodal_field, widened[:, :, :-2], widened[:, :, 2:]))


def patch_solve(residual_ext, element_count, helmholtz, weights, stiffness):
    columns = residual_ext.shape[3]
    forward_np, backward_np, eigen_np = x_tables(element_count, weights, stiffness)
    forward_npy, backward_npy, eigen_npy = y_tables(columns // NODES, weights, stiffness)
    section_y = jnp.matmul(residual_ext, as_table(forward_npy).T, precision=PRECISE)
    spectral = jnp.einsum("px,mcxq->mcpq", as_table(forward_np), section_y, precision=PRECISE)
    denominators = (
        as_table(eigen_np)[None, :, None]
        + as_table(eigen_npy)[None, None, :]
        + helmholtz[:, None, None]
    )
    spectral = spectral / denominators[:, None]
    local_part = jnp.einsum("xp,mcpq->mcxq", as_table(backward_np), spectral, precision=PRECISE)
    return jnp.matmul(local_part, as_table(backward_npy).T, precision=PRECISE)


def shards(plane_load, iterate, helmholtz, coarse_factor):
    points, weights, stiffness = gll_tables(NODES)
    rows_local = iterate.shape[2]
    columns = iterate.shape[3]
    element_count = rows_local // NODES
    planes_total = plane_load.shape[0] * lax.axis_size("modes")
    dft_matrix = fourier_table(planes_total)
    coefficient = helmholtz[:, None, None, None]
    mode_loads = lax.all_to_all(
        spectra(
            lax.all_to_all(plane_load, "modes", split_axis=1, concat_axis=0, tiled=True), dft_matrix
        ),
        "modes",
        split_axis=0,
        concat_axis=2,
        tiled=True,
    )
    applied = copy_sum(element_apply(iterate, coefficient, weights, stiffness))
    residual = mode_loads - applied
    residual_ext = extended(residual, (("dom", 2),), OV + 1)
    schwarz = copy_sum(patch_solve(residual_ext, element_count, helmholtz, weights, stiffness))
    prolong_npx, restrict_npx = hat_tables(element_count, points, True)
    prolong_npy, restrict_npy = hat_tables(columns // NODES, points, False)
    line_size = columns // NODES + 1
    coarse_load = jnp.einsum("ax,mcxy->mcay", as_table(restrict_npx), residual, precision=PRECISE)
    coarse_load = jnp.matmul(coarse_load, as_table(restrict_npy).T, precision=PRECISE)
    coarse_load = coarse_load.reshape(coarse_load.shape[0], 2, (element_count + 1) * line_size)
    partial_value = jnp.einsum("mrk,mcr->mck", coarse_factor, coarse_load, precision=PRECISE)
    levels = lax.axis_size("dom").bit_length() - 1
    first_shared = (element_count - 1) * line_size
    totals = partial_value
    for bit_index in range(levels):
        start_col = first_shared + bit_index * line_size
        shared_part = totals[..., start_col:]
        partner = partner_2(shared_part, "dom", bit_index)
        totals = jnp.concatenate([totals[..., :start_col], shared_part + partner], axis=-1)
    coarse_values = jnp.einsum("mrk,mck->mcr", coarse_factor, totals, precision=PRECISE)
    coarse_values = coarse_values.reshape(coarse_values.shape[0], 2, element_count + 1, line_size)
    nodes_x = jnp.einsum("ax,mcay->mcxy", as_table(prolong_npx), coarse_values, precision=PRECISE)
    coarse_nodes = jnp.matmul(nodes_x, as_table(prolong_npy), precision=PRECISE)
    return (residual, schwarz + coarse_nodes)


def solution(mesh):
    return jax.shard_map(
        shards,
        mesh=mesh,
        in_specs=(
            P("modes", "dom", None),
            P("modes", None, "dom", None),
            P("modes"),
            P("modes", "dom", None),
        ),
        out_specs=(P("modes", None, "dom", None), P("modes", None, "dom", None)),
        check_vma=False,
    )
```

profile of v0, /device:TPU:30, one launch (start us, length us, event | category | flops | bytes accessed | tf_op | source)
XLA Modules:
  0.0 151.1 jit_solution(10473571702285447195)
XLA Ops:
  0.7 1.5 copy.40
  2.2 49.0 %all_to_all.33 = f32[16,32,256]{2,0,1:T(8,128)S(1)} all-to-all(f32[16,32,256]{2,0,1:T(8,128)S(1)} %copy.40), channel_id=1, replica_groups=mesh['modes'=32,'dom'=16] {'modes'}, dimensions={1} | all-to-all | bytes 1048576 | tf_op jit(solution)/shard_map/all_to_all | solution.py:274
  53.8 4.6 %all-to-all-start.1 = ((f32[256,2,1,256]{3,1,2,0:T(2,128)}), f32[256,2,1,256]{3,1,2,0:T(2,128)}, u32[]{:S(2)}, u32[]{:S(2)}) async-start(f32[256,2,1,256]{3,1,2,0:T(2,128)} %copy.42), calls=%async_computation.1 | async-start | bytes 1048576 | tf_op jit(solution)/shard_map/all_to_all | solution.py:272
  59.9 2.0 %collective-permute-start = (f32[8,2,1,256]{3,2,1,0:T(1,128)S(1)}, f32[8,2,1,256]{3,2,1,0:T(1,128)S(1)}, u32[]{:S(2)}, u32[]{:S(2)}) collective-permute-start(f32[8,2,1,256]{3,2,1,0:T(1,128)S(1)} %get-tuple-element.10), channel_id=1, source_target_pairs={{0,1},{1,2},{2,3},{3,4},{4,5},{5,6},{6,7},{7,8},{8,9},{9,10},{10,1... | collective-permute-start | bytes 49160 | tf_op jit(solution)/shard_map/ppermute | solution.py:23
  61.9 3.8 %collective-permute-start.1 = (f32[8,2,1,256]{3,2,1,0:T(1,128)S(1)}, f32[8,2,1,256]{3,2,1,0:T(1,128)S(1)}, u32[]{:S(2)}, u32[]{:S(2)}) collective-permute-start(f32[8,2,1,256]{3,2,1,0:T(1,128)S(1)} %get-tuple-element.11), channel_id=1, source_target_pairs={{1,0},{2,1},{3,2},{4,3},{5,4},{6,5},{7,6},{8,7},{9,8},{10,9},{11,1... | collective-permute-start | bytes 49160 | tf_op jit(solution)/shard_map/ppermute | solution.py:24
  65.8 5.1 %collective-permute-done.1 = f32[8,2,1,256]{3,2,1,0:T(1,128)S(1)} collective-permute-done((f32[8,2,1,256]{3,2,1,0:T(1,128)S(1)}, f32[8,2,1,256]{3,2,1,0:T(1,128)S(1)}, u32[]{:S(2)}, u32[]{:S(2)}) %collective-permute-start.1) | collective-permute-done | bytes 16416 | tf_op jit(solution)/shard_map/ppermute | solution.py:24
  72.3 20.1 %all-to-all-done.1 = f32[256,2,1,256]{3,1,2,0:T(2,128)} async-done(((f32[256,2,1,256]{3,1,2,0:T(2,128)}), f32[256,2,1,256]{3,1,2,0:T(2,128)}, u32[]{:S(2)}, u32[]{:S(2)}) %all-to-all-start.1) | async-done | bytes 524320 | tf_op jit(solution)/shard_map/all_to_all | solution.py:272
  92.4 2.0 %bitcast_subtract_fusion = f32[8,2,32,256]{3,2,1,0:T(8,128)S(1)} fusion(f32[32,8,2,1,256]{4,2,1,0,3:T(2,128)} %bitcast.3, f32[8,2,32,255]{3,2,1,0:T(8,128)} %get-tuple-element.9, f32[8,2,32,255]{3,2,1,0:T(8,128)} %get-tuple-element.8, pred[256]{0:T(512)(128)(4,1)S(1)} %get-tuple-element.14, pred[256]{0:T(512)(128)(4,1)S(1)} %get-tuple-element.15, ...), kind=kLoop, calls=%fused_computation.35 | loop fusion | flops 1441792 | bytes 2650688 | tf_op jit(solution)/shard_map/sub | solution.py:282
  95.2 1.6 %fusion.2 = f32[8,2,264]{2,1,0:T(2,128)S(1)} fusion(f32[8,165,264]{2,0,1:T(8,128)S(1)} %copy-done, f32[8,2,165]{2,0,1:T(8,128)S(1)} %reshape.98), kind=kOutput, calls=%fused_computation.2 | convolution fusion | flops 8363520 | bytes 1421376 | tf_op jit(solution)/shard_map/mrk,mcr->mck/dot_general | solution.py:291
  96.8 2.9 %collective-permute-start.6 = (f32[8,2,165]{2,1,0:T(2,128)S(1)}, f32[8,2,165]{2,1,0:T(2,128)S(1)}, u32[]{:S(2)}, u32[]{:S(2)}) collective-permute-start(f32[8,2,165]{2,1,0:T(2,128)S(1)} %slice.103), channel_id=1, source_target_pairs={{0,1},{1,0},{2,3},{3,2},{4,5},{5,4},{6,7},{7,6},{8,9},{9,8},{10,11... | collective-permute-start | bytes 31688 | tf_op jit(solution)/shard_map/ppermute | solution.py:30
  99.8 2.8 %collective-permute-done.6 = f32[8,2,165]{2,1,0:T(2,128)S(1)} collective-permute-done((f32[8,2,165]{2,1,0:T(2,128)S(1)}, f32[8,2,165]{2,1,0:T(2,128)S(1)}, u32[]{:S(2)}, u32[]{:S(2)}) %collective-permute-start.6) | collective-permute-done | bytes 10592 | tf_op jit(solution)/shard_map/ppermute | solution.py:30
  102.8 3.3 %collective-permute-start.7 = (f32[8,2,132]{2,1,0:T(2,128)S(1)}, f32[8,2,132]{2,1,0:T(2,128)S(1)}, u32[]{:S(2)}, u32[]{:S(2)}) collective-permute-start(f32[8,2,132]{2,1,0:T(2,128)S(1)} %slice.104), channel_id=1, source_target_pairs={{0,2},{1,3},{2,0},{3,1},{4,6},{5,7},{6,4},{7,5},{8,10},{9,11},{10,... | collective-permute-start | bytes 25352 | tf_op jit(solution)/shard_map/ppermute | solution.py:30
  106.2 3.7 %collective-permute-done.7 = f32[8,2,132]{2,1,0:T(2,128)S(1)} collective-permute-done((f32[8,2,132]{2,1,0:T(2,128)S(1)}, f32[8,2,132]{2,1,0:T(2,128)S(1)}, u32[]{:S(2)}, u32[]{:S(2)}) %collective-permute-start.7) | collective-permute-done | bytes 8480 | tf_op jit(solution)/shard_map/ppermute | solution.py:30
  110.1 2.6 %collective-permute-start.8 = (f32[8,2,99]{2,1,0:T(2,128)S(1)}, f32[8,2,99]{2,1,0:T(2,128)S(1)}, u32[]{:S(2)}, u32[]{:S(2)}) collective-permute-start(f32[8,2,99]{2,1,0:T(2,128)S(1)} %slice.105), channel_id=1, source_target_pairs={{0,4},{1,5},{2,6},{3,7},{4,0},{5,1},{6,2},{7,3},{8,12},{9,13},{10,... | collective-permute-start | bytes 19016 | tf_op jit(solution)/shard_map/ppermute | solution.py:30
  112.8 2.9 %collective-permute-start.2 = (f32[8,2,2,256]{3,2,1,0:T(2,128)S(1)}, f32[8,2,2,256]{3,2,1,0:T(2,128)S(1)}, u32[]{:S(2)}, u32[]{:S(2)}) collective-permute-start(f32[8,2,2,256]{3,2,1,0:T(2,128)S(1)} %get-tuple-element.6), channel_id=1, source_target_pairs={{0,1},{1,2},{2,3},{3,4},{4,5},{5,6},{6,7},{7,8},{8,9},{9,10},{10,1... | collective-permute-start | bytes 98312 | tf_op jit(solution)/shard_map/ppermute | solution.py:23
  115.6 3.0 %collective-permute-start.3 = (f32[8,2,2,256]{3,2,1,0:T(2,128)S(1)}, f32[8,2,2,256]{3,2,1,0:T(2,128)}, u32[]{:S(2)}, u32[]{:S(2)}) collective-permute-start(f32[8,2,2,256]{3,2,1,0:T(2,128)S(1)} %get-tuple-element.7), channel_id=1, source_target_pairs={{1,0},{2,1},{3,2},{4,3},{5,4},{6,5},{7,6},{8,7},{9,8},{10,9},{11,1... | collective-permute-start | bytes 98312 | tf_op jit(solution)/shard_map/ppermute | solution.py:24
  118.8 3.3 %collective-permute-start.9 = (f32[8,2,66]{2,1,0:T(2,128)S(1)}, f32[8,2,66]{2,1,0:T(2,128)S(1)}, u32[]{:S(2)}, u32[]{:S(2)}) collective-permute-start(f32[8,2,66]{2,1,0:T(2,128)S(1)} %slice.106), channel_id=1, source_target_pairs={{0,8},{1,9},{2,10},{3,11},{4,12},{5,13},{6,14},{7,15},{8,0},{9,1},... | collective-permute-start | bytes 12680 | tf_op jit(solution)/shard_map/ppermute | solution.py:30
  122.2 3.6 %collective-permute-done.9 = f32[8,2,66]{2,1,0:T(2,128)S(1)} collective-permute-done((f32[8,2,66]{2,1,0:T(2,128)S(1)}, f32[8,2,66]{2,1,0:T(2,128)S(1)}, u32[]{:S(2)}, u32[]{:S(2)}) %collective-permute-start.9) | collective-permute-done | bytes 4256 | tf_op jit(solution)/shard_map/ppermute | solution.py:30
  125.9 2.4 %fusion = f32[8,2,165]{2,1,0:T(2,128)S(1)} fusion(f32[8,165,264]{2,0,1:T(8,128)S(1)} %copy-done, f32[8,2,99]{2,1,0:T(2,128)S(1)} %slice_add_fusion.1, f32[8,2,165]{2,1,0:T(2,128)S(1)} %fusion.34, f32[8,2,66]{2,1,0:T(2,128)S(1)} %slice_add_fusion), kind=kOutput, calls=%fused_computation | convolution fusion | flops 8380416 | bytes 1425600 | tf_op jit(solution)/shard_map/mrk,mck->mcr/dot_general | solution.py:300
  128.4 2.0 %fusion.9 = f32[8,2,36,320]{3,2,1,0:T(8,128)S(1)} fusion(f32[320,256,1,1]{1,0,3,2:T(8,128)S(1)} %copy-done.5, f32[8,2,2,256]{3,2,1,0:T(2,128)} %collective-permute-done.3, f32[8,2,32,256]{3,2,1,0:T(8,128)S(1)} %bitcast_subtract_fusion, f32[8,2,2,256]{3,2,1,0:T(2,128)S(1)} %collective-permute-done.2), kind=kOutput, calls=%fused_computation.17 | convolution fusion | flops 566525952 | bytes 1654784 | tf_op jit(solution)/shard_map/dot_general | solution.py:252
  130.4 1.7 %fusion.4 = f32[8,2,40,320]{3,2,1,0:T(8,128)S(1)} fusion(f32[8,2,36,320]{3,2,1,0:T(8,128)S(1)} %fusion.9, f32[40,36,1,1]{1,0,3,2:T(8,128)} %constant.110, f32[8,40,320]{2,1,0:T(8,128)S(1)} %broadcast_add_fusion), kind=kOutput, calls=%fused_computation.5 | convolution fusion | flops 88678400 | bytes 1971840 | tf_op jit(solution)/shard_map/px,mcxq->mcpq/dot_general | solution.py:253
  134.1 6.2 %collective-permute-start.4 = (f32[8,2,1,256]{3,2,1,0:T(1,128)S(1)}, f32[8,2,1,256]{3,2,1,0:T(1,128)S(1)}, u32[]{:S(2)}, u32[]{:S(2)}) collective-permute-start(f32[8,2,1,256]{3,2,1,0:T(1,128)S(1)} %get-tuple-element.4), channel_id=1, source_target_pairs={{0,1},{1,2},{2,3},{3,4},{4,5},{5,6},{6,7},{7,8},{8,9},{9,10},{10,1... | collective-permute-start | bytes 49160 | tf_op jit(solution)/shard_map/ppermute | solution.py:23
  140.3 1.9 %collective-permute-start.5 = (f32[8,2,1,256]{3,2,1,0:T(1,128)S(1)}, f32[8,2,1,256]{3,2,1,0:T(1,128)S(1)}, u32[]{:S(2)}, u32[]{:S(2)}) collective-permute-start(f32[8,2,1,256]{3,2,1,0:T(1,128)S(1)} %get-tuple-element.5), channel_id=1, source_target_pairs={{1,0},{2,1},{3,2},{4,3},{5,4},{6,5},{7,6},{8,7},{9,8},{10,9},{11,1... | collective-permute-start | bytes 49160 | tf_op jit(solution)/shard_map/ppermute | solution.py:24
  142.7 6.6 %collective-permute-done.5 = f32[8,2,1,256]{3,2,1,0:T(1,128)S(1)} collective-permute-done((f32[8,2,1,256]{3,2,1,0:T(1,128)S(1)}, f32[8,2,1,256]{3,2,1,0:T(1,128)S(1)}, u32[]{:S(2)}, u32[]{:S(2)}) %collective-permute-start.5) | collective-permute-done | bytes 16416 | tf_op jit(solution)/shard_map/ppermute | solution.py:24
  (89 shorter events, 11.1 us)
Async XLA Ops:
  0.6 94.5 %copy-start = (f32[8,165,264]{2,0,1:T(8,128)S(1)}, f32[8,165,264]{2,0,1:T(8,128)}, u32[]{:S(2)}) copy-start(f32[8,165,264]{2,0,1:T(8,128)} %param.22) | copy-start | bytes 4181764
  0.6 50.9 %copy-start.3 = (f32[256,2,512]{2,0,1:T(8,128)S(1)}, f32[256,2,512]{2,0,1:T(8,128)}, u32[]{:S(2)}) copy-start(f32[256,2,512]{2,0,1:T(8,128)} %constant.106) | copy-start | bytes 3145732
  53.8 38.6 %all-to-all-start.1 = ((f32[256,2,1,256]{3,1,2,0:T(2,128)}), f32[256,2,1,256]{3,1,2,0:T(2,128)}, u32[]{:S(2)}, u32[]{:S(2)}) async-start(f32[256,2,1,256]{3,1,2,0:T(2,128)} %copy.42), calls=%async_computation.1 | async-start | bytes 1048576 | tf_op jit(solution)/shard_map/all_to_all | solution.py:272
  59.9 5.9 %collective-permute-start = (f32[8,2,1,256]{3,2,1,0:T(1,128)S(1)}, f32[8,2,1,256]{3,2,1,0:T(1,128)S(1)}, u32[]{:S(2)}, u32[]{:S(2)}) collective-permute-start(f32[8,2,1,256]{3,2,1,0:T(1,128)S(1)} %get-tuple-element.10), channel_id=1, source_target_pairs={{0,1},{1,2},{2,3},{3,4},{4,5},{5,6},{6,7},{7,8},{8,9},{9,10},{10,1... | collective-permute-start | bytes 49160 | tf_op jit(solution)/shard_map/ppermute | solution.py:23
  61.9 9.0 %collective-permute-start.1 = (f32[8,2,1,256]{3,2,1,0:T(1,128)S(1)}, f32[8,2,1,256]{3,2,1,0:T(1,128)S(1)}, u32[]{:S(2)}, u32[]{:S(2)}) collective-permute-start(f32[8,2,1,256]{3,2,1,0:T(1,128)S(1)} %get-tuple-element.11), channel_id=1, source_target_pairs={{1,0},{2,1},{3,2},{4,3},{5,4},{6,5},{7,6},{8,7},{9,8},{10,9},{11,1... | collective-permute-start | bytes 49160 | tf_op jit(solution)/shard_map/ppermute | solution.py:24
  65.8 28.6 %copy-start.10 = (pred[32]{0:T(512)(128)(4,1)}, pred[32]{0:T(512)(128)(4,1)S(1)}, u32[]{:S(2)}) copy-start(pred[32]{0:T(512)(128)(4,1)S(1)} %get-tuple-element.13) | copy-start | bytes 100
  65.8 28.6 %copy-start.16 = (pred[256]{0:T(512)(128)(4,1)}, pred[256]{0:T(512)(128)(4,1)S(1)}, u32[]{:S(2)}) copy-start(pred[256]{0:T(512)(128)(4,1)S(1)} %get-tuple-element.14) | copy-start | bytes 772
  65.8 28.6 %copy-start.18 = (pred[256]{0:T(512)(128)(4,1)}, pred[256]{0:T(512)(128)(4,1)S(1)}, u32[]{:S(2)}) copy-start(pred[256]{0:T(512)(128)(4,1)S(1)} %get-tuple-element.15) | copy-start | bytes 772
  71.1 23.3 %copy-start.12 = (f32[5,32,1,1]{1,0,3,2:T(8,128)S(1)}, f32[5,32,1,1]{1,0,3,2:T(8,128)}, u32[]{:S(2)}) copy-start(f32[5,32,1,1]{1,0,3,2:T(8,128)} %constant.113) | copy-start | bytes 1924
  72.3 22.6 %copy-start.7 = (f32[33,256,1,1]{1,0,2,3:T(8,128)S(1)}, f32[33,256,1,1]{1,0,2,3:T(8,128)}, u32[]{:S(2)}) copy-start(f32[33,256,1,1]{1,0,2,3:T(8,128)} %constant.114) | copy-start | bytes 101380
  94.4 34.0 %copy-start.1 = (f32[8,2,32,256]{3,2,1,0:T(8,128)}, f32[8,2,32,256]{3,2,1,0:T(8,128)S(1)}, u32[]{:S(2)}) copy-start(f32[8,2,32,256]{3,2,1,0:T(8,128)S(1)} %bitcast_subtract_fusion) | copy-start | bytes 1572868
  96.8 31.7 %copy-start.5 = (f32[320,256,1,1]{1,0,3,2:T(8,128)S(1)}, f32[320,256,1,1]{1,0,3,2:T(8,128)}, u32[]{:S(2)}) copy-start(f32[320,256,1,1]{1,0,3,2:T(8,128)} %constant.109) | copy-start | bytes 983044
  96.8 5.8 %collective-permute-start.6 = (f32[8,2,165]{2,1,0:T(2,128)S(1)}, f32[8,2,165]{2,1,0:T(2,128)S(1)}, u32[]{:S(2)}, u32[]{:S(2)}) collective-permute-start(f32[8,2,165]{2,1,0:T(2,128)S(1)} %slice.103), channel_id=1, source_target_pairs={{0,1},{1,0},{2,3},{3,2},{4,5},{5,4},{6,7},{7,6},{8,9},{9,8},{10,11... | collective-permute-start | bytes 31688 | tf_op jit(solution)/shard_map/ppermute | solution.py:30
  102.8 7.1 %collective-permute-start.7 = (f32[8,2,132]{2,1,0:T(2,128)S(1)}, f32[8,2,132]{2,1,0:T(2,128)S(1)}, u32[]{:S(2)}, u32[]{:S(2)}) collective-permute-start(f32[8,2,132]{2,1,0:T(2,128)S(1)} %slice.104), channel_id=1, source_target_pairs={{0,2},{1,3},{2,0},{3,1},{4,6},{5,7},{6,4},{7,5},{8,10},{9,11},{10,... | collective-permute-start | bytes 25352 | tf_op jit(solution)/shard_map/ppermute | solution.py:30
  110.1 8.6 %collective-permute-start.8 = (f32[8,2,99]{2,1,0:T(2,128)S(1)}, f32[8,2,99]{2,1,0:T(2,128)S(1)}, u32[]{:S(2)}, u32[]{:S(2)}) collective-permute-start(f32[8,2,99]{2,1,0:T(2,128)S(1)} %slice.105), channel_id=1, source_target_pairs={{0,4},{1,5},{2,6},{3,7},{4,0},{5,1},{6,2},{7,3},{8,12},{9,13},{10,... | collective-permute-start | bytes 19016 | tf_op jit(solution)/shard_map/ppermute | solution.py:30
  112.8 15.6 %collective-permute-start.2 = (f32[8,2,2,256]{3,2,1,0:T(2,128)S(1)}, f32[8,2,2,256]{3,2,1,0:T(2,128)S(1)}, u32[]{:S(2)}, u32[]{:S(2)}) collective-permute-start(f32[8,2,2,256]{3,2,1,0:T(2,128)S(1)} %get-tuple-element.6), channel_id=1, source_target_pairs={{0,1},{1,2},{2,3},{3,4},{4,5},{5,6},{6,7},{7,8},{8,9},{9,10},{10,1... | collective-permute-start | bytes 98312 | tf_op jit(solution)/shard_map/ppermute | solution.py:23
  115.6 12.7 %collective-permute-start.3 = (f32[8,2,2,256]{3,2,1,0:T(2,128)S(1)}, f32[8,2,2,256]{3,2,1,0:T(2,128)}, u32[]{:S(2)}, u32[]{:S(2)}) collective-permute-start(f32[8,2,2,256]{3,2,1,0:T(2,128)S(1)} %get-tuple-element.7), channel_id=1, source_target_pairs={{1,0},{2,1},{3,2},{4,3},{5,4},{6,5},{7,6},{8,7},{9,8},{10,9},{11,1... | collective-permute-start | bytes 98312 | tf_op jit(solution)/shard_map/ppermute | solution.py:24
  118.8 7.0 %collective-permute-start.9 = (f32[8,2,66]{2,1,0:T(2,128)S(1)}, f32[8,2,66]{2,1,0:T(2,128)S(1)}, u32[]{:S(2)}, u32[]{:S(2)}) collective-permute-start(f32[8,2,66]{2,1,0:T(2,128)S(1)} %slice.106), channel_id=1, source_target_pairs={{0,8},{1,9},{2,10},{3,11},{4,12},{5,13},{6,14},{7,15},{8,0},{9,1},... | collective-permute-start | bytes 12680 | tf_op jit(solution)/shard_map/ppermute | solution.py:30
  132.2 17.1 %copy-start.11 = (pred[32]{0:T(512)(128)(4,1)S(1)}, pred[32]{0:T(512)(128)(4,1)}, u32[]{:S(2)}) copy-start(pred[32]{0:T(512)(128)(4,1)} %copy-done.10) | copy-start | bytes 100
  134.1 15.6 %copy-start.8 = (f32[33,256,1,1]{1,0,3,2:T(8,128)S(1)}, f32[33,256,1,1]{1,0,3,2:T(8,128)}, u32[]{:S(2)}) copy-start(f32[33,256,1,1]{1,0,3,2:T(8,128)} %constant.116) | copy-start | bytes 101380
  134.1 15.6 %copy-start.17 = (pred[256]{0:T(512)(128)(4,1)S(1)}, pred[256]{0:T(512)(128)(4,1)}, u32[]{:S(2)}) copy-start(pred[256]{0:T(512)(128)(4,1)} %copy-done.16) | copy-start | bytes 772
  134.1 15.6 %copy-start.19 = (pred[256]{0:T(512)(128)(4,1)S(1)}, pred[256]{0:T(512)(128)(4,1)}, u32[]{:S(2)}) copy-start(pred[256]{0:T(512)(128)(4,1)} %copy-done.18) | copy-start | bytes 772
  134.1 8.6 %collective-permute-start.4 = (f32[8,2,1,256]{3,2,1,0:T(1,128)S(1)}, f32[8,2,1,256]{3,2,1,0:T(1,128)S(1)}, u32[]{:S(2)}, u32[]{:S(2)}) collective-permute-start(f32[8,2,1,256]{3,2,1,0:T(1,128)S(1)} %get-tuple-element.4), channel_id=1, source_target_pairs={{0,1},{1,2},{2,3},{3,4},{4,5},{5,6},{6,7},{7,8},{8,9},{9,10},{10,1... | collective-permute-start | bytes 49160 | tf_op jit(solution)/shard_map/ppermute | solution.py:23
  140.3 9.0 %collective-permute-start.5 = (f32[8,2,1,256]{3,2,1,0:T(1,128)S(1)}, f32[8,2,1,256]{3,2,1,0:T(1,128)S(1)}, u32[]{:S(2)}, u32[]{:S(2)}) collective-permute-start(f32[8,2,1,256]{3,2,1,0:T(1,128)S(1)} %get-tuple-element.5), channel_id=1, source_target_pairs={{1,0},{2,1},{3,2},{4,3},{5,4},{6,5},{7,6},{8,7},{9,8},{10,9},{11,1... | collective-permute-start | bytes 49160 | tf_op jit(solution)/shard_map/ppermute | solution.py:24
  (11 other events, 66.6 us)
where the time goes:
time: 152 us; the launch traced here: 151 us
  blocking collectives  49 us (32%)
  waiting for transfers between devices  41.9 us (28%)
  starting transfers between devices  36.6 us (24%)
  matrix products  14.1 us (9%)
  local copies, waits for them, and re-layouts  5.1 us (3%)
  other arithmetic  3.11 us (2%)
    all_to_all x1, blocking collectives, shards(): lax.all_to_all(plane_load, 'modes', split_axis=1, concat_axis=0, tiled=True)  49 us
    all_to_all x1, waiting for transfers between devices, shards(): lax.all_to_all(spectra(lax.all_to_all(plane_load, 'modes', split_axis=1,...  20.1 us
    ppermute x4, starting transfers between devices, partner_2(): lax.ppermute(array, axis, [(i, i ^ 1 << bit) for i in range(lax.axis_size...  12.2 us
    ppermute x3, waiting for transfers between devices, extended(): after = lax.ppermute(leading, axis, down)  11.7 us
    ppermute x3, starting transfers between devices, extended(): before = lax.ppermute(last, axis, up)  11.1 us
    ppermute x4, waiting for transfers between devices, partner_2(): lax.ppermute(array, axis, [(i, i ^ 1 << bit) for i in range(lax.axis_size...  10.1 us
    ppermute x3, starting transfers between devices, extended(): after = lax.ppermute(leading, axis, down)  8.69 us
    all_to_all x1, starting transfers between devices, shards(): lax.all_to_all(spectra(lax.all_to_all(plane_load, 'modes', split_axis=1,...  4.62 us
  transfers between devices with their start and end apart: 11, of which 6 were waited for; matrix products, arithmetic and copies ran while one was open for 4% of the time, Pallas kernels for 0%

commit v1 on v0

v1 whole, which is shorter than its diff:
```python
import math

import jax
import jax.numpy as jnp
import numpy as np
from jax import lax
from jax.experimental import pallas as pl
from jax.experimental.pallas import tpu as pltpu
from jax.sharding import PartitionSpec as P

NODES = 8
OV = 1
EXD = 4
UNIQUE = EXD * (NODES - 1)
PATCH = NODES + 2 * OV
LANES = 128
ROWS = 56
CHIPS = 16
FIELDS = 16

F32 = jnp.float32
BF16 = jnp.bfloat16
SIX = lax.Precision.HIGHEST


def legendre_pair(degree, points):
    p_prev = np.ones(points.shape)
    p_now = points * 1.0
    for order in range(2, degree + 1):
        p_next = ((2 * order - 1) * points * p_now - (order - 1) * p_prev) / order
        p_prev = p_now
        p_now = p_next
    return (p_now, p_prev)


def gll_tables(node_count):
    degree = node_count - 1
    grid = np.cos(np.pi * np.arange(node_count) / degree)
    for sweep in range(80):
        p_now, p_prev = legendre_pair(degree, grid)
        grid = grid - (grid * p_now - p_prev) / (node_count * p_now)
    points = grid[::-1] * 1.0
    values = legendre_pair(degree, points)[0]
    weights = 2.0 / (degree * (degree + 1) * values**2)
    identity = np.eye(node_count)
    differ = points[:, None] - points[None, :] + identity
    derivative = (1.0 - identity) * values[:, None] / (values[None, :] * differ)
    corner_value = degree * (degree + 1) / 4.0
    derivative = (
        derivative
        - corner_value * np.outer(identity[0], identity[0])
        + corner_value * np.outer(identity[degree], identity[degree])
    )
    stiffness = derivative.T @ (weights[:, None] * derivative)
    return (points, weights, stiffness)


def jacobi_eigen(matrix):
    order_n = matrix.shape[0]
    current = matrix * 1.0
    vectors = np.eye(order_n)
    for sweep in range(30):
        for first in range(order_n):
            for second in range(first + 1, order_n):
                angle = 0.5 * math.atan2(
                    2.0 * float(current[first, second]),
                    float(current[second, second] - current[first, first]),
                )
                rotation = np.eye(order_n)
                rotation[first, first] = math.cos(angle)
                rotation[second, second] = math.cos(angle)
                rotation[first, second] = math.sin(angle)
                rotation[second, first] = -math.sin(angle)
                current = rotation.T @ current @ rotation
                vectors = vectors @ rotation
    return (np.array([current[place, place] for place in range(order_n)]), vectors)


def assemble(element_count, weights, stiffness):
    node_total = (NODES - 1) * element_count + 1
    stiff_global = np.zeros((node_total, node_total))
    mass_global = np.zeros(node_total)
    for element in range(element_count):
        offset = (NODES - 1) * element
        stiff_global[offset : offset + NODES, offset : offset + NODES] += stiffness
        mass_global[offset : offset + NODES] += weights
    return (stiff_global, mass_global)


def patch_tables(has_left, has_right, weights, stiffness):
    stiff_global, mass_global = assemble(1 + has_left + has_right, weights, stiffness)
    own_start = (NODES - 1) * has_left
    indices = np.arange(own_start - OV * has_left, own_start + NODES + OV * has_right)
    patch_len = NODES + 2 * OV
    front_pad = OV * (1 - has_left)
    span = indices.shape[0]
    kpatch = np.zeros((patch_len, patch_len))
    kpatch[front_pad : front_pad + span, front_pad : front_pad + span] = stiff_global[indices][
        :, indices
    ]
    mpatch = np.ones(patch_len)
    mpatch[front_pad : front_pad + span] = mass_global[indices]
    scaling = 1.0 / np.sqrt(mpatch)
    eigval, eigvec = jacobi_eigen(scaling[:, None] * kpatch * scaling[None, :])
    return (np.maximum(eigval, 0.0), scaling[:, None] * eigvec)


def y_tables(element_count, weights, stiffness):
    patch_len = NODES + 2 * OV
    forward = np.zeros((element_count * patch_len, element_count * NODES))
    backward = np.zeros((element_count * NODES, element_count * patch_len))
    eigen_parts = []
    for element in range(element_count):
        has_left = int(element > 0)
        has_right = int(element < element_count - 1)
        eigval, eigvec = patch_tables(has_left, has_right, weights, stiffness)
        rows_here = slice(element * patch_len, (element + 1) * patch_len)
        for position in range(patch_len):
            outside = position < OV and has_left == 0 or (position >= OV + NODES and has_right == 0)
            if not outside:
                column = (
                    NODES * element
                    + position
                    - OV
                    - 1
                    + int(position >= OV)
                    + int(position >= OV + NODES)
                )
                forward[rows_here, column] = eigvec[position]
        node_place = np.arange(NODES)
        halves = np.where(
            node_place == 0,
            1.0 - 0.5 * has_left,
            np.where(node_place == NODES - 1, 1.0 - 0.5 * has_right, 1.0),
        )
        backward[NODES * element : NODES * (element + 1), rows_here] = (
            halves[:, None] * eigvec[OV : OV + NODES]
        )
        eigen_parts.append(eigval)
    return (forward, backward, np.concatenate(eigen_parts))


def multiplicity(element_count, periodic):
    positions = np.arange(element_count * NODES)
    node_place = positions % NODES
    factors = np.where((node_place == 0) | (node_place == NODES - 1), 0.5, 1.0)
    if not periodic:
        factors = np.where(
            (positions == 0) | (positions == element_count * NODES - 1), 1.0, factors
        )
    return factors


def hat_tables(element_count, points, periodic):
    prolong = np.zeros((element_count + 1, element_count * NODES))
    for element in range(element_count):
        prolong[element, NODES * element : NODES * (element + 1)] = (1.0 - points) / 2.0
        prolong[element + 1, NODES * element : NODES * (element + 1)] = (1.0 + points) / 2.0
    return (prolong, prolong * multiplicity(element_count, periodic)[None, :])


def y_copy_sum(columns):
    table = np.eye(columns)
    for element in range(columns // NODES - 1):
        left = NODES * element + NODES - 1
        table[left, left + 1] = 1.0
        table[left + 1, left] = 1.0
    return table


def halves_of(values):
    head = np.asarray(values, np.float32).astype(jnp.bfloat16)
    rest = (np.asarray(values, np.float32) - head.astype(np.float32)).astype(jnp.bfloat16)
    return np.stack([head, rest])


def fourier_halves(planes_total):
    chips = CHIPS
    z = np.arange(planes_total).reshape(chips, 2, 2, 8).transpose(1, 2, 0, 3)
    k = np.arange(planes_total // 2).reshape(chips, 2, 8).transpose(1, 0, 2)
    phase = (k[:, :, :, None, None, None, None] * z[None, None, None] % planes_total) * (
        2.0 * np.pi / planes_total
    )
    both = np.stack([np.cos(phase), -np.sin(phase)], axis=2) / math.sqrt(planes_total)
    both = both.transpose(4, 0, 1, 2, 3, 5, 6, 7)
    both = both.reshape(2, 2, chips * 16, chips * 16)
    return np.moveaxis(halves_of(both), 0, 2)


def split(values):
    head = values.astype(BF16)
    return head, (values - head.astype(F32)).astype(BF16)


def dot3(left, right_head, right_rest):
    head, rest = split(left)
    out = jnp.dot(head, right_head, preferred_element_type=F32)
    out += jnp.dot(rest, right_head, preferred_element_type=F32)
    return out + jnp.dot(head, right_rest, preferred_element_type=F32)


def lane_index(rows):
    return lax.broadcasted_iota(jnp.int32, (rows, LANES), 1)


def swap_halves(values):
    return pltpu.roll(values, LANES // 2, 1)


def chip_places():
    return [(d, d // 4, d // 2 % 2, d % 2) for d in range(CHIPS)]


def pack_kernel(x_ref, out_ref):
    low = lane_index(8) < LANES // 2
    for d, element, half, side in chip_places():
        lanes = slice(half * LANES, (half + 1) * LANES)
        for step in range(3):
            row = NODES * element + 4 * side + step
            out_ref[d, 16 * step : 16 * step + 16, :] = x_ref[:, row, lanes]
        shared = x_ref[:, NODES * element + 3, lanes]
        first, second = shared[:8], shared[8:]
        if side == 0:
            mixed = jnp.where(low, first, swap_halves(second))
        else:
            mixed = jnp.where(low, swap_halves(first), second)
        out_ref[d, 48:56, :] = mixed


def fourier_kernel(x_ref, table_ref, *out_refs):
    columns = []
    for step in range(3):
        upper = x_ref[:, 16 * step : 16 * step + 8, :].reshape(LANES, LANES)
        lower = x_ref[:, 16 * step + 8 : 16 * step + 16, :].reshape(LANES, LANES)
        columns.append(jnp.concatenate([upper, lower], axis=0))
    mixed = x_ref[:, 48:56, :].reshape(LANES, LANES)
    turned = swap_halves(mixed)
    low = lane_index(LANES) < LANES // 2
    columns.append(
        jnp.concatenate([jnp.where(low, mixed, turned), jnp.where(low, turned, mixed)], axis=0)
    )
    head, rest = split(jnp.concatenate(columns, axis=1))
    low = lane_index(8) < LANES // 2
    for place, out_ref in enumerate(out_refs):
        table_head, table_rest = table_ref[place, 0], table_ref[place, 1]
        out = jnp.dot(table_head, head, preferred_element_type=F32)
        out += jnp.dot(table_head, rest, preferred_element_type=F32)
        out += jnp.dot(table_rest, head, preferred_element_type=F32)
        for d in range(CHIPS):
            for step in range(3):
                out_ref[d, 16 * step : 16 * step + 16, :] = out[
                    16 * d : 16 * d + 16, step * LANES : (step + 1) * LANES
                ]
            last = out[16 * d : 16 * d + 16, 3 * LANES :]
            out_ref[d, 48:56, :] = jnp.where(low, last[:8], last[8:])


def residual_kernel(
    restrict_x, x_ref, applied_ref, factor_ref, restrict_ref, res_ref, up_ref, down_ref, block_ref, own_ref
):
    low = lane_index(8) < LANES // 2
    for d, element, half, side in chip_places():
        lanes = slice(half * LANES, (half + 1) * LANES)
        for step in range(3):
            u = 7 * element + 4 * side + step
            res_ref[u, :, lanes] = x_ref[d, 16 * step : 16 * step + 16, :] - applied_ref[u, :, lanes]
        if side == 0:
            first, second = x_ref[d, 48:56, :], x_ref[d + 1, 48:56, :]
            u = 7 * element + 3
            upper = jnp.where(low, first, swap_halves(second))
            lower = jnp.where(low, swap_halves(first), second)
            res_ref[u, 0:8, lanes] = upper - applied_ref[u, 0:8, lanes]
            res_ref[u, 8:16, lanes] = lower - applied_ref[u, 8:16, lanes]
    for i in range(8):
        up_ref[i] = res_ref[UNIQUE - 8 + i]
    for i in range(9):
        down_ref[i] = res_ref[i]
    lines = []
    for a in range(EXD + 1):
        total = None
        for u in range(UNIQUE):
            if restrict_x[a, u] != 0.0:
                term = res_ref[u] * float(restrict_x[a, u])
                total = term if total is None else total + term
        lines.append(total)
    load = dot3(jnp.concatenate(lines, axis=0), restrict_ref[0], restrict_ref[1])
    line_size = factor_ref.shape[0] // (EXD + 1)
    sums = [jnp.zeros((8, 3 * LANES), F32) for _ in range(2)]
    for a in range(EXD + 1):
        for b in range(line_size):
            row = factor_ref[a * line_size + b]
            for part in range(2):
                at = 16 * a + 8 * part
                sums[part] = sums[part] + load[at : at + 8, b : b + 1] * row
    both = jnp.concatenate(sums, axis=0)
    first, second, third = (both[:, i * LANES : (i + 1) * LANES] for i in range(3))
    own_ref[...] = first
    joined = jnp.where(lane_index(16) < 8, third, first)
    for d in range(CHIPS):
        block_ref[d, 0:16, :] = joined
        block_ref[d, 16:32, :] = second


def patch_kernel(vectors, res_ref, before_ref, after_ref, inverse_ref, forward_ref, backward_ref, out_ref, schwarz_ref):
    columns = res_ref.shape[2]
    width = forward_ref.shape[2]
    rows = jnp.concatenate([before_ref[...], res_ref[...], after_ref[...]], axis=0)
    count = 8 + UNIQUE + 9
    section = dot3(rows.reshape(count * FIELDS, columns), forward_ref[0], forward_ref[1])
    section = section.reshape(count, FIELDS, width)
    weight = np.where((np.arange(NODES) == 0) | (np.arange(NODES) == NODES - 1), 0.5, 1.0)
    inverse = [inverse_ref[p] for p in range(PATCH)]
    faces = [None] * (EXD + 2)
    parts = [None] * (UNIQUE + 1)
    for element in range(-1, EXD + 1):
        start = 8 + 7 * element - 1
        nodes = [section[start + i] for i in range(PATCH)]
        scaled = []
        for p in range(PATCH):
            total = nodes[0] * float(vectors[0, p])
            for i in range(1, PATCH):
                total = total + nodes[i] * float(vectors[i, p])
            scaled.append(total * inverse[p])
        for n in range(NODES):
            if (element == -1 and n < NODES - 1) or (element == EXD and n > 0):
                continue
            total = scaled[0] * float(weight[n] * vectors[OV + n, 0])
            for p in range(1, PATCH):
                total = total + scaled[p] * float(weight[n] * vectors[OV + n, p])
            u = 7 * element + n
            parts[u] = total if parts[u] is None else parts[u] + total
    stacked = jnp.concatenate(parts, axis=0)
    schwarz = dot3(stacked, backward_ref[0], backward_ref[1])
    schwarz_ref[...] = schwarz.reshape(UNIQUE + 1, FIELDS, columns)
    for row in range(EXD * NODES):
        u = 7 * (row // NODES) + row % NODES
        value = res_ref[u] if u < UNIQUE else after_ref[0]
        for part in range(2):
            out_ref[:, part, row, :] = value[8 * part : 8 * part + 8]


def coarse_kernel(points, me_ref, got_ref, own_ref, factor_ref, prolong_ref, schwarz_ref, out_ref):
    me = me_ref[0]
    lane = lane_index(16)
    reach_first = jnp.where(lane < 8, 16, jnp.where(lane < 99, 1, 2))
    reach_second = jnp.where(
        lane < 132 - LANES, 2, jnp.where(lane < 165 - LANES, 4, jnp.where(lane < 198 - LANES, 8, 16))
    )
    first = jnp.zeros((16, LANES), F32)
    second = jnp.zeros((16, LANES), F32)
    for source in range(CHIPS):
        apart = jnp.bitwise_xor(me, source)
        first = first + jnp.where(reach_first > apart, got_ref[source, 0:16, :], 0.0)
        second = second + jnp.where(reach_second > apart, got_ref[source, 16:32, :], 0.0)
    third = jnp.where(lane < 8, first, 0.0)
    first = jnp.where(lane < 8, own_ref[...], first)
    line_size = factor_ref.shape[0] // (EXD + 1)
    lane8 = lane_index(8)
    values = []
    for a in range(EXD + 1):
        lines = [jnp.zeros((8, LANES), F32) for _ in range(2)]
        for b in range(line_size):
            row = factor_ref[a * line_size + b]
            for part in range(2):
                at = slice(8 * part, 8 * part + 8)
                term = row[:, :LANES] * first[at] + row[:, LANES : 2 * LANES] * second[at]
                term = term + row[:, 2 * LANES :] * third[at]
                total = jnp.sum(term, axis=1, keepdims=True)
                lines[part] = jnp.where(lane8 == b, total, lines[part])
        values += lines
    lines = dot3(jnp.concatenate(values, axis=0), prolong_ref[0], prolong_ref[1])
    for row in range(EXD * NODES):
        element, n = row // NODES, row % NODES
        left = lines[16 * element : 16 * element + 16]
        right = lines[16 * element + 16 : 16 * element + 32]
        value = schwarz_ref[7 * element + n]
        value = value + left * float((1.0 - points[n]) / 2.0) + right * float((1.0 + points[n]) / 2.0)
        for part in range(2):
            out_ref[:, part, row, :] = value[8 * part : 8 * part + 8]


def call(kernel, outs, *operands, smem=0, flops=1e6):
    moved = sum(math.prod(o.shape) * o.dtype.itemsize for o in list(operands) + list(outs))
    vmem = pl.BlockSpec(memory_space=pltpu.VMEM)
    return pl.pallas_call(
        kernel,
        out_shape=outs,
        in_specs=[pl.BlockSpec(memory_space=pltpu.SMEM)] * smem + [vmem] * (len(operands) - smem),
        out_specs=[vmem] * len(outs),
        compiler_params=pltpu.CompilerParams(vmem_limit_bytes=32 * 2**20),
        cost_estimate=pl.CostEstimate(
            flops=int(flops), bytes_accessed=int(moved), transcendentals=0
        ),
    )(*operands)


def shape(*dims):
    return jax.ShapeDtypeStruct(dims, F32)


def applied_rows(fields, coefficient, weights, stiffness, columns):
    local = EXD * NODES
    table = np.zeros((UNIQUE + 1, local))
    weight_x = np.zeros(UNIQUE)
    for u in range(UNIQUE):
        element, n = u // 7, u % 7
        table[u, NODES * element : NODES * element + NODES] += stiffness[n]
        if n == 0 and element > 0:
            table[u, NODES * element - NODES : NODES * element] += stiffness[NODES - 1]
        weight_x[u] = weights[n] + (weights[NODES - 1] if n == 0 else 0.0)
    table[UNIQUE, local - NODES :] = stiffness[NODES - 1]
    sums = y_copy_sum(columns)
    weight_y = sums @ np.tile(weights, columns // NODES)
    along_y = np.kron(np.eye(columns // NODES), stiffness) @ sums
    along_x = jnp.einsum("ur,rfy->ufy", jnp.asarray(table, F32), fields, precision=SIX)
    count = lax.axis_size("dom")
    before = lax.ppermute(along_x[UNIQUE], "dom", [(i, (i + 1) % count) for i in range(count)])
    own = fields.reshape(EXD, NODES, FIELDS, columns)[:, : NODES - 1]
    own = own.reshape(UNIQUE, FIELDS, columns)
    turned = jnp.matmul(own, jnp.asarray(along_y, F32), precision=SIX)
    first = jnp.where(jnp.arange(UNIQUE)[:, None, None] == 0, before[None], 0.0)
    wx = jnp.asarray(weight_x, F32)[:, None, None]
    wy = jnp.asarray(weight_y, F32)
    return (along_x[:UNIQUE] + first) * wy + wx * turned + coefficient[:, None] * (wx * wy) * own


def shards(plane_load, iterate, helmholtz, coarse_factor):
    points, weights, stiffness = gll_tables(NODES)
    columns = iterate.shape[3]
    elements_y = columns // NODES
    line_size = elements_y + 1
    planes = plane_load.shape[0]
    planes_total = planes * lax.axis_size("modes")
    count = lax.axis_size("modes")
    cores = [list(range(0, count, 2)), list(range(1, count, 2))]
    core = lax.axis_index("modes") % 2
    partition = lax.axis_index("dom")
    partitions = lax.axis_size("dom")
    up = [(i, (i + 1) % partitions) for i in range(partitions)]
    down = [(j, i) for i, j in up]

    def over_z(blocks):
        return lax.all_to_all(
            blocks, "modes", split_axis=0, concat_axis=0, axis_index_groups=cores, tiled=True
        )

    blocks_shape = shape(CHIPS, ROWS, LANES)
    (packed,) = call(
        pack_kernel, [blocks_shape], plane_load
    )
    planes_here = over_z(packed)

    tables = jnp.asarray(fourier_halves(planes_total))
    send_table = jnp.where(core == 0, tables[0, 1], tables[1, 0])
    keep_table = jnp.where(core == 0, tables[0, 0], tables[1, 1])
    away, kept = call(
        fourier_kernel,
        [blocks_shape, blocks_shape],
        planes_here,
        jnp.stack([send_table, keep_table]),
        flops=8e8,
    )
    back = lax.ppermute(away, "modes", [(i, i ^ 1) for i in range(count)])
    loads = over_z(kept + back)

    coefficient = jnp.tile(helmholtz, 2)
    fields = iterate.transpose(2, 1, 0, 3).reshape(EXD * NODES, FIELDS, columns)
    applied = applied_rows(fields, coefficient, weights, stiffness, columns)
    factor = jnp.pad(coarse_factor.transpose(1, 0, 2), ((0, 0), (0, 0), (0, 3 * LANES - coarse_factor.shape[2])))

    prolong_x, restrict_x = hat_tables(EXD, points, True)
    prolong_y, restrict_y = hat_tables(elements_y, points, False)
    unique_restrict = np.zeros((EXD + 1, UNIQUE))
    for row in range(EXD * NODES - 1):
        unique_restrict[:, 7 * (row // NODES) + row % NODES] += restrict_x[:, row]
    unique_restrict[0, 0] += restrict_x[EXD, EXD * NODES - 1]
    restrict_table = np.zeros((columns, LANES))
    restrict_table[:, :line_size] = restrict_y.T
    residual, to_next, to_last, block, own = call(
        lambda *refs: residual_kernel(unique_restrict, *refs),
        [
            shape(UNIQUE, FIELDS, columns),
            shape(8, FIELDS, columns),
            shape(9, FIELDS, columns),
            shape(CHIPS, 32, LANES),
            shape(16, LANES),
        ],
        loads,
        applied,
        factor,
        jnp.asarray(halves_of(restrict_table)),
        flops=3e7,
    )
    before = lax.ppermute(to_next, "dom", up)
    after = lax.ppermute(to_last, "dom", down)
    sums = lax.all_to_all(block, "dom", split_axis=0, concat_axis=0, tiled=True)

    eigval, eigvec = patch_tables(1, 1, weights, stiffness)
    forward_y, backward_y, eigen_y = y_tables(elements_y, weights, stiffness)
    width = 3 * LANES
    forward_table = np.zeros((columns, width))
    forward_table[:, : forward_y.shape[0]] = forward_y.T
    backward_table = np.zeros((width, columns))
    backward_table[: forward_y.shape[0]] = (y_copy_sum(columns) @ backward_y).T
    eigen_row = np.ones(width)
    eigen_row[: forward_y.shape[0]] = eigen_y
    inverse = 1.0 / (
        jnp.asarray(eigval, F32)[:, None, None]
        + jnp.asarray(eigen_row, F32)[None, None, :]
        + coefficient[None, :, None]
    )
    residual_out, schwarz = call(
        lambda *refs: patch_kernel(eigvec, *refs),
        [shape(8, 2, EXD * NODES, columns), shape(UNIQUE + 1, FIELDS, columns)],
        residual,
        before,
        after,
        inverse,
        jnp.asarray(halves_of(forward_table)),
        jnp.asarray(halves_of(backward_table)),
        flops=8e8,
    )
    prolong_table = np.zeros((LANES, columns))
    prolong_table[:line_size] = prolong_y
    (correction,) = call(
        lambda *refs: coarse_kernel(points, *refs),
        [shape(8, 2, EXD * NODES, columns)],
        partition.astype(jnp.int32).reshape(1),
        sums,
        own,
        factor,
        jnp.asarray(halves_of(prolong_table)),
        schwarz,
        smem=1,
        flops=3e7,
    )
    return (residual_out, correction)


def solution(mesh):
    return jax.shard_map(
        shards,
        mesh=mesh,
        in_specs=(
            P("modes", "dom", None),
            P("modes", None, "dom", None),
            P("modes"),
            P("modes", "dom", None),
        ),
        out_specs=(P("modes", None, "dom", None), P("modes", None, "dom", None)),
        check_vma=False,
    )
```

time: 152 us -> 114 us (0.75)
  the two profiles are of different devices: /device:TPU:30 before, /device:TPU:6 now
where the time goes in v1:
time: 114 us; the launch traced here: 113 us
  waiting for transfers between devices  53.1 us (47%)
  starting transfers between devices  39.7 us (35%)
  Pallas kernels  8.57 us (8%)
  local copies, waits for them, and re-layouts  6.62 us (6%)
  other arithmetic  2.53 us (2%)
  matrix products  1.7 us (1%)
    all_to_all x2, waiting for transfers between devices, over_z(): lax.all_to_all(blocks, 'modes', split_axis=0, concat_axis=0, axis_index_g...  45.2 us
    all_to_all x2, starting transfers between devices, over_z(): lax.all_to_all(blocks, 'modes', split_axis=0, concat_axis=0, axis_index_g...  21 us
    pallas_call x5, Pallas kernels, call(): pl.pallas_call(kernel, out_shape=outs, in_specs=[pl.BlockSpec(memory_spac...  8.57 us
    all_to_all x1, starting transfers between devices, shards(): sums = lax.all_to_all(block, 'dom', split_axis=0, concat_axis=0, tiled=True)  7.55 us
    ppermute x1, waiting for transfers between devices, shards(): after = lax.ppermute(to_last, 'dom', down)  5.66 us
    unnamed x44, local copies, waits for them, and re-layouts  4.72 us
    ppermute x1, starting transfers between devices, applied_rows(): lax.ppermute(along_x[UNIQUE], 'dom', [(i, (i + 1) % count) for i in range...  3.4 us
    ppermute x1, starting transfers between devices, shards(): before = lax.ppermute(to_next, 'dom', up)  3.36 us
  transfers between devices with their start and end apart: 7, of which 5 were waited for; matrix products, arithmetic and copies ran while one was open for 5% of the time, Pallas kernels for 3%

profile of v1, /device:TPU:6, one launch (start us, length us, event | category | flops | bytes accessed | tf_op | source)
XLA Modules:
  0.0 113.1 jit_solution(3543218435124416664)
XLA Ops:
  0.6 1.0 copy-done
  1.7 0.9 shard_map.158
  2.6 15.2 %all-to-all-start = ((f32[16,56,128]{2,1,0:T(8,128)}), f32[16,56,128]{2,1,0:T(8,128)S(1)}, u32[]{:S(2)}, u32[]{:S(2)}) async-start(f32[16,56,128]{2,1,0:T(8,128)} %shard_map.158), calls=%async_computation | async-start | bytes 917504 | tf_op jit(solution)/shard_map/all_to_all | solution.py:443
  18.0 26.6 %all-to-all-done.x_ref = f32[16,56,128]{2,1,0:T(8,128)S(1)} async-done(((f32[16,56,128]{2,1,0:T(8,128)}), f32[16,56,128]{2,1,0:T(8,128)S(1)}, u32[]{:S(2)}, u32[]{:S(2)}) %all-to-all-start) | async-done | bytes 458784 | tf_op jit(solution)/shard_map/all_to_all | solution.py:443
  45.3 1.9 %collective-permute-start = (f32[16,56,128]{2,1,0:T(8,128)S(1)}, f32[16,56,128]{2,1,0:T(8,128)S(1)}, u32[]{:S(2)}, u32[]{:S(2)}) collective-permute-start(f32[16,56,128]{2,1,0:T(8,128)S(1)} %get-tuple-element.12), channel_id=1, source_target_pairs={{0,16},{16,0},{32,48},{48,32},{64,80},{80,64},{96,112},{112,96},{1... | collective-permute-start | bytes 1376264 | tf_op jit(solution)/shard_map/ppermute | solution.py:463
  47.2 1.8 %collective-permute-done = f32[16,56,128]{2,1,0:T(8,128)S(1)} collective-permute-done((f32[16,56,128]{2,1,0:T(8,128)S(1)}, f32[16,56,128]{2,1,0:T(8,128)S(1)}, u32[]{:S(2)}, u32[]{:S(2)}) %collective-permute-start) | collective-permute-done | bytes 458784 | tf_op jit(solution)/shard_map/ppermute | solution.py:463
  49.0 0.8 add.50
  49.8 5.8 %all-to-all-start.1 = ((f32[16,56,128]{2,1,0:T(8,128)}), f32[16,56,128]{2,1,0:T(8,128)S(1)}, u32[]{:S(2)}, u32[]{:S(2)}) async-start(f32[16,56,128]{2,1,0:T(8,128)} %add.50), calls=%async_computation.1 | async-start | bytes 917504 | tf_op jit(solution)/shard_map/all_to_all | solution.py:443
  56.0 0.9 fusion.1
  56.9 3.4 %collective-permute-start.1 = (f32[16,256]{1,0:T(8,128)S(1)}, f32[16,256]{1,0:T(8,128)S(1)}, u32[]{:S(2)}, u32[]{:S(2)}) collective-permute-start(f32[16,256]{1,0:T(8,128)S(1)} %bitcast.31), channel_id=1, source_target_pairs={{0,1},{1,2},{2,3},{3,4},{4,5},{5,6},{6,7},{7,8},{8,9},{9,10},{10,1... | collective-permute-start | bytes 49160 | tf_op jit(solution)/shard_map/ppermute | solution.py:417
  60.3 0.7 broadcast_add_fusion
  61.2 1.8 %pad.4.refs_2_.refs_3_ = f32[165,8,384]{2,1,0:T(8,128)S(1)} pad(f32[165,8,264]{2,1,0:T(8,128)} %bitcast.29, f32[]{:T(128)} %constant.48.clone.1), padding=0_0x0_0x0_120 | pad | bytes 3421444 | tf_op jit(solution)/shard_map/jit(_pad)/pad | solution.py:469
  63.1 0.8 fusion.5.refs_1_
  63.9 18.6 %all-to-all-done.1.refs_0_ = f32[16,56,128]{2,1,0:T(8,128)S(1)} async-done(((f32[16,56,128]{2,1,0:T(8,128)}), f32[16,56,128]{2,1,0:T(8,128)S(1)}, u32[]{:S(2)}, u32[]{:S(2)}) %all-to-all-start.1) | async-done | bytes 458784 | tf_op jit(solution)/shard_map/all_to_all | solution.py:443
  82.6 1.6 %shard_map.160 = (f32[28,16,256]{2,1,0:T(8,128)S(1)}, f32[8,16,256]{2,1,0:T(8,128)S(1)}, f32[9,16,256]{2,1,0:T(8,128)S(1)}, f32[16,32,128]{2,1,0:T(8,128)}, f32[16,128]{1,0:T(8,128)S(1)}) custom-call(f32[16,56,128]{2,1,0:T(8,128)S(1)} %all-to-all-done.1.refs_0_, f32[28,16,256]{2,1,0:T(8,128)S(1)} %fusion.5.refs_1_, f32[165,8,384]{2,1,0:T(8,128)S(1)} %pad.4.refs_2_.refs_3_, ...), custom_call_target="tpu_custom_call" | custom-call | flops 30000000 | bytes 4083712 | tf_op jit(solution)/shard_map/pallas_call | solution.py:385
  85.5 7.5 %all-to-all-start.2 = ((f32[16,32,128]{2,1,0:T(8,128)}), f32[16,32,128]{2,1,0:T(8,128)S(1)}, u32[]{:S(2)}, u32[]{:S(2)}) async-start(f32[16,32,128]{2,1,0:T(8,128)} %get-tuple-element.17), calls=%async_computation.2 | async-start | bytes 524288 | tf_op jit(solution)/shard_map/all_to_all | solution.py:496
  93.0 3.4 %collective-permute-start.2 = (f32[8,16,256]{2,1,0:T(8,128)}, f32[8,16,256]{2,1,0:T(8,128)S(1)}, u32[]{:S(2)}, u32[]{:S(2)}) collective-permute-start(f32[8,16,256]{2,1,0:T(8,128)} %copy-done.4), channel_id=1, source_target_pairs={{0,1},{1,2},{2,3},{3,4},{4,5},{5,6},{6,7},{7,8},{8,9},{9,10},{10,1... | collective-permute-start | bytes 393224 | tf_op jit(solution)/shard_map/ppermute | solution.py:494
  96.4 2.5 %collective-permute-start.3 = (f32[9,16,256]{2,1,0:T(8,128)}, f32[9,16,256]{2,1,0:T(8,128)S(1)}, u32[]{:S(2)}, u32[]{:S(2)}) collective-permute-start(f32[9,16,256]{2,1,0:T(8,128)} %copy-done.3), channel_id=1, source_target_pairs={{1,0},{2,1},{3,2},{4,3},{5,4},{6,5},{7,6},{8,7},{9,8},{10,9},{11,1... | collective-permute-start | bytes 442376 | tf_op jit(solution)/shard_map/ppermute | solution.py:495
  98.9 0.8 add_divide_fusion.refs_3_
  100.1 5.7 %collective-permute-done.3.refs_2_ = f32[9,16,256]{2,1,0:T(8,128)S(1)} collective-permute-done((f32[9,16,256]{2,1,0:T(8,128)}, f32[9,16,256]{2,1,0:T(8,128)S(1)}, u32[]{:S(2)}, u32[]{:S(2)}) %collective-permute-start.3) | collective-permute-done | bytes 147488 | tf_op jit(solution)/shard_map/ppermute | solution.py:495
  105.8 1.0 copy-done.5
  106.8 1.0 copy-done.6
  107.8 3.8 %shard_map.161 = (f32[8,2,32,256]{3,2,1,0:T(8,128)}, f32[29,16,256]{2,1,0:T(8,128)S(1)}) custom-call(f32[28,16,256]{2,1,0:T(8,128)S(1)} %get-tuple-element.13.refs_0_, f32[8,16,256]{2,1,0:T(8,128)S(1)} %collective-permute-done.2.refs_1_, f32[9,16,256]{2,1,0:T(8,128)S(1)} %collective-permute-done.3.refs_2_, f32[10,16,384]{2,1,0:T(8,128)S(1)} %add_divide_fusion.refs_3_, ...), custom_call_target="tpu_custom_call" | custom-call | flops 800000000 | bytes 2768896 | tf_op jit(solution)/shard_map/pallas_call | solution.py:385
  111.5 1.6 %shard_map.162 = f32[8,2,32,256]{3,2,1,0:T(8,128)} custom-call(s32[1]{0:T(128)} %bitcast.10.refs_0_, f32[16,32,128]{2,1,0:T(8,128)S(1)} %all-to-all-done.2.refs_1_, f32[16,128]{1,0:T(8,128)S(1)} %get-tuple-element.18.refs_2_, f32[165,8,384]{2,1,0:T(8,128)S(1)} %pad.4.refs_2_.refs_3_, bf16[2,128,256]{2,1,0:T(8,128)(2,1)S(1)} %copy-done.1, ...), custom_call_target="tpu_custom_call" | custom-call | flops 30000000 | bytes 3428356 | tf_op jit(solution)/shard_map/pallas_call | solution.py:385
  (53 shorter events, 3.0 us)
Async XLA Ops:
  0.6 1.0 copy-start
  1.7 16.2 %copy-start.10 = (bf16[1,1,2,256,256]{4,3,2,1,0:T(8,128)(2,1)S(1)}, bf16[1,1,2,256,256]{4,3,2,1,0:T(8,128)(2,1)}, u32[]{:S(2)}) copy-start(bf16[1,1,2,256,256]{4,3,2,1,0:T(8,128)(2,1)} %constant.71) | copy-start | bytes 786436
  1.7 16.2 %copy-start.11 = (bf16[1,1,2,256,256]{4,3,2,1,0:T(8,128)(2,1)S(1)}, bf16[1,1,2,256,256]{4,3,2,1,0:T(8,128)(2,1)}, u32[]{:S(2)}) copy-start(bf16[1,1,2,256,256]{4,3,2,1,0:T(8,128)(2,1)} %constant.70) | copy-start | bytes 786436
  1.7 16.2 %copy-start.12 = (bf16[1,1,2,256,256]{4,3,2,1,0:T(8,128)(2,1)S(1)}, bf16[1,1,2,256,256]{4,3,2,1,0:T(8,128)(2,1)}, u32[]{:S(2)}) copy-start(bf16[1,1,2,256,256]{4,3,2,1,0:T(8,128)(2,1)} %constant.69) | copy-start | bytes 786436
  1.7 16.2 %copy-start.13 = (bf16[1,1,2,256,256]{4,3,2,1,0:T(8,128)(2,1)S(1)}, bf16[1,1,2,256,256]{4,3,2,1,0:T(8,128)(2,1)}, u32[]{:S(2)}) copy-start(bf16[1,1,2,256,256]{4,3,2,1,0:T(8,128)(2,1)} %constant.68) | copy-start | bytes 786436
  2.6 42.0 %all-to-all-start = ((f32[16,56,128]{2,1,0:T(8,128)}), f32[16,56,128]{2,1,0:T(8,128)S(1)}, u32[]{:S(2)}, u32[]{:S(2)}) async-start(f32[16,56,128]{2,1,0:T(8,128)} %shard_map.158), calls=%async_computation | async-start | bytes 917504 | tf_op jit(solution)/shard_map/all_to_all | solution.py:443
  18.0 37.6 %copy-start.9 = (f32[8,2,32,256]{3,2,1,0:T(8,128)S(1)}, f32[8,2,32,256]{3,2,1,0:T(8,128)}, u32[]{:S(2)}) copy-start(f32[8,2,32,256]{3,2,1,0:T(8,128)} %param.16) | copy-start | bytes 1572868
  45.3 10.7 %copy-start.15 = (f32[29,32,1]{1,0,2:T(8,128)S(1)}, f32[29,32,1]{1,0,2:T(8,128)}, u32[]{:S(2)}) copy-start(f32[29,32,1]{1,0,2:T(8,128)} %constant.72) | copy-start | bytes 11140
  45.3 3.7 %collective-permute-start = (f32[16,56,128]{2,1,0:T(8,128)S(1)}, f32[16,56,128]{2,1,0:T(8,128)S(1)}, u32[]{:S(2)}, u32[]{:S(2)}) collective-permute-start(f32[16,56,128]{2,1,0:T(8,128)S(1)} %get-tuple-element.12), channel_id=1, source_target_pairs={{0,16},{16,0},{32,48},{48,32},{64,80},{80,64},{96,112},{112,96},{1... | collective-permute-start | bytes 1376264 | tf_op jit(solution)/shard_map/ppermute | solution.py:463
  49.0 11.3 %copy-start.17 = (f32[384]{0:T(512)S(1)}, f32[384]{0:T(512)}, u32[]{:S(2)}) copy-start(f32[384]{0:T(512)} %constant.58.clone) | copy-start | bytes 4612
  49.0 11.3 %copy-start.19 = (f32[10]{0:T(128)S(1)}, f32[10]{0:T(128)}, u32[]{:S(2)}) copy-start(f32[10]{0:T(128)} %constant.57.clone) | copy-start | bytes 124
  49.0 12.0 %copy-start.16 = (f32[256]{0:T(256)S(1)}, f32[256]{0:T(256)}, u32[]{:S(2)}) copy-start(f32[256]{0:T(256)} %constant.55.clone) | copy-start | bytes 3076
  49.0 12.0 %copy-start.18 = (f32[28]{0:T(128)S(1)}, f32[28]{0:T(128)}, u32[]{:S(2)}) copy-start(f32[28]{0:T(128)} %constant.54.clone) | copy-start | bytes 340
  49.0 12.1 %copy-start.20 = (f32[8]{0:T(128)S(1)}, f32[8]{0:T(128)}, u32[]{:S(2)}) copy-start(f32[8]{0:T(128)} %param.17) | copy-start | bytes 100
  49.8 32.7 %all-to-all-start.1 = ((f32[16,56,128]{2,1,0:T(8,128)}), f32[16,56,128]{2,1,0:T(8,128)S(1)}, u32[]{:S(2)}, u32[]{:S(2)}) async-start(f32[16,56,128]{2,1,0:T(8,128)} %add.50), calls=%async_computation.1 | async-start | bytes 917504 | tf_op jit(solution)/shard_map/all_to_all | solution.py:443
  56.8 4.4 %copy-start.7 = (f32[29,16,256]{2,0,1:T(8,128)}, f32[29,16,256]{2,0,1:T(8,128)S(1)}, u32[]{:S(2)}) copy-start(f32[29,16,256]{2,0,1:T(8,128)S(1)} %fusion.1) | copy-start | bytes 1425412
  56.9 6.1 %collective-permute-start.1 = (f32[16,256]{1,0:T(8,128)S(1)}, f32[16,256]{1,0:T(8,128)S(1)}, u32[]{:S(2)}, u32[]{:S(2)}) collective-permute-start(f32[16,256]{1,0:T(8,128)S(1)} %bitcast.31), channel_id=1, source_target_pairs={{0,1},{1,2},{2,3},{3,4},{4,5},{5,6},{6,7},{7,8},{8,9},{9,10},{10,1... | collective-permute-start | bytes 49160 | tf_op jit(solution)/shard_map/ppermute | solution.py:417
  61.2 1.8 %copy-start.8 = (f32[29,16,256]{2,0,1:T(8,128)S(1)}, f32[29,16,256]{2,0,1:T(8,128)}, u32[]{:S(2)}) copy-start(f32[29,16,256]{2,0,1:T(8,128)} %copy-done.7) | copy-start | bytes 1425412
  61.2 1.8 %copy-start.14 = (f32[256,256,1]{1,0,2:T(8,128)S(1)}, f32[256,256,1]{1,0,2:T(8,128)}, u32[]{:S(2)}) copy-start(f32[256,256,1]{1,0,2:T(8,128)} %constant.73) | copy-start | bytes 786436
  63.0 19.5 %copy-start.2 = (bf16[2,256,128]{2,1,0:T(8,128)(2,1)S(1)}, bf16[2,256,128]{2,1,0:T(8,128)(2,1)}, u32[]{:S(2)}) copy-start(bf16[2,256,128]{2,1,0:T(8,128)(2,1)} %constant.56.clone.refs_3_) | copy-start | bytes 393220
  85.5 26.0 %copy-start.1 = (bf16[2,128,256]{2,1,0:T(8,128)(2,1)S(1)}, bf16[2,128,256]{2,1,0:T(8,128)(2,1)}, u32[]{:S(2)}) copy-start(bf16[2,128,256]{2,1,0:T(8,128)(2,1)} %constant.61.clone.refs_4_) | copy-start | bytes 393220
  85.5 26.0 %all-to-all-start.2 = ((f32[16,32,128]{2,1,0:T(8,128)}), f32[16,32,128]{2,1,0:T(8,128)S(1)}, u32[]{:S(2)}, u32[]{:S(2)}) async-start(f32[16,32,128]{2,1,0:T(8,128)} %get-tuple-element.17), calls=%async_computation.2 | async-start | bytes 524288 | tf_op jit(solution)/shard_map/all_to_all | solution.py:496
  93.0 7.1 %collective-permute-start.2 = (f32[8,16,256]{2,1,0:T(8,128)}, f32[8,16,256]{2,1,0:T(8,128)S(1)}, u32[]{:S(2)}, u32[]{:S(2)}) collective-permute-start(f32[8,16,256]{2,1,0:T(8,128)} %copy-done.4), channel_id=1, source_target_pairs={{0,1},{1,2},{2,3},{3,4},{4,5},{5,6},{6,7},{7,8},{8,9},{9,10},{10,1... | collective-permute-start | bytes 393224 | tf_op jit(solution)/shard_map/ppermute | solution.py:494
  96.4 9.4 %collective-permute-start.3 = (f32[9,16,256]{2,1,0:T(8,128)}, f32[9,16,256]{2,1,0:T(8,128)S(1)}, u32[]{:S(2)}, u32[]{:S(2)}) collective-permute-start(f32[9,16,256]{2,1,0:T(8,128)} %copy-done.3), channel_id=1, source_target_pairs={{1,0},{2,1},{3,2},{4,3},{5,4},{6,5},{7,6},{8,7},{9,8},{10,9},{11,1... | collective-permute-start | bytes 442376 | tf_op jit(solution)/shard_map/ppermute | solution.py:495
  (4 other events, 3.3 us)

commit v2 on v1

--- a/solution.py
+++ b/solution.py
@@ -174,6 +174,11 @@
     return np.stack([head, rest])
 
 
+def stacked(values):
+    head, rest = halves_of(values)
+    return jnp.asarray(np.concatenate([head, rest], axis=0))
+
+
 def fourier_halves(planes_total):
     chips = CHIPS
     z = np.arange(planes_total).reshape(chips, 2, 2, 8).transpose(1, 2, 0, 3)
@@ -192,11 +197,12 @@
     return head, (values - head.astype(F32)).astype(BF16)
 
 
-def dot3(left, right_head, right_rest):
+def dot3(left, right_ref):
     head, rest = split(left)
-    out = jnp.dot(head, right_head, preferred_element_type=F32)
-    out += jnp.dot(rest, right_head, preferred_element_type=F32)
-    return out + jnp.dot(head, right_rest, preferred_element_type=F32)
+    out = jnp.dot(
+        jnp.concatenate([head, head], axis=1), right_ref[...], preferred_element_type=F32
+    )
+    return out + jnp.dot(rest, right_ref[0 : left.shape[1]], preferred_element_type=F32)
 
 
 def lane_index(rows):
@@ -227,7 +233,7 @@
         out_ref[d, 48:56, :] = mixed
 
 
-def fourier_kernel(x_ref, table_ref, *out_refs):
+def fourier_kernel(kept, core_ref, x_ref, table_ref, *refs):
     columns = []
     for step in range(3):
         upper = x_ref[:, 16 * step : 16 * step + 8, :].reshape(LANES, LANES)
@@ -241,23 +247,28 @@
     )
     head, rest = split(jnp.concatenate(columns, axis=1))
     low = lane_index(8) < LANES // 2
-    for place, out_ref in enumerate(out_refs):
-        table_head, table_rest = table_ref[place, 0], table_ref[place, 1]
-        out = jnp.dot(table_head, head, preferred_element_type=F32)
-        out += jnp.dot(table_head, rest, preferred_element_type=F32)
-        out += jnp.dot(table_rest, head, preferred_element_type=F32)
-        for d in range(CHIPS):
-            for step in range(3):
-                out_ref[d, 16 * step : 16 * step + 16, :] = out[
-                    16 * d : 16 * d + 16, step * LANES : (step + 1) * LANES
-                ]
-            last = out[16 * d : 16 * d + 16, 3 * LANES :]
-            out_ref[d, 48:56, :] = jnp.where(low, last[:8], last[8:])
-
-
-def residual_kernel(
-    restrict_x, x_ref, applied_ref, factor_ref, restrict_ref, res_ref, up_ref, down_ref, block_ref, own_ref
-):
+    core = core_ref[0]
+    other = core if kept else 1 - core
+    table_head, table_rest = table_ref[core, other, 0], table_ref[core, other, 1]
+    out = jnp.dot(table_head, head, preferred_element_type=F32)
+    out += jnp.dot(table_head, rest, preferred_element_type=F32)
+    out += jnp.dot(table_rest, head, preferred_element_type=F32)
+    out_ref = refs[-1]
+
+    def put(d, rows, value):
+        if len(refs) == 2:
+            value = value + refs[0][d, rows, :]
+        out_ref[d, rows, :] = value
+
+    for d in range(CHIPS):
+        for step in range(3):
+            rows = slice(16 * step, 16 * step + 16)
+            put(d, rows, out[16 * d : 16 * d + 16, step * LANES : (step + 1) * LANES])
+        last = out[16 * d : 16 * d + 16, 3 * LANES :]
+        put(d, slice(48, 56), jnp.where(low, last[:8], last[8:]))
+
+
+def residual_kernel(x_ref, applied_ref, res_ref, up_ref, down_ref):
     low = lane_index(8) < LANES // 2
     for d, element, half, side in chip_places():
         lanes = slice(half * LANES, (half + 1) * LANES)
@@ -275,6 +286,9 @@
         up_ref[i] = res_ref[UNIQUE - 8 + i]
     for i in range(9):
         down_ref[i] = res_ref[i]
+
+
+def partial_kernel(restrict_x, res_ref, factor_ref, restrict_ref, block_ref, own_ref):
     lines = []
     for a in range(EXD + 1):
         total = None
@@ -283,7 +297,7 @@
                 term = res_ref[u] * float(restrict_x[a, u])
                 total = term if total is None else total + term
         lines.append(total)
-    load = dot3(jnp.concatenate(lines, axis=0), restrict_ref[0], restrict_ref[1])
+    load = dot3(jnp.concatenate(lines, axis=0), restrict_ref)
     line_size = factor_ref.shape[0] // (EXD + 1)
     sums = [jnp.zeros((8, 3 * LANES), F32) for _ in range(2)]
     for a in range(EXD + 1):
@@ -301,45 +315,134 @@
         block_ref[d, 16:32, :] = second
 
 
-def patch_kernel(vectors, res_ref, before_ref, after_ref, inverse_ref, forward_ref, backward_ref, out_ref, schwarz_ref):
+def node_weights():
+    place = np.arange(NODES)
+    return np.where((place == 0) | (place == NODES - 1), 0.5, 1.0)
+
+
+def taps(terms):
+    total = None
+    for value, factor in terms:
+        if factor != 0.0:
+            term = value * float(factor)
+            total = term if total is None else total + term
+    return total
+
+
+def mirror_signs(vectors):
+    return [1 if np.dot(vectors[:, p], vectors[::-1, p]) > 0 else -1 for p in range(PATCH)]
+
+
+def patch_lines(vectors, nodes, inverse, wanted):
+    signs = mirror_signs(vectors)
+    near = range(PATCH // 2)
+    sums = {
+        1: [nodes[i] + nodes[PATCH - 1 - i] for i in near],
+        -1: [nodes[i] - nodes[PATCH - 1 - i] for i in near],
+    }
+    scaled = [
+        taps((sums[signs[p]][i], vectors[i, p]) for i in near) * inverse[p] for p in range(PATCH)
+    ]
+    place = np.arange(NODES)
+    weight = np.where((place == 0) | (place == NODES - 1), 0.5, 1.0)
+    out = {}
+    for n in range(NODES // 2):
+        pair = [m for m in (n, NODES - 1 - n) if m in wanted]
+        if not pair:
+            continue
+        even, odd = (
+            taps((scaled[p], weight[n] * vectors[OV + n, p]) for p in range(PATCH) if signs[p] == sign)
+            for sign in (1, -1)
+        )
+        for m in pair:
+            out[m] = even + odd if m == n else even - odd
+    return out
+
+
+def patch_tiles(width):
+    for f in range(0, FIELDS, 8):
+        for q in range(0, width, LANES):
+            yield (slice(f, f + 8), slice(q, q + LANES))
+
+
+def inner_kernel(
+    vectors, res_ref, inverse_ref, forward_ref, backward_ref, edge_ref, shared_ref, inner_ref,
+    section_ref, parts_ref,
+):
     columns = res_ref.shape[2]
-    width = forward_ref.shape[2]
-    rows = jnp.concatenate([before_ref[...], res_ref[...], after_ref[...]], axis=0)
-    count = 8 + UNIQUE + 9
-    section = dot3(rows.reshape(count * FIELDS, columns), forward_ref[0], forward_ref[1])
-    section = section.reshape(count, FIELDS, width)
-    weight = np.where((np.arange(NODES) == 0) | (np.arange(NODES) == NODES - 1), 0.5, 1.0)
-    inverse = [inverse_ref[p] for p in range(PATCH)]
-    faces = [None] * (EXD + 2)
-    parts = [None] * (UNIQUE + 1)
-    for element in range(-1, EXD + 1):
-        start = 8 + 7 * element - 1
-        nodes = [section[start + i] for i in range(PATCH)]
-        scaled = []
-        for p in range(PATCH):
-            total = nodes[0] * float(vectors[0, p])
-            for i in range(1, PATCH):
-                total = total + nodes[i] * float(vectors[i, p])
-            scaled.append(total * inverse[p])
-        for n in range(NODES):
-            if (element == -1 and n < NODES - 1) or (element == EXD and n > 0):
-                continue
-            total = scaled[0] * float(weight[n] * vectors[OV + n, 0])
-            for p in range(1, PATCH):
-                total = total + scaled[p] * float(weight[n] * vectors[OV + n, p])
-            u = 7 * element + n
-            parts[u] = total if parts[u] is None else parts[u] + total
-    stacked = jnp.concatenate(parts, axis=0)
-    schwarz = dot3(stacked, backward_ref[0], backward_ref[1])
-    schwarz_ref[...] = schwarz.reshape(UNIQUE + 1, FIELDS, columns)
+    width = forward_ref.shape[1]
+    section = dot3(res_ref[...].reshape(UNIQUE * FIELDS, columns), forward_ref)
+    section_ref[...] = section.reshape(UNIQUE, FIELDS, width)
+    edge_ref[0:9] = section_ref[0:9]
+    edge_ref[9:17] = section_ref[20:28]
+    for at in patch_tiles(width):
+        inverse = [inverse_ref[(p,) + at] for p in range(PATCH)]
+        outs = []
+        for element in (1, 2):
+            nodes = [section_ref[(7 * element - 1 + i,) + at] for i in range(PATCH)]
+            outs.append(patch_lines(vectors, nodes, inverse, range(NODES)))
+        shared_ref[(0,) + at] = outs[0][0]
+        shared_ref[(1,) + at] = outs[1][NODES - 1]
+        for n in range(1, 7):
+            parts_ref[(n - 1,) + at] = outs[0][n]
+            parts_ref[(n + 6,) + at] = outs[1][n]
+        parts_ref[(6,) + at] = outs[0][NODES - 1] + outs[1][0]
+    inner = dot3(parts_ref[...].reshape(13 * FIELDS, width), backward_ref)
+    inner_ref[...] = inner.reshape(13, FIELDS, columns)
+
+
+def outer_parts(vectors, near_ref, edge_ref, shared_ref, inverse_ref, parts_ref):
+    def row_of(u, at):
+        if u < 0:
+            return near_ref[(u + 8,) + at]
+        if u >= UNIQUE:
+            return near_ref[(u - UNIQUE + 8,) + at]
+        return edge_ref[(u if u < 9 else u - 11,) + at]
+
+    for at in patch_tiles(near_ref.shape[2]):
+        inverse = [inverse_ref[(p,) + at] for p in range(PATCH)]
+        outs = {}
+        for element, wanted in ((-1, (NODES - 1,)), (0, range(NODES)), (3, range(NODES)), (4, (0,))):
+            nodes = [row_of(7 * element - 1 + i, at) for i in range(PATCH)]
+            outs[element] = patch_lines(vectors, nodes, inverse, wanted)
+        for n in range(1, 7):
+            parts_ref[(n,) + at] = outs[0][n]
+            parts_ref[(n + 8,) + at] = outs[3][n]
+        parts_ref[(0,) + at] = outs[-1][NODES - 1] + outs[0][0]
+        parts_ref[(7,) + at] = outs[0][NODES - 1] + shared_ref[(0,) + at]
+        parts_ref[(8,) + at] = shared_ref[(1,) + at] + outs[3][0]
+        parts_ref[(15,) + at] = outs[3][NODES - 1] + outs[4][0]
+
+
+def final_kernel(
+    points, vectors, me_ref, got_ref, own_ref, factor_hbm, prolong_ref, res_ref, before_ref, after_ref,
+    edge_ref, shared_ref, inner_ref, inverse_ref, forward_ref, backward_ref, residual_hbm, out_hbm,
+    out_ref, near_ref, parts_ref, factor_ref, sems,
+):
+    factor_copy = pltpu.make_async_copy(factor_hbm, factor_ref, sems.at[2 * EXD * NODES + EXD])
+    factor_copy.start()
+    columns = res_ref.shape[2]
+    width = forward_ref.shape[1]
+    stores = []
     for row in range(EXD * NODES):
         u = 7 * (row // NODES) + row % NODES
-        value = res_ref[u] if u < UNIQUE else after_ref[0]
+        source = res_ref.at[u] if u < UNIQUE else after_ref.at[0]
         for part in range(2):
-            out_ref[:, part, row, :] = value[8 * part : 8 * part + 8]
-
-
-def coarse_kernel(points, me_ref, got_ref, own_ref, factor_ref, prolong_ref, schwarz_ref, out_ref):
+            stores.append(
+                pltpu.make_async_copy(
+                    source.at[8 * part : 8 * part + 8],
+                    residual_hbm.at[:, part, row, :],
+                    sems.at[len(stores)],
+                )
+            )
+            stores[-1].start()
+    rows = jnp.concatenate([before_ref[...], after_ref[...]], axis=0)
+    near = dot3(rows.reshape(17 * FIELDS, columns), forward_ref)
+    near_ref[...] = near.reshape(17, FIELDS, width)
+    outer_parts(vectors, near_ref, edge_ref, shared_ref, inverse_ref, parts_ref)
+    outer = dot3(parts_ref[...].reshape(16 * FIELDS, width), backward_ref)
+    outer = outer.reshape(16, FIELDS, columns)
+    factor_copy.wait()
     me = me_ref[0]
     lane = lane_index(16)
     reach_first = jnp.where(lane < 8, 16, jnp.where(lane < 99, 1, 2))
@@ -368,26 +471,51 @@
                 total = jnp.sum(term, axis=1, keepdims=True)
                 lines[part] = jnp.where(lane8 == b, total, lines[part])
         values += lines
-    lines = dot3(jnp.concatenate(values, axis=0), prolong_ref[0], prolong_ref[1])
+    lines = dot3(jnp.concatenate(values, axis=0), prolong_ref)
     for row in range(EXD * NODES):
         element, n = row // NODES, row % NODES
         left = lines[16 * element : 16 * element + 16]
         right = lines[16 * element + 16 : 16 * element + 32]
-        value = schwarz_ref[7 * element + n]
+        u = 7 * element + n
+        value = outer[u] if u < 8 else (inner_ref[u - 8] if u < 21 else outer[u - 13])
         value = value + left * float((1.0 - points[n]) / 2.0) + right * float((1.0 + points[n]) / 2.0)
         for part in range(2):
             out_ref[:, part, row, :] = value[8 * part : 8 * part + 8]
-
-
-def call(kernel, outs, *operands, smem=0, flops=1e6):
+        if n == NODES - 1:
+            rows = slice(NODES * element, NODES * element + NODES)
+            stores.append(
+                pltpu.make_async_copy(
+                    out_ref.at[:, :, rows, :], out_hbm.at[:, :, rows, :], sems.at[len(stores)]
+                )
+            )
+            stores[-1].start()
+    for store in stores:
+        store.wait()
+
+
+def in_hbm(value):
+    return pltpu.with_memory_space_constraint(value, pltpu.HBM)
+
+
+def call(kernel, outs, *operands, smem=0, hbm=(), hbm_out=(), scratch=(), copies=0, flops=1e6):
     moved = sum(math.prod(o.shape) * o.dtype.itemsize for o in list(operands) + list(outs))
-    vmem = pl.BlockSpec(memory_space=pltpu.VMEM)
+    operands = [
+        in_hbm(o) if i in hbm else o for i, o in enumerate(operands)
+    ]
+    spaces = [
+        pltpu.SMEM if i < smem else pltpu.HBM if i in hbm else pltpu.VMEM for i in range(len(operands))
+    ]
+    out_spaces = [pl.ANY if i in hbm_out else pltpu.VMEM for i in range(len(outs))]
+    scratch = [pltpu.VMEM(o.shape, o.dtype) for o in scratch]
+    if copies:
+        scratch.append(pltpu.SemaphoreType.DMA((copies,)))
     return pl.pallas_call(
         kernel,
         out_shape=outs,
-        in_specs=[pl.BlockSpec(memory_space=pltpu.SMEM)] * smem + [vmem] * (len(operands) - smem),
-        out_specs=[vmem] * len(outs),
-        compiler_params=pltpu.CompilerParams(vmem_limit_bytes=32 * 2**20),
+        in_specs=[pl.BlockSpec(memory_space=space) for space in spaces],
+        out_specs=[pl.BlockSpec(memory_space=space) for space in out_spaces],
+        scratch_shapes=scratch,
+        compiler_params=pltpu.CompilerParams(vmem_limit_bytes=14 * 2**20),
         cost_estimate=pl.CostEstimate(
             flops=int(flops), bytes_accessed=int(moved), transcendentals=0
         ),
@@ -450,50 +578,10 @@
     )
     planes_here = over_z(packed)
 
-    tables = jnp.asarray(fourier_halves(planes_total))
-    send_table = jnp.where(core == 0, tables[0, 1], tables[1, 0])
-    keep_table = jnp.where(core == 0, tables[0, 0], tables[1, 1])
-    away, kept = call(
-        fourier_kernel,
-        [blocks_shape, blocks_shape],
-        planes_here,
-        jnp.stack([send_table, keep_table]),
-        flops=8e8,
-    )
-    back = lax.ppermute(away, "modes", [(i, i ^ 1) for i in range(count)])
-    loads = over_z(kept + back)
-
     coefficient = jnp.tile(helmholtz, 2)
     fields = iterate.transpose(2, 1, 0, 3).reshape(EXD * NODES, FIELDS, columns)
     applied = applied_rows(fields, coefficient, weights, stiffness, columns)
     factor = jnp.pad(coarse_factor.transpose(1, 0, 2), ((0, 0), (0, 0), (0, 3 * LANES - coarse_factor.shape[2])))
-
-    prolong_x, restrict_x = hat_tables(EXD, points, True)
-    prolong_y, restrict_y = hat_tables(elements_y, points, False)
-    unique_restrict = np.zeros((EXD + 1, UNIQUE))
-    for row in range(EXD * NODES - 1):
-        unique_restrict[:, 7 * (row // NODES) + row % NODES] += restrict_x[:, row]
-    unique_restrict[0, 0] += restrict_x[EXD, EXD * NODES - 1]
-    restrict_table = np.zeros((columns, LANES))
-    restrict_table[:, :line_size] = restrict_y.T
-    residual, to_next, to_last, block, own = call(
-        lambda *refs: residual_kernel(unique_restrict, *refs),
-        [
-            shape(UNIQUE, FIELDS, columns),
-            shape(8, FIELDS, columns),
-            shape(9, FIELDS, columns),
-            shape(CHIPS, 32, LANES),
-            shape(16, LANES),
-        ],
-        loads,
-        applied,
-        factor,
-        jnp.asarray(halves_of(restrict_table)),
-        flops=3e7,
-    )
-    before = lax.ppermute(to_next, "dom", up)
-    after = lax.ppermute(to_last, "dom", down)
-    sums = lax.all_to_all(block, "dom", split_axis=0, concat_axis=0, tiled=True)
 
     eigval, eigvec = patch_tables(1, 1, weights, stiffness)
     forward_y, backward_y, eigen_y = y_tables(elements_y, weights, stiffness)
@@ -509,30 +597,106 @@
         + jnp.asarray(eigen_row, F32)[None, None, :]
         + coefficient[None, :, None]
     )
-    residual_out, schwarz = call(
-        lambda *refs: patch_kernel(eigvec, *refs),
-        [shape(8, 2, EXD * NODES, columns), shape(UNIQUE + 1, FIELDS, columns)],
+    here = partition.astype(jnp.int32).reshape(1)
+    planes_here, applied, factor, inverse, here = lax.optimization_barrier(
+        (planes_here, applied, factor, inverse, here)
+    )
+    tables = jnp.asarray(fourier_halves(planes_total))
+    which = core.astype(jnp.int32).reshape(1)
+    (away,) = call(
+        lambda *refs: fourier_kernel(False, *refs),
+        [blocks_shape],
+        which,
+        planes_here,
+        tables,
+        smem=1,
+        flops=4e8,
+    )
+    back = lax.ppermute(away, "modes", [(i, i ^ 1) for i in range(count)])
+    (joined,) = call(
+        lambda *refs: fourier_kernel(True, *refs),
+        [blocks_shape],
+        which,
+        planes_here,
+        tables,
+        back,
+        smem=1,
+        flops=4e8,
+    )
+    loads = over_z(joined)
+
+    prolong_x, restrict_x = hat_tables(EXD, points, True)
+    prolong_y, restrict_y = hat_tables(elements_y, points, False)
+    unique_restrict = np.zeros((EXD + 1, UNIQUE))
+    for row in range(EXD * NODES - 1):
+        unique_restrict[:, 7 * (row // NODES) + row % NODES] += restrict_x[:, row]
+    unique_restrict[0, 0] += restrict_x[EXD, EXD * NODES - 1]
+    restrict_table = np.zeros((columns, LANES))
+    restrict_table[:, :line_size] = restrict_y.T
+    residual, to_next, to_last = call(
+        residual_kernel,
+        [
+            shape(UNIQUE, FIELDS, columns),
+            shape(8, FIELDS, columns),
+            shape(9, FIELDS, columns),
+        ],
+        loads,
+        applied,
+    )
+    before = lax.ppermute(to_next, "dom", up)
+    after = lax.ppermute(to_last, "dom", down)
+    block, own = call(
+        lambda *refs: partial_kernel(unique_restrict, *refs),
+        [shape(CHIPS, 32, LANES), shape(16, LANES)],
+        residual,
+        factor,
+        stacked(restrict_table),
+        flops=3e7,
+    )
+    block, here = lax.optimization_barrier((block, here))
+    sums = lax.all_to_all(block, "dom", split_axis=0, concat_axis=0, tiled=True)
+
+    forward, backward = stacked(forward_table), stacked(backward_table)
+    edge, shared, inner = call(
+        lambda *refs: inner_kernel(eigvec, *refs),
+        [shape(17, FIELDS, width), shape(2, FIELDS, width), shape(13, FIELDS, columns)],
+        residual,
+        inverse,
+        forward,
+        backward,
+        scratch=(shape(UNIQUE, FIELDS, width), shape(13, FIELDS, width)),
+        flops=6e8,
+    )
+    prolong_table = np.zeros((LANES, columns))
+    prolong_table[:line_size] = prolong_y
+    residual_out, correction = call(
+        lambda *refs: final_kernel(points, eigvec, *refs),
+        [shape(8, 2, EXD * NODES, columns)] * 2,
+        here,
+        sums,
+        own,
+        factor,
+        stacked(prolong_table),
         residual,
         before,
         after,
+        edge,
+        shared,
+        inner,
         inverse,
-        jnp.asarray(halves_of(forward_table)),
-        jnp.asarray(halves_of(backward_table)),
+        forward,
+        backward,
+        smem=1,
+        hbm=(3,),
+        hbm_out=(0, 1),
+        scratch=(
+            shape(8, 2, EXD * NODES, columns),
+            shape(17, FIELDS, width),
+            shape(16, FIELDS, width),
+            factor,
+        ),
+        copies=2 * EXD * NODES + EXD + 1,
         flops=8e8,
-    )
-    prolong_table = np.zeros((LANES, columns))
-    prolong_table[:line_size] = prolong_y
-    (correction,) = call(
-        lambda *refs: coarse_kernel(points, *refs),
-        [shape(8, 2, EXD * NODES, columns)],
-        partition.astype(jnp.int32).reshape(1),
-        sums,
-        own,
-        factor,
-        jnp.asarray(halves_of(prolong_table)),
-        schwarz,
-        smem=1,
-        flops=3e7,
     )
     return (residual_out, correction)
 

time: 114 us -> 111 us (0.974)
  the two profiles are of different devices: /device:TPU:6 before, /device:TPU:96 now
where the time goes in v2:
time: 111 us; the launch traced here: 110 us
  starting transfers between devices  36 us (32%)
  blocking collectives  32.8 us (30%)
  waiting for transfers between devices  22.6 us (20%)
  Pallas kernels  7.76 us (7%)
  local copies, waits for them, and re-layouts  5.6 us (5%)
  matrix products  2.48 us (2%)
  other arithmetic  2.15 us (2%)
    all_to_all x1, blocking collectives, over_z(): lax.all_to_all(blocks, 'modes', split_axis=0, concat_axis=0, axis_index_g...  32.8 us
    all_to_all x1, starting transfers between devices, over_z(): lax.all_to_all(blocks, 'modes', split_axis=0, concat_axis=0, axis_index_g...  14.3 us
    all_to_all x1, waiting for transfers between devices, over_z(): lax.all_to_all(blocks, 'modes', split_axis=0, concat_axis=0, axis_index_g...  12.8 us
    pallas_call x7, Pallas kernels, call(): pl.pallas_call(kernel, out_shape=outs, in_specs=[pl.BlockSpec(memory_spac...  7.76 us
    ppermute x1, waiting for transfers between devices, shards(): before = lax.ppermute(to_next, 'dom', up)  7.29 us
    all_to_all x1, starting transfers between devices, shards(): sums = lax.all_to_all(block, 'dom', split_axis=0, concat_axis=0, tiled=True)  7.17 us
    ppermute x1, starting transfers between devices, shards(): after = lax.ppermute(to_last, 'dom', down)  7.15 us
    ppermute x1, starting transfers between devices, applied_rows(): lax.ppermute(along_x[UNIQUE], 'dom', [(i, (i + 1) % count) for i in range...  3.38 us
  transfers between devices with their start and end apart: 6, of which 4 were waited for; matrix products, arithmetic and copies ran while one was open for 8% of the time, Pallas kernels for 1%

profile of v2, /device:TPU:96, one launch (start us, length us, event | category | flops | bytes accessed | tf_op | source)
XLA Modules:
  0.0 110.4 jit_solution(10234562697816963814)
XLA Ops:
  0.7 1.1 copy-done.4
  1.8 0.9 shard_map.158
  2.7 14.3 %all-to-all-start = ((f32[16,56,128]{2,1,0:T(8,128)}), f32[16,56,128]{2,1,0:T(8,128)S(1)}, u32[]{:S(2)}, u32[]{:S(2)}) async-start(f32[16,56,128]{2,1,0:T(8,128)} %shard_map.158), calls=%async_computation | async-start | bytes 917504 | tf_op jit(solution)/shard_map/all_to_all | solution.py:571
  17.3 0.9 fusion.1
  18.2 0.7 copy.41
  18.9 3.4 %collective-permute-start = (f32[16,256]{1,0:T(8,128)}, f32[16,256]{1,0:T(8,128)S(1)}, u32[]{:S(2)}, u32[]{:S(2)}) collective-permute-start(f32[16,256]{1,0:T(8,128)} %bitcast.20), channel_id=1, source_target_pairs={{0,1},{1,2},{2,3},{3,4},{4,5},{5,6},{6,7},{7,8},{8,9},{9,10},{10,1... | collective-permute-start | bytes 49160 | tf_op jit(solution)/shard_map/ppermute | solution.py:545
  22.5 0.7 broadcast_multiply_fusion
  23.2 0.8 add_divide_fusion.refs_1_.refs_11_
  24.6 0.8 slice.14
  25.5 1.8 %pad.4.refs_1_.refs_3_ = f32[165,8,384]{2,1,0:T(8,128)S(1)} pad(f32[165,8,264]{2,1,0:T(8,128)} %bitcast.26, f32[]{:T(128)} %constant.48.clone.1), padding=0_0x0_0x0_120 | pad | bytes 3421444 | tf_op jit(solution)/shard_map/jit(_pad)/pad | solution.py:584
  27.3 0.8 collective-permute-done
  28.1 1.6 %fusion.5.applied_ref = f32[28,16,256]{2,1,0:T(8,128)} fusion(f32[28,16,256]{2,0,1:T(8,128)S(1)} %bitcast.27, f32[28,256]{1,0:T(8,128)S(1)} %copy-done.17, f32[16]{0:T(128)S(1)} %copy-done.24, f32[256]{0:T(256)S(1)} %copy-done.19, f32[16,256]{1,0:T(8,128)S(1)} %collective-permute-done, pred[28]{0:T(512)(128)(4,1)S(1)} %copy-done.26, ...), kind=kOutput, calls=%fused_computation.7 | convolution fusion | flops 353239040 | bytes 2143436 | tf_op jit(solution)/shard_map/dot_general | solution.py:548
  29.8 12.8 %all-to-all-done.refs_1_ = f32[16,56,128]{2,1,0:T(8,128)S(1)} async-done(((f32[16,56,128]{2,1,0:T(8,128)}), f32[16,56,128]{2,1,0:T(8,128)S(1)}, u32[]{:S(2)}, u32[]{:S(2)}) %all-to-all-start) | async-done | bytes 458784 | tf_op jit(solution)/shard_map/all_to_all | solution.py:571
  43.0 2.1 %collective-permute-start.1 = (f32[16,56,128]{2,1,0:T(8,128)S(1)}, f32[16,56,128]{2,1,0:T(8,128)S(1)}, u32[]{:S(2)}, u32[]{:S(2)}) collective-permute-start(f32[16,56,128]{2,1,0:T(8,128)S(1)} %shard_map.159), channel_id=1, source_target_pairs={{0,16},{16,0},{32,48},{48,32},{64,80},{80,64},{96,112},{112,96},{1... | collective-permute-start | bytes 1376264 | tf_op jit(solution)/shard_map/ppermute | solution.py:615
  45.1 1.8 %collective-permute-done.1.refs_3_ = f32[16,56,128]{2,1,0:T(8,128)S(1)} collective-permute-done((f32[16,56,128]{2,1,0:T(8,128)S(1)}, f32[16,56,128]{2,1,0:T(8,128)S(1)}, u32[]{:S(2)}, u32[]{:S(2)}) %collective-permute-start.1) | collective-permute-done | bytes 458784 | tf_op jit(solution)/shard_map/ppermute | solution.py:615
  47.3 32.8 %all_to_all.15.x_ref = f32[16,56,128]{2,1,0:T(8,128)S(1)} all-to-all(f32[16,56,128]{2,1,0:T(8,128)S(1)} %shard_map.160), channel_id=1, replica_groups={{0,32,64,96,128,160,192,224,256,288,320,352,384,416,448,480},{16,48,80,..., dimensions={0} | all-to-all | bytes 917504 | tf_op jit(solution)/shard_map/all_to_all | solution.py:571
  80.2 0.8 shard_map.162
  81.1 0.7 copy-done.7
  81.8 7.2 %all-to-all-start.2 = ((f32[16,32,128]{2,1,0:T(8,128)}), f32[16,32,128]{2,1,0:T(8,128)S(1)}, u32[]{:S(2)}, u32[]{:S(2)}) async-start(f32[16,32,128]{2,1,0:T(8,128)} %copy-done.7), calls=%async_computation.2 | async-start | bytes 524288 | tf_op jit(solution)/shard_map/all_to_all | solution.py:657
  89.0 7.1 %collective-permute-start.3 = (f32[9,16,256]{2,1,0:T(8,128)}, f32[9,16,256]{2,1,0:T(8,128)S(1)}, u32[]{:S(2)}, u32[]{:S(2)}) collective-permute-start(f32[9,16,256]{2,1,0:T(8,128)} %copy-done.10), channel_id=1, source_target_pairs={{1,0},{2,1},{3,2},{4,3},{5,4},{6,5},{7,6},{8,7},{9,8},{10,9},{11,1... | collective-permute-start | bytes 442376 | tf_op jit(solution)/shard_map/ppermute | solution.py:647
  96.1 1.9 %collective-permute-start.2 = (f32[8,16,256]{2,1,0:T(8,128)}, f32[8,16,256]{2,1,0:T(8,128)S(1)}, u32[]{:S(2)}, u32[]{:S(2)}) collective-permute-start(f32[8,16,256]{2,1,0:T(8,128)} %copy-done.11), channel_id=1, source_target_pairs={{0,1},{1,2},{2,3},{3,4},{4,5},{5,6},{6,7},{7,8},{8,9},{9,10},{10,1... | collective-permute-start | bytes 393224 | tf_op jit(solution)/shard_map/ppermute | solution.py:646
  98.1 1.1 %shard_map.163 = (f32[17,16,384]{2,1,0:T(8,128)S(1)}, f32[2,16,384]{2,1,0:T(8,128)S(1)}, f32[13,16,256]{2,1,0:T(8,128)S(1)}) custom-call(f32[28,16,256]{2,1,0:T(8,128)S(1)} %get-tuple-element.19.refs_0_.refs_5_, f32[10,16,384]{2,1,0:T(8,128)S(1)} %copy-done.3, bf16[512,384]{1,0:T(8,128)(2,1)S(1)} %copy-done.6, bf16[768,256]{1,0:T(8,128)(2,1)S(1)} %copy-done.5), custom_call_target="tpu_custom_call" | custom-call | flops 600000000 | bytes 2170880 | tf_op jit(solution)/shard_map/pallas_call | solution.py:512
  99.2 7.3 %collective-permute-done.2.refs_6_ = f32[8,16,256]{2,1,0:T(8,128)S(1)} collective-permute-done((f32[8,16,256]{2,1,0:T(8,128)}, f32[8,16,256]{2,1,0:T(8,128)S(1)}, u32[]{:S(2)}, u32[]{:S(2)}) %collective-permute-start.2) | collective-permute-done | bytes 131104 | tf_op jit(solution)/shard_map/ppermute | solution.py:646
  106.5 3.9 %shard_map.164 = (f32[8,2,32,256]{3,2,1,0:T(8,128)}, f32[8,2,32,256]{3,2,1,0:T(8,128)}) custom-call(s32[1]{0:T(128)} %bitcast.9.refs_0_, f32[16,32,128]{2,1,0:T(8,128)S(1)} %all-to-all-done.2.refs_1_, f32[16,128]{1,0:T(8,128)S(1)} %get-tuple-element.25.refs_2_, f32[165,8,384]{2,1,0:T(8,128)} %copy-done, bf16[256,256]{1,0:T(8,128)(2,1)S(1)} %copy-done.8, ...), custom_call_target="tpu_custom_call" | custom-call | flops 800000000 | bytes 5926916 | tf_op jit(solution)/shard_map/pallas_call | solution.py:512
  (65 shorter events, 2.2 us)
Async XLA Ops:
  0.6 16.7 %copy-start.18 = (f32[29,32,1]{1,0,2:T(8,128)S(1)}, f32[29,32,1]{1,0,2:T(8,128)}, u32[]{:S(2)}) copy-start(f32[29,32,1]{1,0,2:T(8,128)} %constant.68) | copy-start | bytes 11140
  0.6 21.8 %copy-start.25 = (f32[10]{0:T(128)S(1)}, f32[10]{0:T(128)}, u32[]{:S(2)}) copy-start(f32[10]{0:T(128)} %constant.55.clone) | copy-start | bytes 124
  0.7 21.8 %copy-start.20 = (f32[384]{0:T(512)S(1)}, f32[384]{0:T(512)}, u32[]{:S(2)}) copy-start(f32[384]{0:T(512)} %constant.56.clone) | copy-start | bytes 4612
  0.7 21.8 %copy-start.19 = (f32[256]{0:T(256)S(1)}, f32[256]{0:T(256)}, u32[]{:S(2)}) copy-start(f32[256]{0:T(256)} %constant.54.clone) | copy-start | bytes 3076
  0.7 21.8 %copy-start.21 = (f32[28]{0:T(128)S(1)}, f32[28]{0:T(128)}, u32[]{:S(2)}) copy-start(f32[28]{0:T(128)} %constant.53.clone) | copy-start | bytes 340
  1.8 15.3 %copy-start.15 = (f32[8,2,32,256]{3,2,1,0:T(8,128)S(1)}, f32[8,2,32,256]{3,2,1,0:T(8,128)}, u32[]{:S(2)}) copy-start(f32[8,2,32,256]{3,2,1,0:T(8,128)} %param.16) | copy-start | bytes 1572868
  1.8 20.6 %copy-start.27 = (f32[8]{0:T(128)S(1)}, f32[8]{0:T(128)}, u32[]{:S(2)}) copy-start(f32[8]{0:T(128)} %param.17) | copy-start | bytes 100
  2.7 39.8 %all-to-all-start = ((f32[16,56,128]{2,1,0:T(8,128)}), f32[16,56,128]{2,1,0:T(8,128)S(1)}, u32[]{:S(2)}, u32[]{:S(2)}) async-start(f32[16,56,128]{2,1,0:T(8,128)} %shard_map.158), calls=%async_computation | async-start | bytes 917504 | tf_op jit(solution)/shard_map/all_to_all | solution.py:571
  18.2 7.2 %copy-start.13 = (f32[29,16,256]{2,0,1:T(8,128)}, f32[29,16,256]{2,0,1:T(8,128)S(1)}, u32[]{:S(2)}) copy-start(f32[29,16,256]{2,0,1:T(8,128)S(1)} %fusion.1) | copy-start | bytes 1425412
  18.9 9.2 %collective-permute-start = (f32[16,256]{1,0:T(8,128)}, f32[16,256]{1,0:T(8,128)S(1)}, u32[]{:S(2)}, u32[]{:S(2)}) collective-permute-start(f32[16,256]{1,0:T(8,128)} %bitcast.20), channel_id=1, source_target_pairs={{0,1},{1,2},{2,3},{3,4},{4,5},{5,6},{6,7},{7,8},{8,9},{9,10},{10,1... | collective-permute-start | bytes 49160 | tf_op jit(solution)/shard_map/ppermute | solution.py:545
  22.4 3.0 %copy-start.23 = (f32[16]{0:T(128)}, f32[16]{0:T(128)S(1)}, u32[]{:S(2)}) copy-start(f32[16]{0:T(128)S(1)} %mul.56) | copy-start | bytes 196
  25.4 2.7 %copy-start.14 = (f32[29,16,256]{2,0,1:T(8,128)S(1)}, f32[29,16,256]{2,0,1:T(8,128)}, u32[]{:S(2)}) copy-start(f32[29,16,256]{2,0,1:T(8,128)} %copy-done.13) | copy-start | bytes 1425412
  27.3 52.9 %copy-start = (f32[165,8,384]{2,1,0:T(8,128)}, f32[165,8,384]{2,1,0:T(8,128)S(1)}, u32[]{:S(2)}) copy-start(f32[165,8,384]{2,1,0:T(8,128)S(1)} %pad.4.refs_1_.refs_3_) | copy-start | bytes 6082564
  27.3 15.2 %copy-start.1 = (bf16[2,2,2,256,256]{4,3,2,1,0:T(8,128)(2,1)S(1)}, bf16[2,2,2,256,256]{4,3,2,1,0:T(8,128)(2,1)}, u32[]{:S(2)}) copy-start(bf16[2,2,2,256,256]{4,3,2,1,0:T(8,128)(2,1)} %constant.57.clone.refs_2_) | copy-start | bytes 3145732
  43.0 37.1 %copy-start.2 = (f32[28,16,256]{2,1,0:T(8,128)S(1)}, f32[28,16,256]{2,1,0:T(8,128)}, u32[]{:S(2)}) copy-start(f32[28,16,256]{2,1,0:T(8,128)} %fusion.5.applied_ref) | copy-start | bytes 1376260
  43.0 37.2 %copy-start.9 = (bf16[512,128]{1,0:T(8,128)(2,1)S(1)}, bf16[512,128]{1,0:T(8,128)(2,1)}, u32[]{:S(2)}) copy-start(bf16[512,128]{1,0:T(8,128)(2,1)} %constant.58.clone.refs_2_) | copy-start | bytes 393220
  43.0 3.8 %collective-permute-start.1 = (f32[16,56,128]{2,1,0:T(8,128)S(1)}, f32[16,56,128]{2,1,0:T(8,128)S(1)}, u32[]{:S(2)}, u32[]{:S(2)}) collective-permute-start(f32[16,56,128]{2,1,0:T(8,128)S(1)} %shard_map.159), channel_id=1, source_target_pairs={{0,16},{16,0},{32,48},{48,32},{64,80},{80,64},{96,112},{112,96},{1... | collective-permute-start | bytes 1376264 | tf_op jit(solution)/shard_map/ppermute | solution.py:615
  80.1 18.0 %copy-start.3 = (f32[10,16,384]{2,1,0:T(8,128)S(1)}, f32[10,16,384]{2,1,0:T(8,128)}, u32[]{:S(2)}) copy-start(f32[10,16,384]{2,1,0:T(8,128)} %add_divide_fusion.refs_1_.refs_11_) | copy-start | bytes 737284
  80.1 18.0 %copy-start.5 = (bf16[768,256]{1,0:T(8,128)(2,1)S(1)}, bf16[768,256]{1,0:T(8,128)(2,1)}, u32[]{:S(2)}) copy-start(bf16[768,256]{1,0:T(8,128)(2,1)} %constant.60.clone.refs_3_.refs_13_) | copy-start | bytes 1179652
  80.1 18.0 %copy-start.6 = (bf16[512,384]{1,0:T(8,128)(2,1)S(1)}, bf16[512,384]{1,0:T(8,128)(2,1)}, u32[]{:S(2)}) copy-start(bf16[512,384]{1,0:T(8,128)(2,1)} %constant.59.clone.refs_2_.refs_12_) | copy-start | bytes 1179652
  81.8 24.7 %copy-start.8 = (bf16[256,256]{1,0:T(8,128)(2,1)S(1)}, bf16[256,256]{1,0:T(8,128)(2,1)}, u32[]{:S(2)}) copy-start(bf16[256,256]{1,0:T(8,128)(2,1)} %constant.61.clone.refs_4_) | copy-start | bytes 393220
  81.8 24.7 %all-to-all-start.2 = ((f32[16,32,128]{2,1,0:T(8,128)}), f32[16,32,128]{2,1,0:T(8,128)S(1)}, u32[]{:S(2)}, u32[]{:S(2)}) async-start(f32[16,32,128]{2,1,0:T(8,128)} %copy-done.7), calls=%async_computation.2 | async-start | bytes 524288 | tf_op jit(solution)/shard_map/all_to_all | solution.py:657
  89.0 17.6 %collective-permute-start.3 = (f32[9,16,256]{2,1,0:T(8,128)}, f32[9,16,256]{2,1,0:T(8,128)S(1)}, u32[]{:S(2)}, u32[]{:S(2)}) collective-permute-start(f32[9,16,256]{2,1,0:T(8,128)} %copy-done.10), channel_id=1, source_target_pairs={{1,0},{2,1},{3,2},{4,3},{5,4},{6,5},{7,6},{8,7},{9,8},{10,9},{11,1... | collective-permute-start | bytes 442376 | tf_op jit(solution)/shard_map/ppermute | solution.py:647
  96.1 10.4 %collective-permute-start.2 = (f32[8,16,256]{2,1,0:T(8,128)}, f32[8,16,256]{2,1,0:T(8,128)S(1)}, u32[]{:S(2)}, u32[]{:S(2)}) collective-permute-start(f32[8,16,256]{2,1,0:T(8,128)} %copy-done.11), channel_id=1, source_target_pairs={{0,1},{1,2},{2,3},{3,4},{4,5},{5,6},{6,7},{7,8},{8,9},{9,10},{10,1... | collective-permute-start | bytes 393224 | tf_op jit(solution)/shard_map/ppermute | solution.py:646
  (10 other events, 19.4 us)

commit v3 on v2

--- a/solution.py
+++ b/solution.py
@@ -288,7 +288,9 @@
         down_ref[i] = res_ref[i]
 
 
-def partial_kernel(restrict_x, res_ref, factor_ref, restrict_ref, block_ref, own_ref):
+def partial_kernel(
+    restrict_x, res_ref, factor_ref, end_ref, restrict_ref, block_ref, own_ref
+):
     lines = []
     for a in range(EXD + 1):
         total = None
@@ -299,7 +301,7 @@
         lines.append(total)
     load = dot3(jnp.concatenate(lines, axis=0), restrict_ref)
     line_size = factor_ref.shape[0] // (EXD + 1)
-    sums = [jnp.zeros((8, 3 * LANES), F32) for _ in range(2)]
+    sums = [jnp.zeros((8, 2 * LANES), F32) for _ in range(2)]
     for a in range(EXD + 1):
         for b in range(line_size):
             row = factor_ref[a * line_size + b]
@@ -307,17 +309,25 @@
                 at = 16 * a + 8 * part
                 sums[part] = sums[part] + load[at : at + 8, b : b + 1] * row
     both = jnp.concatenate(sums, axis=0)
-    first, second, third = (both[:, i * LANES : (i + 1) * LANES] for i in range(3))
+    first, second = both[:, :LANES], both[:, LANES:]
+    lane8 = lane_index(8)
+    ends = [jnp.zeros((8, LANES), F32) for _ in range(2)]
+    for j in range(end_ref.shape[0]):
+        for part in range(2):
+            term = None
+            for a in range(EXD + 1):
+                at = 16 * a + 8 * part
+                value = load[at : at + 8] * end_ref[j, a]
+                term = value if term is None else term + value
+            ends[part] = jnp.where(lane8 == j, jnp.sum(term, axis=1, keepdims=True), ends[part])
+    third = jnp.concatenate(ends, axis=0)
     own_ref[...] = first
-    joined = jnp.where(lane_index(16) < 8, third, first)
+    joined = jnp.where(lane_index(16) < 8, third, swap_halves(first))
+    low = lane_index(8) < LANES // 2
+    joined = jnp.where(low, joined[:8], swap_halves(joined[8:]))
     for d in range(CHIPS):
-        block_ref[d, 0:16, :] = joined
-        block_ref[d, 16:32, :] = second
-
-
-def node_weights():
-    place = np.arange(NODES)
-    return np.where((place == 0) | (place == NODES - 1), 0.5, 1.0)
+        block_ref[d, 0:16, :] = second
+        block_ref[d, 16:24, :] = joined
 
 
 def taps(terms):
@@ -359,6 +369,16 @@
     return out
 
 
+def fetch(sources, targets, sems):
+    copies = [
+        pltpu.make_async_copy(source, target, sems.at[i])
+        for i, (source, target) in enumerate(zip(sources, targets))
+    ]
+    for copy in copies:
+        copy.start()
+    return copies
+
+
 def patch_tiles(width):
     for f in range(0, FIELDS, 8):
         for q in range(0, width, LANES):
@@ -367,9 +387,17 @@
 
 def inner_kernel(
     vectors, res_ref, inverse_ref, forward_ref, backward_ref, edge_ref, shared_ref, inner_ref,
-    section_ref, parts_ref,
+    residual_hbm, section_ref, parts_ref, sems,
 ):
     columns = res_ref.shape[2]
+    stores = []
+    for row in range(EXD * NODES - 1):
+        source = res_ref.at[7 * (row // NODES) + row % NODES]
+        stores += fetch(
+            [source.at[8 * part : 8 * part + 8] for part in range(2)],
+            [residual_hbm.at[:, part, row, :] for part in range(2)],
+            sems.at[2 * row : 2 * row + 2],
+        )
     width = forward_ref.shape[1]
     section = dot3(res_ref[...].reshape(UNIQUE * FIELDS, columns), forward_ref)
     section_ref[...] = section.reshape(UNIQUE, FIELDS, width)
@@ -389,6 +417,8 @@
         parts_ref[(6,) + at] = outs[0][NODES - 1] + outs[1][0]
     inner = dot3(parts_ref[...].reshape(13 * FIELDS, width), backward_ref)
     inner_ref[...] = inner.reshape(13, FIELDS, columns)
+    for store in stores:
+        store.wait()
 
 
 def outer_parts(vectors, near_ref, edge_ref, shared_ref, inverse_ref, parts_ref):
@@ -415,62 +445,57 @@
 
 
 def final_kernel(
-    points, vectors, me_ref, got_ref, own_ref, factor_hbm, prolong_ref, res_ref, before_ref, after_ref,
-    edge_ref, shared_ref, inner_ref, inverse_ref, forward_ref, backward_ref, residual_hbm, out_hbm,
-    out_ref, near_ref, parts_ref, factor_ref, sems,
+    points, vectors, me_ref, got_ref, own_ref, factor_hbm, end_hbm, prolong_ref, before_ref, after_ref, edge_ref,
+    shared_ref, inner_ref, inverse_ref, forward_ref, backward_ref, begun_hbm, residual_hbm, out_hbm,
+    out_ref, near_ref, parts_ref, factor_ref, end_ref, sems,
 ):
-    factor_copy = pltpu.make_async_copy(factor_hbm, factor_ref, sems.at[2 * EXD * NODES + EXD])
-    factor_copy.start()
-    columns = res_ref.shape[2]
+    factor_copies = fetch((factor_hbm, end_hbm), (factor_ref, end_ref), sems)
+    columns = after_ref.shape[2]
     width = forward_ref.shape[1]
-    stores = []
-    for row in range(EXD * NODES):
-        u = 7 * (row // NODES) + row % NODES
-        source = res_ref.at[u] if u < UNIQUE else after_ref.at[0]
-        for part in range(2):
-            stores.append(
-                pltpu.make_async_copy(
-                    source.at[8 * part : 8 * part + 8],
-                    residual_hbm.at[:, part, row, :],
-                    sems.at[len(stores)],
-                )
-            )
-            stores[-1].start()
+    stores = fetch(
+        [after_ref.at[0, 8 * part : 8 * part + 8] for part in range(2)],
+        [residual_hbm.at[:, part, EXD * NODES - 1, :] for part in range(2)],
+        sems.at[2:4],
+    )
     rows = jnp.concatenate([before_ref[...], after_ref[...]], axis=0)
     near = dot3(rows.reshape(17 * FIELDS, columns), forward_ref)
     near_ref[...] = near.reshape(17, FIELDS, width)
     outer_parts(vectors, near_ref, edge_ref, shared_ref, inverse_ref, parts_ref)
     outer = dot3(parts_ref[...].reshape(16 * FIELDS, width), backward_ref)
     outer = outer.reshape(16, FIELDS, columns)
-    factor_copy.wait()
+    for copy in factor_copies:
+        copy.wait()
     me = me_ref[0]
     lane = lane_index(16)
-    reach_first = jnp.where(lane < 8, 16, jnp.where(lane < 99, 1, 2))
+    place = jnp.bitwise_and(lane_index(8), LANES // 2 - 1)
+    reach_joined = jnp.where(place < 8, 16, jnp.where(place < 99 - LANES // 2, 0, 2))
     reach_second = jnp.where(
         lane < 132 - LANES, 2, jnp.where(lane < 165 - LANES, 4, jnp.where(lane < 198 - LANES, 8, 16))
     )
-    first = jnp.zeros((16, LANES), F32)
+    joined = jnp.zeros((8, LANES), F32)
     second = jnp.zeros((16, LANES), F32)
     for source in range(CHIPS):
         apart = jnp.bitwise_xor(me, source)
-        first = first + jnp.where(reach_first > apart, got_ref[source, 0:16, :], 0.0)
-        second = second + jnp.where(reach_second > apart, got_ref[source, 16:32, :], 0.0)
-    third = jnp.where(lane < 8, first, 0.0)
-    first = jnp.where(lane < 8, own_ref[...], first)
+        second = second + jnp.where(reach_second > apart, got_ref[source, 0:16, :], 0.0)
+        joined = joined + jnp.where(reach_joined > apart, got_ref[source, 16:24, :], 0.0)
+    joined = jnp.concatenate([joined, swap_halves(joined)], axis=0)
+    third = jnp.where(lane < 8, joined, 0.0)
+    first = jnp.where(lane < 99, own_ref[...], swap_halves(joined))
     line_size = factor_ref.shape[0] // (EXD + 1)
     lane8 = lane_index(8)
     values = []
     for a in range(EXD + 1):
-        lines = [jnp.zeros((8, LANES), F32) for _ in range(2)]
-        for b in range(line_size):
-            row = factor_ref[a * line_size + b]
-            for part in range(2):
-                at = slice(8 * part, 8 * part + 8)
-                term = row[:, :LANES] * first[at] + row[:, LANES : 2 * LANES] * second[at]
-                term = term + row[:, 2 * LANES :] * third[at]
+        for part in range(2):
+            at = slice(8 * part, 8 * part + 8)
+            line = jnp.zeros((8, LANES), F32)
+            for j in range(end_ref.shape[0]):
+                line = line + third[at][:, j : j + 1] * end_ref[j, a]
+            for b in range(line_size):
+                row = factor_ref[a * line_size + b]
+                term = row[:, :LANES] * first[at] + row[:, LANES:] * second[at]
                 total = jnp.sum(term, axis=1, keepdims=True)
-                lines[part] = jnp.where(lane8 == b, total, lines[part])
-        values += lines
+                line = line + jnp.where(lane8 == b, total, 0.0)
+            values.append(line)
     lines = dot3(jnp.concatenate(values, axis=0), prolong_ref)
     for row in range(EXD * NODES):
         element, n = row // NODES, row % NODES
@@ -485,7 +510,7 @@
             rows = slice(NODES * element, NODES * element + NODES)
             stores.append(
                 pltpu.make_async_copy(
-                    out_ref.at[:, :, rows, :], out_hbm.at[:, :, rows, :], sems.at[len(stores)]
+                    out_ref.at[:, :, rows, :], out_hbm.at[:, :, rows, :], sems.at[2 + len(stores)]
                 )
             )
             stores[-1].start()
@@ -497,7 +522,9 @@
     return pltpu.with_memory_space_constraint(value, pltpu.HBM)
 
 
-def call(kernel, outs, *operands, smem=0, hbm=(), hbm_out=(), scratch=(), copies=0, flops=1e6):
+def call(
+    kernel, outs, *operands, smem=0, hbm=(), hbm_out=(), scratch=(), copies=0, aliases=None, flops=1e6
+):
     moved = sum(math.prod(o.shape) * o.dtype.itemsize for o in list(operands) + list(outs))
     operands = [
         in_hbm(o) if i in hbm else o for i, o in enumerate(operands)
@@ -515,6 +542,7 @@
         in_specs=[pl.BlockSpec(memory_space=space) for space in spaces],
         out_specs=[pl.BlockSpec(memory_space=space) for space in out_spaces],
         scratch_shapes=scratch,
+        input_output_aliases=aliases or {},
         compiler_params=pltpu.CompilerParams(vmem_limit_bytes=14 * 2**20),
         cost_estimate=pl.CostEstimate(
             flops=int(flops), bytes_accessed=int(moved), transcendentals=0
@@ -581,7 +609,10 @@
     coefficient = jnp.tile(helmholtz, 2)
     fields = iterate.transpose(2, 1, 0, 3).reshape(EXD * NODES, FIELDS, columns)
     applied = applied_rows(fields, coefficient, weights, stiffness, columns)
-    factor = jnp.pad(coarse_factor.transpose(1, 0, 2), ((0, 0), (0, 0), (0, 3 * LANES - coarse_factor.shape[2])))
+    turned = coarse_factor.transpose(1, 0, 2)
+    factor = turned[:, :, : 2 * LANES]
+    factor_end = turned[:, :, 2 * LANES :].reshape(EXD + 1, line_size, 8, -1).transpose(3, 0, 2, 1)
+    factor_end = jnp.pad(factor_end, ((0, 0),) * 3 + ((0, LANES - line_size),))
 
     eigval, eigvec = patch_tables(1, 1, weights, stiffness)
     forward_y, backward_y, eigen_y = y_tables(elements_y, weights, stiffness)
@@ -598,8 +629,8 @@
         + coefficient[None, :, None]
     )
     here = partition.astype(jnp.int32).reshape(1)
-    planes_here, applied, factor, inverse, here = lax.optimization_barrier(
-        (planes_here, applied, factor, inverse, here)
+    planes_here, applied, factor, factor_end, inverse, here = lax.optimization_barrier(
+        (planes_here, applied, factor, factor_end, inverse, here)
     )
     tables = jnp.asarray(fourier_halves(planes_total))
     which = core.astype(jnp.int32).reshape(1)
@@ -647,9 +678,10 @@
     after = lax.ppermute(to_last, "dom", down)
     block, own = call(
         lambda *refs: partial_kernel(unique_restrict, *refs),
-        [shape(CHIPS, 32, LANES), shape(16, LANES)],
+        [shape(CHIPS, 24, LANES), shape(16, LANES)],
         residual,
         factor,
+        factor_end,
         stacked(restrict_table),
         flops=3e7,
     )
@@ -657,14 +689,21 @@
     sums = lax.all_to_all(block, "dom", split_axis=0, concat_axis=0, tiled=True)
 
     forward, backward = stacked(forward_table), stacked(backward_table)
-    edge, shared, inner = call(
+    edge, shared, inner, begun = call(
         lambda *refs: inner_kernel(eigvec, *refs),
-        [shape(17, FIELDS, width), shape(2, FIELDS, width), shape(13, FIELDS, columns)],
+        [
+            shape(17, FIELDS, width),
+            shape(2, FIELDS, width),
+            shape(13, FIELDS, columns),
+            shape(8, 2, EXD * NODES, columns),
+        ],
         residual,
         inverse,
         forward,
         backward,
+        hbm_out=(3,),
         scratch=(shape(UNIQUE, FIELDS, width), shape(13, FIELDS, width)),
+        copies=2 * (EXD * NODES - 1),
         flops=6e8,
     )
     prolong_table = np.zeros((LANES, columns))
@@ -676,8 +715,8 @@
         sums,
         own,
         factor,
+        factor_end,
         stacked(prolong_table),
-        residual,
         before,
         after,
         edge,
@@ -686,16 +725,19 @@
         inverse,
         forward,
         backward,
+        begun,
         smem=1,
-        hbm=(3,),
+        hbm=(3, 4, 14),
         hbm_out=(0, 1),
         scratch=(
             shape(8, 2, EXD * NODES, columns),
             shape(17, FIELDS, width),
             shape(16, FIELDS, width),
             factor,
+            factor_end,
         ),
-        copies=2 * EXD * NODES + EXD + 1,
+        copies=4 + EXD,
+        aliases={14: 0},
         flops=8e8,
     )
     return (residual_out, correction)

time: 111 us -> 110 us (level)
  waiting for transfers between devices: 22.6 us -> 17.6 us
  local copies, waits for them, and re-layouts: 5.6 us -> 8.27 us
  matrix products: 2.48 us -> 3.95 us
    slice x0 -> x2, local copies, waits for them, and re-layouts: none -> 3.4 us  [the longest x1 1.98 us: shards(): turned[:, :, 2 * LANES:].reshape(EXD + 1, line_size, 8, -1)]
    all_to_all x1, waiting for transfers between devices: 12.8 us -> 9.44 us  [over_z(): lax.all_to_all(blocks, 'modes', split_axis=0, concat_axis=0, axis_index_g...]
    pad x1, local copies, waits for them, and re-layouts: 1.79 us -> 0.02 us  [shards(): factor_end = jnp.pad(factor_end, ((0, 0),) * 3 + ((0, LANES - line_size),))]
    reshape x0 -> x1, local copies, waits for them, and re-layouts: none -> 1.58 us  [shards(): turned[:, :, 2 * LANES:].reshape(EXD + 1, line_size, 8, -1)]
    unnamed x58 -> x40, local copies, waits for them, and re-layouts: 2.88 us -> 1.47 us
  transfers between devices with their start and end apart: 6 -> 6, of which waited for: 4 -> 3; matrix products, arithmetic and copies ran while one was open for 8% -> 11% of each run, Pallas kernels for 1% -> 2%
where the time goes in v3:
time: 110 us
  starting transfers between devices  35.9 us (33%)
  blocking collectives  32.9 us (30%)
  waiting for transfers between devices  17.6 us (16%)
  Pallas kernels  8.57 us (8%)
  local copies, waits for them, and re-layouts  8.27 us (8%)
  matrix products  3.95 us (4%)
  other arithmetic  1.48 us (1%)
    all_to_all x1, blocking collectives, over_z(): lax.all_to_all(blocks, 'modes', split_axis=0, concat_axis=0, axis_index_g...  32.9 us
    all_to_all x1, starting transfers between devices, over_z(): lax.all_to_all(blocks, 'modes', split_axis=0, concat_axis=0, axis_index_g...  14.3 us
    all_to_all x1, waiting for transfers between devices, over_z(): lax.all_to_all(blocks, 'modes', split_axis=0, concat_axis=0, axis_index_g...  9.44 us
    pallas_call x7, Pallas kernels, call(): pl.pallas_call(kernel, out_shape=outs, in_specs=[pl.BlockSpec(memory_spac...  8.57 us
    ppermute x1, starting transfers between devices, shards(): after = lax.ppermute(to_last, 'dom', down)  7.15 us
    all_to_all x1, starting transfers between devices, shards(): sums = lax.all_to_all(block, 'dom', split_axis=0, concat_axis=0, tiled=True)  7.03 us
    ppermute x1, waiting for transfers between devices, shards(): before = lax.ppermute(to_next, 'dom', up)  6.37 us
    ppermute x1, starting transfers between devices, applied_rows(): lax.ppermute(along_x[UNIQUE], 'dom', [(i, (i + 1) % count) for i in range...  3.4 us
  transfers between devices with their start and end apart: 6, of which 3 were waited for; matrix products, arithmetic and copies ran while one was open for 11% of the time, Pallas kernels for 2%

profile of v3, /device:TPU:96, one launch (start us, length us, event | category | flops | bytes accessed | tf_op | source)
XLA Modules:
  0.0 109.6 jit_solution(5652208273386658033)
XLA Ops:
  0.7 1.1 copy-done.4
  1.8 0.9 shard_map.158
  2.7 14.3 %all-to-all-start = ((f32[16,56,128]{2,1,0:T(8,128)}), f32[16,56,128]{2,1,0:T(8,128)S(1)}, u32[]{:S(2)}, u32[]{:S(2)}) async-start(f32[16,56,128]{2,1,0:T(8,128)} %shard_map.158), calls=%async_computation | async-start | bytes 917504 | tf_op jit(solution)/shard_map/all_to_all | solution.py:599
  17.3 1.7 %fusion.1 = f32[29,16,256]{2,0,1:T(8,128)} fusion(f32[29,32,1]{1,0,2:T(8,128)S(1)} %copy-done.12, f32[32,16,256]{2,1,0:T(8,128)S(1)} %bitcast.25), kind=kOutput, calls=%fused_computation.2 | convolution fusion | flops 45613056 | bytes 1003136 | tf_op jit(solution)/shard_map/ur,rfy->ufy/dot_general | solution.py:571
  19.0 0.9 slice.21
  19.9 3.4 %collective-permute-start = (f32[16,256]{1,0:T(8,128)S(1)}, f32[16,256]{1,0:T(8,128)S(1)}, u32[]{:S(2)}, u32[]{:S(2)}) collective-permute-start(f32[16,256]{1,0:T(8,128)S(1)} %bitcast.32), channel_id=1, source_target_pairs={{0,1},{1,2},{2,3},{3,4},{4,5},{5,6},{6,7},{7,8},{8,9},{9,10},{10,1... | collective-permute-start | bytes 49160 | tf_op jit(solution)/shard_map/ppermute | solution.py:573
  23.6 0.8 add_divide_fusion.refs_1_.refs_11_
  24.4 0.5 iota_compare_fusion
  24.9 2.0 %slice.24 = f32[165,8,8]{2,1,0:T(8,128)} slice(f32[165,8,264]{2,1,0:T(8,128)} %bitcast.29), slice={[0:165], [0:8], [256:264]} | slice | bytes 84480 | tf_op jit(solution)/shard_map/slice | solution.py:614
  26.9 1.4 %slice.23.refs_1_.refs_3_ = f32[165,8,256]{2,1,0:T(8,128)S(1)} slice(f32[165,8,264]{2,1,0:T(8,128)} %bitcast.30), slice={[0:165], [0:8], [0:256]} | slice | bytes 2703360 | tf_op jit(solution)/shard_map/slice | solution.py:613
  28.4 0.8 slice.22
  29.2 1.6 %copy.27 = f32[5,33,8,8]{1,2,0,3:T(8,128)S(1)} copy(f32[5,33,8,8]{3,2,1,0:T(8,128)} %bitcast.28) | data formatting | bytes 84480 | tf_op jit(solution)/shard_map/reshape | solution.py:614
  30.8 2.3 %fusion.5.applied_ref = f32[28,16,256]{2,1,0:T(8,128)S(1)} fusion(f32[28,16,256]{2,0,1:T(8,128)} %bitcast.24, f32[28,256]{1,0:T(8,128)S(1)} %broadcast_multiply_fusion, f32[16]{0:T(128)} %copy-done.16, f32[256]{0:T(256)S(1)} %copy-done.13, f32[16,256]{1,0:T(8,128)S(1)} %collective-permute-done, pred[28]{0:T(512)(128)(4,1)} %iota_compare_fusion, ...), kind=kOutput, calls=%fused_computation.7 | convolution fusion | flops 353239040 | bytes 2143436 | tf_op jit(solution)/shard_map/dot_general | solution.py:576
  33.1 9.4 %all-to-all-done.refs_1_ = f32[16,56,128]{2,1,0:T(8,128)S(1)} async-done(((f32[16,56,128]{2,1,0:T(8,128)}), f32[16,56,128]{2,1,0:T(8,128)S(1)}, u32[]{:S(2)}, u32[]{:S(2)}) %all-to-all-start) | async-done | bytes 458784 | tf_op jit(solution)/shard_map/all_to_all | solution.py:599
  43.0 2.1 %collective-permute-start.1 = (f32[16,56,128]{2,1,0:T(8,128)S(1)}, f32[16,56,128]{2,1,0:T(8,128)S(1)}, u32[]{:S(2)}, u32[]{:S(2)}) collective-permute-start(f32[16,56,128]{2,1,0:T(8,128)S(1)} %shard_map.159), channel_id=1, source_target_pairs={{0,16},{16,0},{32,48},{48,32},{64,80},{80,64},{96,112},{112,96},{1... | collective-permute-start | bytes 1376264 | tf_op jit(solution)/shard_map/ppermute | solution.py:646
  45.0 1.8 %collective-permute-done.1.refs_3_ = f32[16,56,128]{2,1,0:T(8,128)S(1)} collective-permute-done((f32[16,56,128]{2,1,0:T(8,128)S(1)}, f32[16,56,128]{2,1,0:T(8,128)S(1)}, u32[]{:S(2)}, u32[]{:S(2)}) %collective-permute-start.1) | collective-permute-done | bytes 458784 | tf_op jit(solution)/shard_map/ppermute | solution.py:646
  47.3 32.9 %all_to_all.15.x_ref = f32[16,56,128]{2,1,0:T(8,128)S(1)} all-to-all(f32[16,56,128]{2,1,0:T(8,128)S(1)} %shard_map.160), channel_id=1, replica_groups={{0,32,64,96,128,160,192,224,256,288,320,352,384,416,448,480},{16,48,80,..., dimensions={0} | all-to-all | bytes 917504 | tf_op jit(solution)/shard_map/all_to_all | solution.py:599
  80.4 1.6 %shard_map.162 = (f32[16,24,128]{2,1,0:T(8,128)}, f32[16,128]{1,0:T(8,128)S(1)}) custom-call(f32[28,16,256]{2,1,0:T(8,128)S(1)} %get-tuple-element.21.refs_0_, f32[165,8,256]{2,1,0:T(8,128)S(1)} %slice.23.refs_1_.refs_3_, f32[8,5,8,128]{3,2,1,0:T(8,128)S(1)} %pad.4.refs_2_.refs_4_, bf16[512,128]{1,0:T(8,128)(2,1)S(1)} %copy-done.8), custom_call_target="tpu_custom_call" | custom-call | flops 30000000 | bytes 2310144 | tf_op jit(solution)/shard_map/pallas_call | solution.py:539
  82.0 7.0 %all-to-all-start.2 = ((f32[16,24,128]{2,1,0:T(8,128)}), f32[16,24,128]{2,1,0:T(8,128)S(1)}, u32[]{:S(2)}, u32[]{:S(2)}) async-start(f32[16,24,128]{2,1,0:T(8,128)} %get-tuple-element.27), calls=%async_computation.2 | async-start | bytes 393216 | tf_op jit(solution)/shard_map/all_to_all | solution.py:689
  89.1 7.1 %collective-permute-start.3 = (f32[9,16,256]{2,1,0:T(8,128)}, f32[9,16,256]{2,1,0:T(8,128)S(1)}, u32[]{:S(2)}, u32[]{:S(2)}) collective-permute-start(f32[9,16,256]{2,1,0:T(8,128)} %copy-done.9), channel_id=1, source_target_pairs={{1,0},{2,1},{3,2},{4,3},{5,4},{6,5},{7,6},{8,7},{9,8},{10,9},{11,1... | collective-permute-start | bytes 442376 | tf_op jit(solution)/shard_map/ppermute | solution.py:678
  96.2 1.9 %collective-permute-start.2 = (f32[8,16,256]{2,1,0:T(8,128)}, f32[8,16,256]{2,1,0:T(8,128)S(1)}, u32[]{:S(2)}, u32[]{:S(2)}) collective-permute-start(f32[8,16,256]{2,1,0:T(8,128)} %copy-done.10), channel_id=1, source_target_pairs={{0,1},{1,2},{2,3},{3,4},{4,5},{5,6},{6,7},{7,8},{8,9},{9,10},{10,1... | collective-permute-start | bytes 393224 | tf_op jit(solution)/shard_map/ppermute | solution.py:677
  98.2 2.1 %shard_map.163 = (f32[17,16,384]{2,1,0:T(8,128)S(1)}, f32[2,16,384]{2,1,0:T(8,128)S(1)}, f32[13,16,256]{2,1,0:T(8,128)S(1)}, f32[8,2,32,256]{3,2,1,0:T(8,128)}) custom-call(f32[28,16,256]{2,1,0:T(8,128)S(1)} %get-tuple-element.21.refs_0_, f32[10,16,384]{2,1,0:T(8,128)S(1)} %copy-done.3, bf16[512,384]{1,0:T(8,128)(2,1)S(1)} %copy-done.6, ...), custom_call_target="tpu_custom_call" | custom-call | flops 600000000 | bytes 2695168 | tf_op jit(solution)/shard_map/pallas_call | solution.py:539
  100.2 6.4 %collective-permute-done.2.refs_6_ = f32[8,16,256]{2,1,0:T(8,128)S(1)} collective-permute-done((f32[8,16,256]{2,1,0:T(8,128)}, f32[8,16,256]{2,1,0:T(8,128)S(1)}, u32[]{:S(2)}, u32[]{:S(2)}) %collective-permute-start.2) | collective-permute-done | bytes 131104 | tf_op jit(solution)/shard_map/ppermute | solution.py:677
  106.6 3.0 %shard_map.164 = (f32[8,2,32,256]{3,2,1,0:T(8,128)}, f32[8,2,32,256]{3,2,1,0:T(8,128)}) custom-call(s32[1]{0:T(128)} %bitcast.11.refs_0_, f32[16,24,128]{2,1,0:T(8,128)S(1)} %all-to-all-done.2.refs_1_, f32[16,128]{1,0:T(8,128)S(1)} %get-tuple-element.28.refs_2_, f32[165,8,256]{2,1,0:T(8,128)} %copy-done, ...), custom_call_target="tpu_custom_call", output_to_operand_aliasing={{0}: (14, {})} | custom-call | flops 800000000 | bytes 5414916 | tf_op jit(solution)/shard_map/pallas_call | solution.py:539
  (50 shorter events, 1.6 us)
Async XLA Ops:
  0.6 16.7 %copy-start.12 = (f32[29,32,1]{1,0,2:T(8,128)S(1)}, f32[29,32,1]{1,0,2:T(8,128)}, u32[]{:S(2)}) copy-start(f32[29,32,1]{1,0,2:T(8,128)} %constant.68) | copy-start | bytes 11140
  0.6 22.8 %copy-start.17 = (f32[10]{0:T(128)S(1)}, f32[10]{0:T(128)}, u32[]{:S(2)}) copy-start(f32[10]{0:T(128)} %constant.55.clone) | copy-start | bytes 124
  0.7 22.8 %copy-start.14 = (f32[384]{0:T(512)S(1)}, f32[384]{0:T(512)}, u32[]{:S(2)}) copy-start(f32[384]{0:T(512)} %constant.56.clone) | copy-start | bytes 4612
  0.7 22.9 %copy-start.13 = (f32[256]{0:T(256)S(1)}, f32[256]{0:T(256)}, u32[]{:S(2)}) copy-start(f32[256]{0:T(256)} %constant.54.clone) | copy-start | bytes 3076
  0.7 22.8 %copy-start.15 = (f32[28]{0:T(128)S(1)}, f32[28]{0:T(128)}, u32[]{:S(2)}) copy-start(f32[28]{0:T(128)} %constant.53.clone) | copy-start | bytes 340
  1.8 15.3 %copy-start.11 = (f32[8,2,32,256]{3,2,1,0:T(8,128)S(1)}, f32[8,2,32,256]{3,2,1,0:T(8,128)}, u32[]{:S(2)}) copy-start(f32[8,2,32,256]{3,2,1,0:T(8,128)} %param.16) | copy-start | bytes 1572868
  1.8 21.6 %copy-start.18 = (f32[8]{0:T(128)S(1)}, f32[8]{0:T(128)}, u32[]{:S(2)}) copy-start(f32[8]{0:T(128)} %param.17) | copy-start | bytes 100
  2.7 39.8 %all-to-all-start = ((f32[16,56,128]{2,1,0:T(8,128)}), f32[16,56,128]{2,1,0:T(8,128)S(1)}, u32[]{:S(2)}, u32[]{:S(2)}) async-start(f32[16,56,128]{2,1,0:T(8,128)} %shard_map.158), calls=%async_computation | async-start | bytes 917504 | tf_op jit(solution)/shard_map/all_to_all | solution.py:599
  19.9 10.9 %collective-permute-start = (f32[16,256]{1,0:T(8,128)S(1)}, f32[16,256]{1,0:T(8,128)S(1)}, u32[]{:S(2)}, u32[]{:S(2)}) collective-permute-start(f32[16,256]{1,0:T(8,128)S(1)} %bitcast.32), channel_id=1, source_target_pairs={{0,1},{1,2},{2,3},{3,4},{4,5},{5,6},{6,7},{7,8},{8,9},{9,10},{10,1... | collective-permute-start | bytes 49160 | tf_op jit(solution)/shard_map/ppermute | solution.py:573
  23.4 4.9 %copy-start.16 = (f32[16]{0:T(128)}, f32[16]{0:T(128)S(1)}, u32[]{:S(2)}) copy-start(f32[16]{0:T(128)S(1)} %mul.56) | copy-start | bytes 196
  28.3 52.0 %copy-start = (f32[165,8,256]{2,1,0:T(8,128)}, f32[165,8,256]{2,1,0:T(8,128)S(1)}, u32[]{:S(2)}) copy-start(f32[165,8,256]{2,1,0:T(8,128)S(1)} %slice.23.refs_1_.refs_3_) | copy-start | bytes 4055044
  28.4 14.2 %copy-start.1 = (bf16[2,2,2,256,256]{4,3,2,1,0:T(8,128)(2,1)S(1)}, bf16[2,2,2,256,256]{4,3,2,1,0:T(8,128)(2,1)}, u32[]{:S(2)}) copy-start(bf16[2,2,2,256,256]{4,3,2,1,0:T(8,128)(2,1)} %constant.57.clone.refs_2_) | copy-start | bytes 3145732
  30.8 49.6 %copy-start.2 = (f32[8,5,8,128]{3,2,1,0:T(8,128)}, f32[8,5,8,128]{3,2,1,0:T(8,128)S(1)}, u32[]{:S(2)}) copy-start(f32[8,5,8,128]{3,2,1,0:T(8,128)S(1)} %pad.4.refs_2_.refs_4_) | copy-start | bytes 491524
  43.0 37.4 %copy-start.8 = (bf16[512,128]{1,0:T(8,128)(2,1)S(1)}, bf16[512,128]{1,0:T(8,128)(2,1)}, u32[]{:S(2)}) copy-start(bf16[512,128]{1,0:T(8,128)(2,1)} %constant.58.clone.refs_3_) | copy-start | bytes 393220
  43.0 3.8 %collective-permute-start.1 = (f32[16,56,128]{2,1,0:T(8,128)S(1)}, f32[16,56,128]{2,1,0:T(8,128)S(1)}, u32[]{:S(2)}, u32[]{:S(2)}) collective-permute-start(f32[16,56,128]{2,1,0:T(8,128)S(1)} %shard_map.159), channel_id=1, source_target_pairs={{0,16},{16,0},{32,48},{48,32},{64,80},{80,64},{96,112},{112,96},{1... | collective-permute-start | bytes 1376264 | tf_op jit(solution)/shard_map/ppermute | solution.py:646
  47.3 50.9 %copy-start.3 = (f32[10,16,384]{2,1,0:T(8,128)S(1)}, f32[10,16,384]{2,1,0:T(8,128)}, u32[]{:S(2)}) copy-start(f32[10,16,384]{2,1,0:T(8,128)} %add_divide_fusion.refs_1_.refs_11_) | copy-start | bytes 737284
  47.3 50.9 %copy-start.5 = (bf16[768,256]{1,0:T(8,128)(2,1)S(1)}, bf16[768,256]{1,0:T(8,128)(2,1)}, u32[]{:S(2)}) copy-start(bf16[768,256]{1,0:T(8,128)(2,1)} %constant.60.clone.refs_3_.refs_13_) | copy-start | bytes 1179652
  47.3 50.9 %copy-start.6 = (bf16[512,384]{1,0:T(8,128)(2,1)S(1)}, bf16[512,384]{1,0:T(8,128)(2,1)}, u32[]{:S(2)}) copy-start(bf16[512,384]{1,0:T(8,128)(2,1)} %constant.59.clone.refs_2_.refs_12_) | copy-start | bytes 1179652
  80.3 1.7 %copy-start.9 = (f32[9,16,256]{2,1,0:T(8,128)}, f32[9,16,256]{2,1,0:T(8,128)S(1)}, u32[]{:S(2)}) copy-start(f32[9,16,256]{2,1,0:T(8,128)S(1)} %get-tuple-element.30) | copy-start | bytes 442372
  80.3 1.7 %copy-start.10 = (f32[8,16,256]{2,1,0:T(8,128)}, f32[8,16,256]{2,1,0:T(8,128)S(1)}, u32[]{:S(2)}) copy-start(f32[8,16,256]{2,1,0:T(8,128)S(1)} %get-tuple-element.29) | copy-start | bytes 393220
  80.4 26.3 %copy-start.7 = (bf16[256,256]{1,0:T(8,128)(2,1)S(1)}, bf16[256,256]{1,0:T(8,128)(2,1)}, u32[]{:S(2)}) copy-start(bf16[256,256]{1,0:T(8,128)(2,1)} %constant.61.clone.refs_5_) | copy-start | bytes 393220
  82.0 24.6 %all-to-all-start.2 = ((f32[16,24,128]{2,1,0:T(8,128)}), f32[16,24,128]{2,1,0:T(8,128)S(1)}, u32[]{:S(2)}, u32[]{:S(2)}) async-start(f32[16,24,128]{2,1,0:T(8,128)} %get-tuple-element.27), calls=%async_computation.2 | async-start | bytes 393216 | tf_op jit(solution)/shard_map/all_to_all | solution.py:689
  89.1 17.6 %collective-permute-start.3 = (f32[9,16,256]{2,1,0:T(8,128)}, f32[9,16,256]{2,1,0:T(8,128)S(1)}, u32[]{:S(2)}, u32[]{:S(2)}) collective-permute-start(f32[9,16,256]{2,1,0:T(8,128)} %copy-done.9), channel_id=1, source_target_pairs={{1,0},{2,1},{3,2},{4,3},{5,4},{6,5},{7,6},{8,7},{9,8},{10,9},{11,1... | collective-permute-start | bytes 442376 | tf_op jit(solution)/shard_map/ppermute | solution.py:678
  96.2 10.4 %collective-permute-start.2 = (f32[8,16,256]{2,1,0:T(8,128)}, f32[8,16,256]{2,1,0:T(8,128)S(1)}, u32[]{:S(2)}, u32[]{:S(2)}) collective-permute-start(f32[8,16,256]{2,1,0:T(8,128)} %copy-done.10), channel_id=1, source_target_pairs={{0,1},{1,2},{2,3},{3,4},{4,5},{5,6},{6,7},{7,8},{8,9},{9,10},{10,1... | collective-permute-start | bytes 393224 | tf_op jit(solution)/shard_map/ppermute | solution.py:677
  (1 other events, 1.1 us)

commit v4 on v3

--- a/solution.py
+++ b/solution.py
@@ -217,8 +217,14 @@
     return [(d, d // 4, d // 2 % 2, d % 2) for d in range(CHIPS)]
 
 
-def pack_kernel(x_ref, out_ref):
+def pack_kernel(x_hbm, out_hbm, x_ref, out_ref, sems):
     low = lane_index(8) < LANES // 2
+    loads = fetch(
+        [x_hbm.at[2 * i : 2 * i + 2] for i in range(8)], [x_ref.at[2 * i : 2 * i + 2] for i in range(8)], sems
+    )
+    for load in loads:
+        load.wait()
+    stores = []
     for d, element, half, side in chip_places():
         lanes = slice(half * LANES, (half + 1) * LANES)
         for step in range(3):
@@ -231,6 +237,11 @@
         else:
             mixed = jnp.where(low, swap_halves(first), second)
         out_ref[d, 48:56, :] = mixed
+        if d % 4 == 3:
+            blocks = slice(d - 3, d + 1)
+            stores += fetch((out_ref.at[blocks],), (out_hbm.at[blocks],), sems.at[8 + element :])
+    for store in stores:
+        store.wait()
 
 
 def fourier_kernel(kept, core_ref, x_ref, table_ref, *refs):
@@ -497,6 +508,7 @@
                 line = line + jnp.where(lane8 == b, total, 0.0)
             values.append(line)
     lines = dot3(jnp.concatenate(values, axis=0), prolong_ref)
+    line_up = []
     for row in range(EXD * NODES):
         element, n = row // NODES, row % NODES
         left = lines[16 * element : 16 * element + 16]
@@ -504,9 +516,12 @@
         u = 7 * element + n
         value = outer[u] if u < 8 else (inner_ref[u - 8] if u < 21 else outer[u - 13])
         value = value + left * float((1.0 - points[n]) / 2.0) + right * float((1.0 + points[n]) / 2.0)
-        for part in range(2):
-            out_ref[:, part, row, :] = value[8 * part : 8 * part + 8]
+        line_up.append(value)
         if n == NODES - 1:
+            whole = jnp.stack(line_up[-NODES:], axis=0)
+            for part in range(2):
+                at = slice(8 * part, 8 * part + 8)
+                out_ref[:, part, row - 7 : row + 1, :] = jnp.swapaxes(whole[:, at], 0, 1)
             rows = slice(NODES * element, NODES * element + NODES)
             stores.append(
                 pltpu.make_async_copy(
@@ -602,7 +617,13 @@
 
     blocks_shape = shape(CHIPS, ROWS, LANES)
     (packed,) = call(
-        pack_kernel, [blocks_shape], plane_load
+        pack_kernel,
+        [blocks_shape],
+        plane_load,
+        hbm=(0,),
+        hbm_out=(0,),
+        scratch=(plane_load, blocks_shape),
+        copies=8 + EXD,
     )
     planes_here = over_z(packed)
 

time: 110 us -> 110 us (level)
  no operation moved by 1% of the time
where the time goes in v4:
time: 110 us
  starting transfers between devices  35.9 us (33%)
  blocking collectives  32.9 us (30%)
  waiting for transfers between devices  17.6 us (16%)
  Pallas kernels  9.63 us (9%)
  local copies, waits for them, and re-layouts  7.22 us (7%)
  matrix products  3.95 us (4%)
  other arithmetic  1.48 us (1%)
    all_to_all x1, blocking collectives, over_z(): lax.all_to_all(blocks, 'modes', split_axis=0, concat_axis=0, axis_index_g...  32.9 us
    all_to_all x1, starting transfers between devices, over_z(): lax.all_to_all(blocks, 'modes', split_axis=0, concat_axis=0, axis_index_g...  14.3 us
    pallas_call x7, Pallas kernels, call(): pl.pallas_call(kernel, out_shape=outs, in_specs=[pl.BlockSpec(memory_spac...  9.63 us
    all_to_all x1, waiting for transfers between devices, over_z(): lax.all_to_all(blocks, 'modes', split_axis=0, concat_axis=0, axis_index_g...  9.42 us
    ppermute x1, starting transfers between devices, shards(): after = lax.ppermute(to_last, 'dom', down)  7.15 us
    all_to_all x1, starting transfers between devices, shards(): sums = lax.all_to_all(block, 'dom', split_axis=0, concat_axis=0, tiled=True)  7.04 us
    ppermute x1, waiting for transfers between devices, shards(): before = lax.ppermute(to_next, 'dom', up)  6.37 us
    ppermute x1, starting transfers between devices, applied_rows(): lax.ppermute(along_x[UNIQUE], 'dom', [(i, (i + 1) % count) for i in range...  3.41 us
  transfers between devices with their start and end apart: 6, of which 3 were waited for; matrix products, arithmetic and copies ran while one was open for 11% of the time, Pallas kernels for 2%

profile of v4, /device:TPU:96, one launch (start us, length us, event | category | flops | bytes accessed | tf_op | source)
XLA Modules:
  0.0 109.6 jit_solution(18188202981920485274)
XLA Ops:
  0.7 2.1 %shard_map.158 = f32[16,56,128]{2,1,0:T(8,128)} custom-call(f32[16,32,256]{2,1,0:T(8,128)} %x_hbm.1), custom_call_target="tpu_custom_call" | custom-call | flops 1000000 | bytes 983040 | tf_op jit(solution)/shard_map/pallas_call | solution.py:554
  2.8 14.3 %all-to-all-start = ((f32[16,56,128]{2,1,0:T(8,128)}), f32[16,56,128]{2,1,0:T(8,128)S(1)}, u32[]{:S(2)}, u32[]{:S(2)}) async-start(f32[16,56,128]{2,1,0:T(8,128)} %shard_map.158), calls=%async_computation | async-start | bytes 917504 | tf_op jit(solution)/shard_map/all_to_all | solution.py:614
  17.4 1.7 %fusion.1 = f32[29,16,256]{2,0,1:T(8,128)} fusion(f32[29,32,1]{1,0,2:T(8,128)S(1)} %copy-done.11, f32[32,16,256]{2,1,0:T(8,128)S(1)} %bitcast.25), kind=kOutput, calls=%fused_computation.2 | convolution fusion | flops 45613056 | bytes 1003136 | tf_op jit(solution)/shard_map/ur,rfy->ufy/dot_general | solution.py:586
  19.1 0.9 slice.21
  20.0 3.4 %collective-permute-start = (f32[16,256]{1,0:T(8,128)S(1)}, f32[16,256]{1,0:T(8,128)S(1)}, u32[]{:S(2)}, u32[]{:S(2)}) collective-permute-start(f32[16,256]{1,0:T(8,128)S(1)} %bitcast.32), channel_id=1, source_target_pairs={{0,1},{1,2},{2,3},{3,4},{4,5},{5,6},{6,7},{7,8},{8,9},{9,10},{10,1... | collective-permute-start | bytes 49160 | tf_op jit(solution)/shard_map/ppermute | solution.py:588
  23.7 0.8 add_divide_fusion.refs_1_.refs_11_
  24.5 0.5 iota_compare_fusion
  25.0 2.0 %slice.24 = f32[165,8,8]{2,1,0:T(8,128)} slice(f32[165,8,264]{2,1,0:T(8,128)} %bitcast.29), slice={[0:165], [0:8], [256:264]} | slice | bytes 84480 | tf_op jit(solution)/shard_map/slice | solution.py:635
  27.0 1.4 %slice.23.refs_1_.refs_3_ = f32[165,8,256]{2,1,0:T(8,128)S(1)} slice(f32[165,8,264]{2,1,0:T(8,128)} %bitcast.30), slice={[0:165], [0:8], [0:256]} | slice | bytes 2703360 | tf_op jit(solution)/shard_map/slice | solution.py:634
  28.5 0.8 slice.22
  29.3 1.6 %copy.27 = f32[5,33,8,8]{1,2,0,3:T(8,128)S(1)} copy(f32[5,33,8,8]{3,2,1,0:T(8,128)} %bitcast.28) | data formatting | bytes 84480 | tf_op jit(solution)/shard_map/reshape | solution.py:635
  30.9 2.3 %fusion.5.applied_ref = f32[28,16,256]{2,1,0:T(8,128)S(1)} fusion(f32[28,16,256]{2,0,1:T(8,128)} %bitcast.24, f32[28,256]{1,0:T(8,128)S(1)} %broadcast_multiply_fusion, f32[16]{0:T(128)} %copy-done.15, f32[256]{0:T(256)S(1)} %copy-done.12, f32[16,256]{1,0:T(8,128)S(1)} %collective-permute-done, pred[28]{0:T(512)(128)(4,1)} %iota_compare_fusion, ...), kind=kOutput, calls=%fused_computation.7 | convolution fusion | flops 353239040 | bytes 2143436 | tf_op jit(solution)/shard_map/dot_general | solution.py:591
  33.2 9.4 %all-to-all-done.refs_1_ = f32[16,56,128]{2,1,0:T(8,128)S(1)} async-done(((f32[16,56,128]{2,1,0:T(8,128)}), f32[16,56,128]{2,1,0:T(8,128)S(1)}, u32[]{:S(2)}, u32[]{:S(2)}) %all-to-all-start) | async-done | bytes 458784 | tf_op jit(solution)/shard_map/all_to_all | solution.py:614
  43.1 2.1 %collective-permute-start.1 = (f32[16,56,128]{2,1,0:T(8,128)S(1)}, f32[16,56,128]{2,1,0:T(8,128)S(1)}, u32[]{:S(2)}, u32[]{:S(2)}) collective-permute-start(f32[16,56,128]{2,1,0:T(8,128)S(1)} %shard_map.159), channel_id=1, source_target_pairs={{0,16},{16,0},{32,48},{48,32},{64,80},{80,64},{96,112},{112,96},{1... | collective-permute-start | bytes 1376264 | tf_op jit(solution)/shard_map/ppermute | solution.py:667
  45.1 1.8 %collective-permute-done.1.refs_3_ = f32[16,56,128]{2,1,0:T(8,128)S(1)} collective-permute-done((f32[16,56,128]{2,1,0:T(8,128)S(1)}, f32[16,56,128]{2,1,0:T(8,128)S(1)}, u32[]{:S(2)}, u32[]{:S(2)}) %collective-permute-start.1) | collective-permute-done | bytes 458784 | tf_op jit(solution)/shard_map/ppermute | solution.py:667
  46.9 0.4 shard_map.160
  47.4 32.9 %all_to_all.15.x_ref = f32[16,56,128]{2,1,0:T(8,128)S(1)} all-to-all(f32[16,56,128]{2,1,0:T(8,128)S(1)} %shard_map.160), channel_id=1, replica_groups={{0,32,64,96,128,160,192,224,256,288,320,352,384,416,448,480},{16,48,80,..., dimensions={0} | all-to-all | bytes 917504 | tf_op jit(solution)/shard_map/all_to_all | solution.py:614
  80.5 1.6 %shard_map.162 = (f32[16,24,128]{2,1,0:T(8,128)}, f32[16,128]{1,0:T(8,128)S(1)}) custom-call(f32[28,16,256]{2,1,0:T(8,128)S(1)} %get-tuple-element.21.refs_0_, f32[165,8,256]{2,1,0:T(8,128)S(1)} %slice.23.refs_1_.refs_3_, f32[8,5,8,128]{3,2,1,0:T(8,128)S(1)} %pad.4.refs_2_.refs_4_, bf16[512,128]{1,0:T(8,128)(2,1)S(1)} %copy-done.7), custom_call_target="tpu_custom_call" | custom-call | flops 30000000 | bytes 2310144 | tf_op jit(solution)/shard_map/pallas_call | solution.py:554
  82.1 7.0 %all-to-all-start.2 = ((f32[16,24,128]{2,1,0:T(8,128)}), f32[16,24,128]{2,1,0:T(8,128)S(1)}, u32[]{:S(2)}, u32[]{:S(2)}) async-start(f32[16,24,128]{2,1,0:T(8,128)} %get-tuple-element.27), calls=%async_computation.2 | async-start | bytes 393216 | tf_op jit(solution)/shard_map/all_to_all | solution.py:710
  89.2 7.1 %collective-permute-start.3 = (f32[9,16,256]{2,1,0:T(8,128)}, f32[9,16,256]{2,1,0:T(8,128)S(1)}, u32[]{:S(2)}, u32[]{:S(2)}) collective-permute-start(f32[9,16,256]{2,1,0:T(8,128)} %copy-done.8), channel_id=1, source_target_pairs={{1,0},{2,1},{3,2},{4,3},{5,4},{6,5},{7,6},{8,7},{9,8},{10,9},{11,1... | collective-permute-start | bytes 442376 | tf_op jit(solution)/shard_map/ppermute | solution.py:699
  96.3 1.9 %collective-permute-start.2 = (f32[8,16,256]{2,1,0:T(8,128)}, f32[8,16,256]{2,1,0:T(8,128)S(1)}, u32[]{:S(2)}, u32[]{:S(2)}) collective-permute-start(f32[8,16,256]{2,1,0:T(8,128)} %copy-done.9), channel_id=1, source_target_pairs={{0,1},{1,2},{2,3},{3,4},{4,5},{5,6},{6,7},{7,8},{8,9},{9,10},{10,1... | collective-permute-start | bytes 393224 | tf_op jit(solution)/shard_map/ppermute | solution.py:698
  98.3 2.1 %shard_map.163 = (f32[17,16,384]{2,1,0:T(8,128)S(1)}, f32[2,16,384]{2,1,0:T(8,128)S(1)}, f32[13,16,256]{2,1,0:T(8,128)S(1)}, f32[8,2,32,256]{3,2,1,0:T(8,128)}) custom-call(f32[28,16,256]{2,1,0:T(8,128)S(1)} %get-tuple-element.21.refs_0_, f32[10,16,384]{2,1,0:T(8,128)S(1)} %copy-done.3, bf16[512,384]{1,0:T(8,128)(2,1)S(1)} %copy-done.5, ...), custom_call_target="tpu_custom_call" | custom-call | flops 600000000 | bytes 2695168 | tf_op jit(solution)/shard_map/pallas_call | solution.py:554
  100.3 6.4 %collective-permute-done.2.refs_6_ = f32[8,16,256]{2,1,0:T(8,128)S(1)} collective-permute-done((f32[8,16,256]{2,1,0:T(8,128)}, f32[8,16,256]{2,1,0:T(8,128)S(1)}, u32[]{:S(2)}, u32[]{:S(2)}) %collective-permute-start.2) | collective-permute-done | bytes 131104 | tf_op jit(solution)/shard_map/ppermute | solution.py:698
  106.7 2.9 %shard_map.164 = (f32[8,2,32,256]{3,2,1,0:T(8,128)}, f32[8,2,32,256]{3,2,1,0:T(8,128)}) custom-call(s32[1]{0:T(128)} %bitcast.11.refs_0_, f32[16,24,128]{2,1,0:T(8,128)S(1)} %all-to-all-done.2.refs_1_, f32[16,128]{1,0:T(8,128)S(1)} %get-tuple-element.28.refs_2_, f32[165,8,256]{2,1,0:T(8,128)} %copy-done, ...), custom_call_target="tpu_custom_call", output_to_operand_aliasing={{0}: (14, {})} | custom-call | flops 800000000 | bytes 5414916 | tf_op jit(solution)/shard_map/pallas_call | solution.py:554
  (48 shorter events, 1.2 us)
Async XLA Ops:
  0.6 16.8 %copy-start.11 = (f32[29,32,1]{1,0,2:T(8,128)S(1)}, f32[29,32,1]{1,0,2:T(8,128)}, u32[]{:S(2)}) copy-start(f32[29,32,1]{1,0,2:T(8,128)} %constant.68) | copy-start | bytes 11140
  0.6 22.9 %copy-start.13 = (f32[384]{0:T(512)S(1)}, f32[384]{0:T(512)}, u32[]{:S(2)}) copy-start(f32[384]{0:T(512)} %constant.56.clone) | copy-start | bytes 4612
  0.7 22.9 %copy-start.16 = (f32[10]{0:T(128)S(1)}, f32[10]{0:T(128)}, u32[]{:S(2)}) copy-start(f32[10]{0:T(128)} %constant.55.clone) | copy-start | bytes 124
  0.7 22.9 %copy-start.12 = (f32[256]{0:T(256)S(1)}, f32[256]{0:T(256)}, u32[]{:S(2)}) copy-start(f32[256]{0:T(256)} %constant.54.clone) | copy-start | bytes 3076
  0.7 22.9 %copy-start.14 = (f32[28]{0:T(128)S(1)}, f32[28]{0:T(128)}, u32[]{:S(2)}) copy-start(f32[28]{0:T(128)} %constant.53.clone) | copy-start | bytes 340
  0.7 16.4 %copy-start.10 = (f32[8,2,32,256]{3,2,1,0:T(8,128)S(1)}, f32[8,2,32,256]{3,2,1,0:T(8,128)}, u32[]{:S(2)}) copy-start(f32[8,2,32,256]{3,2,1,0:T(8,128)} %param.16) | copy-start | bytes 1572868
  0.7 22.7 %copy-start.17 = (f32[8]{0:T(128)S(1)}, f32[8]{0:T(128)}, u32[]{:S(2)}) copy-start(f32[8]{0:T(128)} %param.17) | copy-start | bytes 100
  2.8 39.8 %all-to-all-start = ((f32[16,56,128]{2,1,0:T(8,128)}), f32[16,56,128]{2,1,0:T(8,128)S(1)}, u32[]{:S(2)}, u32[]{:S(2)}) async-start(f32[16,56,128]{2,1,0:T(8,128)} %shard_map.158), calls=%async_computation | async-start | bytes 917504 | tf_op jit(solution)/shard_map/all_to_all | solution.py:614
  20.0 10.9 %collective-permute-start = (f32[16,256]{1,0:T(8,128)S(1)}, f32[16,256]{1,0:T(8,128)S(1)}, u32[]{:S(2)}, u32[]{:S(2)}) collective-permute-start(f32[16,256]{1,0:T(8,128)S(1)} %bitcast.32), channel_id=1, source_target_pairs={{0,1},{1,2},{2,3},{3,4},{4,5},{5,6},{6,7},{7,8},{8,9},{9,10},{10,1... | collective-permute-start | bytes 49160 | tf_op jit(solution)/shard_map/ppermute | solution.py:588
  23.5 4.9 %copy-start.15 = (f32[16]{0:T(128)}, f32[16]{0:T(128)S(1)}, u32[]{:S(2)}) copy-start(f32[16]{0:T(128)S(1)} %mul.56) | copy-start | bytes 196
  28.4 52.0 %copy-start = (f32[165,8,256]{2,1,0:T(8,128)}, f32[165,8,256]{2,1,0:T(8,128)S(1)}, u32[]{:S(2)}) copy-start(f32[165,8,256]{2,1,0:T(8,128)S(1)} %slice.23.refs_1_.refs_3_) | copy-start | bytes 4055044
  28.5 14.2 %copy-start.1 = (bf16[2,2,2,256,256]{4,3,2,1,0:T(8,128)(2,1)S(1)}, bf16[2,2,2,256,256]{4,3,2,1,0:T(8,128)(2,1)}, u32[]{:S(2)}) copy-start(bf16[2,2,2,256,256]{4,3,2,1,0:T(8,128)(2,1)} %constant.57.clone.refs_2_) | copy-start | bytes 3145732
  30.9 49.6 %copy-start.2 = (f32[8,5,8,128]{3,2,1,0:T(8,128)}, f32[8,5,8,128]{3,2,1,0:T(8,128)S(1)}, u32[]{:S(2)}) copy-start(f32[8,5,8,128]{3,2,1,0:T(8,128)S(1)} %pad.4.refs_2_.refs_4_) | copy-start | bytes 491524
  43.1 37.4 %copy-start.7 = (bf16[512,128]{1,0:T(8,128)(2,1)S(1)}, bf16[512,128]{1,0:T(8,128)(2,1)}, u32[]{:S(2)}) copy-start(bf16[512,128]{1,0:T(8,128)(2,1)} %constant.58.clone.refs_3_) | copy-start | bytes 393220
  43.1 3.8 %collective-permute-start.1 = (f32[16,56,128]{2,1,0:T(8,128)S(1)}, f32[16,56,128]{2,1,0:T(8,128)S(1)}, u32[]{:S(2)}, u32[]{:S(2)}) collective-permute-start(f32[16,56,128]{2,1,0:T(8,128)S(1)} %shard_map.159), channel_id=1, source_target_pairs={{0,16},{16,0},{32,48},{48,32},{64,80},{80,64},{96,112},{112,96},{1... | collective-permute-start | bytes 1376264 | tf_op jit(solution)/shard_map/ppermute | solution.py:667
  47.4 50.9 %copy-start.3 = (f32[10,16,384]{2,1,0:T(8,128)S(1)}, f32[10,16,384]{2,1,0:T(8,128)}, u32[]{:S(2)}) copy-start(f32[10,16,384]{2,1,0:T(8,128)} %add_divide_fusion.refs_1_.refs_11_) | copy-start | bytes 737284
  47.4 50.9 %copy-start.4 = (bf16[768,256]{1,0:T(8,128)(2,1)S(1)}, bf16[768,256]{1,0:T(8,128)(2,1)}, u32[]{:S(2)}) copy-start(bf16[768,256]{1,0:T(8,128)(2,1)} %constant.60.clone.refs_3_.refs_13_) | copy-start | bytes 1179652
  47.4 50.9 %copy-start.5 = (bf16[512,384]{1,0:T(8,128)(2,1)S(1)}, bf16[512,384]{1,0:T(8,128)(2,1)}, u32[]{:S(2)}) copy-start(bf16[512,384]{1,0:T(8,128)(2,1)} %constant.59.clone.refs_2_.refs_12_) | copy-start | bytes 1179652
  80.4 1.7 %copy-start.8 = (f32[9,16,256]{2,1,0:T(8,128)}, f32[9,16,256]{2,1,0:T(8,128)S(1)}, u32[]{:S(2)}) copy-start(f32[9,16,256]{2,1,0:T(8,128)S(1)} %get-tuple-element.30) | copy-start | bytes 442372
  80.4 1.7 %copy-start.9 = (f32[8,16,256]{2,1,0:T(8,128)}, f32[8,16,256]{2,1,0:T(8,128)S(1)}, u32[]{:S(2)}) copy-start(f32[8,16,256]{2,1,0:T(8,128)S(1)} %get-tuple-element.29) | copy-start | bytes 393220
  80.5 26.3 %copy-start.6 = (bf16[256,256]{1,0:T(8,128)(2,1)S(1)}, bf16[256,256]{1,0:T(8,128)(2,1)}, u32[]{:S(2)}) copy-start(bf16[256,256]{1,0:T(8,128)(2,1)} %constant.61.clone.refs_5_) | copy-start | bytes 393220
  82.1 24.6 %all-to-all-start.2 = ((f32[16,24,128]{2,1,0:T(8,128)}), f32[16,24,128]{2,1,0:T(8,128)S(1)}, u32[]{:S(2)}, u32[]{:S(2)}) async-start(f32[16,24,128]{2,1,0:T(8,128)} %get-tuple-element.27), calls=%async_computation.2 | async-start | bytes 393216 | tf_op jit(solution)/shard_map/all_to_all | solution.py:710
  89.2 17.6 %collective-permute-start.3 = (f32[9,16,256]{2,1,0:T(8,128)}, f32[9,16,256]{2,1,0:T(8,128)S(1)}, u32[]{:S(2)}, u32[]{:S(2)}) collective-permute-start(f32[9,16,256]{2,1,0:T(8,128)} %copy-done.8), channel_id=1, source_target_pairs={{1,0},{2,1},{3,2},{4,3},{5,4},{6,5},{7,6},{8,7},{9,8},{10,9},{11,1... | collective-permute-start | bytes 442376 | tf_op jit(solution)/shard_map/ppermute | solution.py:699
  96.3 10.4 %collective-permute-start.2 = (f32[8,16,256]{2,1,0:T(8,128)}, f32[8,16,256]{2,1,0:T(8,128)S(1)}, u32[]{:S(2)}, u32[]{:S(2)}) collective-permute-start(f32[8,16,256]{2,1,0:T(8,128)} %copy-done.9), channel_id=1, source_target_pairs={{0,1},{1,2},{2,3},{3,4},{4,5},{5,6},{6,7},{7,8},{8,9},{9,10},{10,1... | collective-permute-start | bytes 393224 | tf_op jit(solution)/shard_map/ppermute | solution.py:698

commit v5 on v4

--- a/solution.py
+++ b/solution.py
@@ -398,16 +398,22 @@
 
 def inner_kernel(
     vectors, res_ref, inverse_ref, forward_ref, backward_ref, edge_ref, shared_ref, inner_ref,
-    residual_hbm, section_ref, parts_ref, sems,
+    residual_hbm, section_ref, parts_ref, turned_ref, sems,
 ):
     columns = res_ref.shape[2]
-    stores = []
-    for row in range(EXD * NODES - 1):
-        source = res_ref.at[7 * (row // NODES) + row % NODES]
+    for element in range(EXD - 1):
+        rows = res_ref[7 * element : 7 * element + NODES]
+        for part in range(2):
+            turned = jnp.swapaxes(rows[:, 8 * part : 8 * part + 8], 0, 1)
+            turned_ref[:, part, NODES * element : NODES * element + NODES, :] = turned
+    begin = slice(0, NODES * (EXD - 1))
+    stores = fetch((turned_ref,), (residual_hbm.at[:, :, begin, :],), sems)
+    for n in range(NODES - 1):
+        source = res_ref.at[UNIQUE - 7 + n]
         stores += fetch(
             [source.at[8 * part : 8 * part + 8] for part in range(2)],
-            [residual_hbm.at[:, part, row, :] for part in range(2)],
-            sems.at[2 * row : 2 * row + 2],
+            [residual_hbm.at[:, part, NODES * (EXD - 1) + n, :] for part in range(2)],
+            sems.at[1 + 2 * n : 3 + 2 * n],
         )
     width = forward_ref.shape[1]
     section = dot3(res_ref[...].reshape(UNIQUE * FIELDS, columns), forward_ref)
@@ -723,8 +729,12 @@
         forward,
         backward,
         hbm_out=(3,),
-        scratch=(shape(UNIQUE, FIELDS, width), shape(13, FIELDS, width)),
-        copies=2 * (EXD * NODES - 1),
+        scratch=(
+            shape(UNIQUE, FIELDS, width),
+            shape(13, FIELDS, width),
+            shape(8, 2, NODES * (EXD - 1), columns),
+        ),
+        copies=1 + 2 * (NODES - 1),
         flops=6e8,
     )
     prolong_table = np.zeros((LANES, columns))

time: 110 us -> 110 us (level)
  transfers between devices with their start and end apart: 6 -> 6, of which waited for: 3 -> 3; matrix products, arithmetic and copies ran while one was open for 11% -> 11% of each run, Pallas kernels for 2% -> 1%
where the time goes in v5:
time: 110 us
  starting transfers between devices  35.9 us (33%)
  blocking collectives  32.9 us (30%)
  waiting for transfers between devices  18.2 us (17%)
  Pallas kernels  9 us (8%)
  local copies, waits for them, and re-layouts  7.22 us (7%)
  matrix products  3.95 us (4%)
  other arithmetic  1.48 us (1%)
    all_to_all x1, blocking collectives, over_z(): lax.all_to_all(blocks, 'modes', split_axis=0, concat_axis=0, axis_index_g...  32.9 us
    all_to_all x1, starting transfers between devices, over_z(): lax.all_to_all(blocks, 'modes', split_axis=0, concat_axis=0, axis_index_g...  14.3 us
    all_to_all x1, waiting for transfers between devices, over_z(): lax.all_to_all(blocks, 'modes', split_axis=0, concat_axis=0, axis_index_g...  9.42 us
    pallas_call x7, Pallas kernels, call(): pl.pallas_call(kernel, out_shape=outs, in_specs=[pl.BlockSpec(memory_spac...  9 us
    ppermute x1, starting transfers between devices, shards(): after = lax.ppermute(to_last, 'dom', down)  7.15 us
    all_to_all x1, starting transfers between devices, shards(): sums = lax.all_to_all(block, 'dom', split_axis=0, concat_axis=0, tiled=True)  7.04 us
    ppermute x1, waiting for transfers between devices, shards(): before = lax.ppermute(to_next, 'dom', up)  7 us
    ppermute x1, starting transfers between devices, applied_rows(): lax.ppermute(along_x[UNIQUE], 'dom', [(i, (i + 1) % count) for i in range...  3.41 us
  transfers between devices with their start and end apart: 6, of which 3 were waited for; matrix products, arithmetic and copies ran while one was open for 11% of the time, Pallas kernels for 1%

profile of v5, /device:TPU:96, one launch (start us, length us, event | category | flops | bytes accessed | tf_op | source)
XLA Modules:
  0.0 109.6 jit_solution(18033266666264508404)
XLA Ops:
  0.7 2.1 %shard_map.158 = f32[16,56,128]{2,1,0:T(8,128)} custom-call(f32[16,32,256]{2,1,0:T(8,128)} %x_hbm.1), custom_call_target="tpu_custom_call" | custom-call | flops 1000000 | bytes 983040 | tf_op jit(solution)/shard_map/pallas_call | solution.py:560
  2.8 14.3 %all-to-all-start = ((f32[16,56,128]{2,1,0:T(8,128)}), f32[16,56,128]{2,1,0:T(8,128)S(1)}, u32[]{:S(2)}, u32[]{:S(2)}) async-start(f32[16,56,128]{2,1,0:T(8,128)} %shard_map.158), calls=%async_computation | async-start | bytes 917504 | tf_op jit(solution)/shard_map/all_to_all | solution.py:620
  17.4 1.7 %fusion.1 = f32[29,16,256]{2,0,1:T(8,128)} fusion(f32[29,32,1]{1,0,2:T(8,128)S(1)} %copy-done.11, f32[32,16,256]{2,1,0:T(8,128)S(1)} %bitcast.25), kind=kOutput, calls=%fused_computation.2 | convolution fusion | flops 45613056 | bytes 1003136 | tf_op jit(solution)/shard_map/ur,rfy->ufy/dot_general | solution.py:592
  19.1 0.9 slice.21
  20.0 3.4 %collective-permute-start = (f32[16,256]{1,0:T(8,128)S(1)}, f32[16,256]{1,0:T(8,128)S(1)}, u32[]{:S(2)}, u32[]{:S(2)}) collective-permute-start(f32[16,256]{1,0:T(8,128)S(1)} %bitcast.32), channel_id=1, source_target_pairs={{0,1},{1,2},{2,3},{3,4},{4,5},{5,6},{6,7},{7,8},{8,9},{9,10},{10,1... | collective-permute-start | bytes 49160 | tf_op jit(solution)/shard_map/ppermute | solution.py:594
  23.7 0.8 add_divide_fusion.refs_1_.refs_11_
  24.5 0.5 iota_compare_fusion
  25.0 2.0 %slice.24 = f32[165,8,8]{2,1,0:T(8,128)} slice(f32[165,8,264]{2,1,0:T(8,128)} %bitcast.29), slice={[0:165], [0:8], [256:264]} | slice | bytes 84480 | tf_op jit(solution)/shard_map/slice | solution.py:641
  27.0 1.4 %slice.23.refs_1_.refs_3_ = f32[165,8,256]{2,1,0:T(8,128)S(1)} slice(f32[165,8,264]{2,1,0:T(8,128)} %bitcast.30), slice={[0:165], [0:8], [0:256]} | slice | bytes 2703360 | tf_op jit(solution)/shard_map/slice | solution.py:640
  28.5 0.8 slice.22
  29.3 1.6 %copy.27 = f32[5,33,8,8]{1,2,0,3:T(8,128)S(1)} copy(f32[5,33,8,8]{3,2,1,0:T(8,128)} %bitcast.28) | data formatting | bytes 84480 | tf_op jit(solution)/shard_map/reshape | solution.py:641
  30.9 2.3 %fusion.5.applied_ref = f32[28,16,256]{2,1,0:T(8,128)S(1)} fusion(f32[28,16,256]{2,0,1:T(8,128)} %bitcast.24, f32[28,256]{1,0:T(8,128)S(1)} %broadcast_multiply_fusion, f32[16]{0:T(128)} %copy-done.15, f32[256]{0:T(256)S(1)} %copy-done.12, f32[16,256]{1,0:T(8,128)S(1)} %collective-permute-done, pred[28]{0:T(512)(128)(4,1)} %iota_compare_fusion, ...), kind=kOutput, calls=%fused_computation.7 | convolution fusion | flops 353239040 | bytes 2143436 | tf_op jit(solution)/shard_map/dot_general | solution.py:597
  33.2 9.4 %all-to-all-done.refs_1_ = f32[16,56,128]{2,1,0:T(8,128)S(1)} async-done(((f32[16,56,128]{2,1,0:T(8,128)}), f32[16,56,128]{2,1,0:T(8,128)S(1)}, u32[]{:S(2)}, u32[]{:S(2)}) %all-to-all-start) | async-done | bytes 458784 | tf_op jit(solution)/shard_map/all_to_all | solution.py:620
  43.1 2.1 %collective-permute-start.1 = (f32[16,56,128]{2,1,0:T(8,128)S(1)}, f32[16,56,128]{2,1,0:T(8,128)S(1)}, u32[]{:S(2)}, u32[]{:S(2)}) collective-permute-start(f32[16,56,128]{2,1,0:T(8,128)S(1)} %shard_map.159), channel_id=1, source_target_pairs={{0,16},{16,0},{32,48},{48,32},{64,80},{80,64},{96,112},{112,96},{1... | collective-permute-start | bytes 1376264 | tf_op jit(solution)/shard_map/ppermute | solution.py:673
  45.1 1.8 %collective-permute-done.1.refs_3_ = f32[16,56,128]{2,1,0:T(8,128)S(1)} collective-permute-done((f32[16,56,128]{2,1,0:T(8,128)S(1)}, f32[16,56,128]{2,1,0:T(8,128)S(1)}, u32[]{:S(2)}, u32[]{:S(2)}) %collective-permute-start.1) | collective-permute-done | bytes 458784 | tf_op jit(solution)/shard_map/ppermute | solution.py:673
  46.9 0.4 shard_map.160
  47.4 32.9 %all_to_all.15.x_ref = f32[16,56,128]{2,1,0:T(8,128)S(1)} all-to-all(f32[16,56,128]{2,1,0:T(8,128)S(1)} %shard_map.160), channel_id=1, replica_groups={{0,32,64,96,128,160,192,224,256,288,320,352,384,416,448,480},{16,48,80,..., dimensions={0} | all-to-all | bytes 917504 | tf_op jit(solution)/shard_map/all_to_all | solution.py:620
  80.5 1.6 %shard_map.162 = (f32[16,24,128]{2,1,0:T(8,128)}, f32[16,128]{1,0:T(8,128)S(1)}) custom-call(f32[28,16,256]{2,1,0:T(8,128)S(1)} %get-tuple-element.21.refs_0_, f32[165,8,256]{2,1,0:T(8,128)S(1)} %slice.23.refs_1_.refs_3_, f32[8,5,8,128]{3,2,1,0:T(8,128)S(1)} %pad.4.refs_2_.refs_4_, bf16[512,128]{1,0:T(8,128)(2,1)S(1)} %copy-done.7), custom_call_target="tpu_custom_call" | custom-call | flops 30000000 | bytes 2310144 | tf_op jit(solution)/shard_map/pallas_call | solution.py:560
  82.1 7.0 %all-to-all-start.2 = ((f32[16,24,128]{2,1,0:T(8,128)}), f32[16,24,128]{2,1,0:T(8,128)S(1)}, u32[]{:S(2)}, u32[]{:S(2)}) async-start(f32[16,24,128]{2,1,0:T(8,128)} %get-tuple-element.27), calls=%async_computation.2 | async-start | bytes 393216 | tf_op jit(solution)/shard_map/all_to_all | solution.py:716
  89.2 7.1 %collective-permute-start.3 = (f32[9,16,256]{2,1,0:T(8,128)}, f32[9,16,256]{2,1,0:T(8,128)S(1)}, u32[]{:S(2)}, u32[]{:S(2)}) collective-permute-start(f32[9,16,256]{2,1,0:T(8,128)} %copy-done.8), channel_id=1, source_target_pairs={{1,0},{2,1},{3,2},{4,3},{5,4},{6,5},{7,6},{8,7},{9,8},{10,9},{11,1... | collective-permute-start | bytes 442376 | tf_op jit(solution)/shard_map/ppermute | solution.py:705
  96.3 1.9 %collective-permute-start.2 = (f32[8,16,256]{2,1,0:T(8,128)}, f32[8,16,256]{2,1,0:T(8,128)S(1)}, u32[]{:S(2)}, u32[]{:S(2)}) collective-permute-start(f32[8,16,256]{2,1,0:T(8,128)} %copy-done.9), channel_id=1, source_target_pairs={{0,1},{1,2},{2,3},{3,4},{4,5},{5,6},{6,7},{7,8},{8,9},{9,10},{10,1... | collective-permute-start | bytes 393224 | tf_op jit(solution)/shard_map/ppermute | solution.py:704
  98.3 1.4 %shard_map.163 = (f32[17,16,384]{2,1,0:T(8,128)S(1)}, f32[2,16,384]{2,1,0:T(8,128)S(1)}, f32[13,16,256]{2,1,0:T(8,128)S(1)}, f32[8,2,32,256]{3,2,1,0:T(8,128)}) custom-call(f32[28,16,256]{2,1,0:T(8,128)S(1)} %get-tuple-element.21.refs_0_, f32[10,16,384]{2,1,0:T(8,128)S(1)} %copy-done.3, bf16[512,384]{1,0:T(8,128)(2,1)S(1)} %copy-done.5, ...), custom_call_target="tpu_custom_call" | custom-call | flops 600000000 | bytes 2695168 | tf_op jit(solution)/shard_map/pallas_call | solution.py:560
  99.7 7.0 %collective-permute-done.2.refs_6_ = f32[8,16,256]{2,1,0:T(8,128)S(1)} collective-permute-done((f32[8,16,256]{2,1,0:T(8,128)}, f32[8,16,256]{2,1,0:T(8,128)S(1)}, u32[]{:S(2)}, u32[]{:S(2)}) %collective-permute-start.2) | collective-permute-done | bytes 131104 | tf_op jit(solution)/shard_map/ppermute | solution.py:704
  106.7 2.9 %shard_map.164 = (f32[8,2,32,256]{3,2,1,0:T(8,128)}, f32[8,2,32,256]{3,2,1,0:T(8,128)}) custom-call(s32[1]{0:T(128)} %bitcast.11.refs_0_, f32[16,24,128]{2,1,0:T(8,128)S(1)} %all-to-all-done.2.refs_1_, f32[16,128]{1,0:T(8,128)S(1)} %get-tuple-element.28.refs_2_, f32[165,8,256]{2,1,0:T(8,128)} %copy-done, ...), custom_call_target="tpu_custom_call", output_to_operand_aliasing={{0}: (14, {})} | custom-call | flops 800000000 | bytes 5414916 | tf_op jit(solution)/shard_map/pallas_call | solution.py:560
  (48 shorter events, 1.2 us)
Async XLA Ops:
  0.6 16.8 %copy-start.11 = (f32[29,32,1]{1,0,2:T(8,128)S(1)}, f32[29,32,1]{1,0,2:T(8,128)}, u32[]{:S(2)}) copy-start(f32[29,32,1]{1,0,2:T(8,128)} %constant.68) | copy-start | bytes 11140
  0.6 22.9 %copy-start.13 = (f32[384]{0:T(512)S(1)}, f32[384]{0:T(512)}, u32[]{:S(2)}) copy-start(f32[384]{0:T(512)} %constant.56.clone) | copy-start | bytes 4612
  0.7 22.9 %copy-start.16 = (f32[10]{0:T(128)S(1)}, f32[10]{0:T(128)}, u32[]{:S(2)}) copy-start(f32[10]{0:T(128)} %constant.55.clone) | copy-start | bytes 124
  0.7 22.9 %copy-start.12 = (f32[256]{0:T(256)S(1)}, f32[256]{0:T(256)}, u32[]{:S(2)}) copy-start(f32[256]{0:T(256)} %constant.54.clone) | copy-start | bytes 3076
  0.7 22.9 %copy-start.14 = (f32[28]{0:T(128)S(1)}, f32[28]{0:T(128)}, u32[]{:S(2)}) copy-start(f32[28]{0:T(128)} %constant.53.clone) | copy-start | bytes 340
  0.7 16.4 %copy-start.10 = (f32[8,2,32,256]{3,2,1,0:T(8,128)S(1)}, f32[8,2,32,256]{3,2,1,0:T(8,128)}, u32[]{:S(2)}) copy-start(f32[8,2,32,256]{3,2,1,0:T(8,128)} %param.16) | copy-start | bytes 1572868
  0.7 22.7 %copy-start.17 = (f32[8]{0:T(128)S(1)}, f32[8]{0:T(128)}, u32[]{:S(2)}) copy-start(f32[8]{0:T(128)} %param.17) | copy-start | bytes 100
  2.8 39.8 %all-to-all-start = ((f32[16,56,128]{2,1,0:T(8,128)}), f32[16,56,128]{2,1,0:T(8,128)S(1)}, u32[]{:S(2)}, u32[]{:S(2)}) async-start(f32[16,56,128]{2,1,0:T(8,128)} %shard_map.158), calls=%async_computation | async-start | bytes 917504 | tf_op jit(solution)/shard_map/all_to_all | solution.py:620
  20.0 10.9 %collective-permute-start = (f32[16,256]{1,0:T(8,128)S(1)}, f32[16,256]{1,0:T(8,128)S(1)}, u32[]{:S(2)}, u32[]{:S(2)}) collective-permute-start(f32[16,256]{1,0:T(8,128)S(1)} %bitcast.32), channel_id=1, source_target_pairs={{0,1},{1,2},{2,3},{3,4},{4,5},{5,6},{6,7},{7,8},{8,9},{9,10},{10,1... | collective-permute-start | bytes 49160 | tf_op jit(solution)/shard_map/ppermute | solution.py:594
  23.5 4.9 %copy-start.15 = (f32[16]{0:T(128)}, f32[16]{0:T(128)S(1)}, u32[]{:S(2)}) copy-start(f32[16]{0:T(128)S(1)} %mul.56) | copy-start | bytes 196
  28.4 52.0 %copy-start = (f32[165,8,256]{2,1,0:T(8,128)}, f32[165,8,256]{2,1,0:T(8,128)S(1)}, u32[]{:S(2)}) copy-start(f32[165,8,256]{2,1,0:T(8,128)S(1)} %slice.23.refs_1_.refs_3_) | copy-start | bytes 4055044
  28.5 14.2 %copy-start.1 = (bf16[2,2,2,256,256]{4,3,2,1,0:T(8,128)(2,1)S(1)}, bf16[2,2,2,256,256]{4,3,2,1,0:T(8,128)(2,1)}, u32[]{:S(2)}) copy-start(bf16[2,2,2,256,256]{4,3,2,1,0:T(8,128)(2,1)} %constant.57.clone.refs_2_) | copy-start | bytes 3145732
  30.9 49.6 %copy-start.2 = (f32[8,5,8,128]{3,2,1,0:T(8,128)}, f32[8,5,8,128]{3,2,1,0:T(8,128)S(1)}, u32[]{:S(2)}) copy-start(f32[8,5,8,128]{3,2,1,0:T(8,128)S(1)} %pad.4.refs_2_.refs_4_) | copy-start | bytes 491524
  43.1 37.4 %copy-start.7 = (bf16[512,128]{1,0:T(8,128)(2,1)S(1)}, bf16[512,128]{1,0:T(8,128)(2,1)}, u32[]{:S(2)}) copy-start(bf16[512,128]{1,0:T(8,128)(2,1)} %constant.58.clone.refs_3_) | copy-start | bytes 393220
  43.1 3.8 %collective-permute-start.1 = (f32[16,56,128]{2,1,0:T(8,128)S(1)}, f32[16,56,128]{2,1,0:T(8,128)S(1)}, u32[]{:S(2)}, u32[]{:S(2)}) collective-permute-start(f32[16,56,128]{2,1,0:T(8,128)S(1)} %shard_map.159), channel_id=1, source_target_pairs={{0,16},{16,0},{32,48},{48,32},{64,80},{80,64},{96,112},{112,96},{1... | collective-permute-start | bytes 1376264 | tf_op jit(solution)/shard_map/ppermute | solution.py:673
  47.4 50.9 %copy-start.3 = (f32[10,16,384]{2,1,0:T(8,128)S(1)}, f32[10,16,384]{2,1,0:T(8,128)}, u32[]{:S(2)}) copy-start(f32[10,16,384]{2,1,0:T(8,128)} %add_divide_fusion.refs_1_.refs_11_) | copy-start | bytes 737284
  47.4 50.9 %copy-start.4 = (bf16[768,256]{1,0:T(8,128)(2,1)S(1)}, bf16[768,256]{1,0:T(8,128)(2,1)}, u32[]{:S(2)}) copy-start(bf16[768,256]{1,0:T(8,128)(2,1)} %constant.60.clone.refs_3_.refs_13_) | copy-start | bytes 1179652
  47.4 50.9 %copy-start.5 = (bf16[512,384]{1,0:T(8,128)(2,1)S(1)}, bf16[512,384]{1,0:T(8,128)(2,1)}, u32[]{:S(2)}) copy-start(bf16[512,384]{1,0:T(8,128)(2,1)} %constant.59.clone.refs_2_.refs_12_) | copy-start | bytes 1179652
  80.4 1.7 %copy-start.8 = (f32[9,16,256]{2,1,0:T(8,128)}, f32[9,16,256]{2,1,0:T(8,128)S(1)}, u32[]{:S(2)}) copy-start(f32[9,16,256]{2,1,0:T(8,128)S(1)} %get-tuple-element.30) | copy-start | bytes 442372
  80.4 1.7 %copy-start.9 = (f32[8,16,256]{2,1,0:T(8,128)}, f32[8,16,256]{2,1,0:T(8,128)S(1)}, u32[]{:S(2)}) copy-start(f32[8,16,256]{2,1,0:T(8,128)S(1)} %get-tuple-element.29) | copy-start | bytes 393220
  80.5 26.3 %copy-start.6 = (bf16[256,256]{1,0:T(8,128)(2,1)S(1)}, bf16[256,256]{1,0:T(8,128)(2,1)}, u32[]{:S(2)}) copy-start(bf16[256,256]{1,0:T(8,128)(2,1)} %constant.61.clone.refs_5_) | copy-start | bytes 393220
  82.1 24.6 %all-to-all-start.2 = ((f32[16,24,128]{2,1,0:T(8,128)}), f32[16,24,128]{2,1,0:T(8,128)S(1)}, u32[]{:S(2)}, u32[]{:S(2)}) async-start(f32[16,24,128]{2,1,0:T(8,128)} %get-tuple-element.27), calls=%async_computation.2 | async-start | bytes 393216 | tf_op jit(solution)/shard_map/all_to_all | solution.py:716
  89.2 17.6 %collective-permute-start.3 = (f32[9,16,256]{2,1,0:T(8,128)}, f32[9,16,256]{2,1,0:T(8,128)S(1)}, u32[]{:S(2)}, u32[]{:S(2)}) collective-permute-start(f32[9,16,256]{2,1,0:T(8,128)} %copy-done.8), channel_id=1, source_target_pairs={{1,0},{2,1},{3,2},{4,3},{5,4},{6,5},{7,6},{8,7},{9,8},{10,9},{11,1... | collective-permute-start | bytes 442376 | tf_op jit(solution)/shard_map/ppermute | solution.py:705
  96.3 10.4 %collective-permute-start.2 = (f32[8,16,256]{2,1,0:T(8,128)}, f32[8,16,256]{2,1,0:T(8,128)S(1)}, u32[]{:S(2)}, u32[]{:S(2)}) collective-permute-start(f32[8,16,256]{2,1,0:T(8,128)} %copy-done.9), channel_id=1, source_target_pairs={{0,1},{1,2},{2,3},{3,4},{4,5},{5,6},{6,7},{7,8},{8,9},{9,10},{10,1... | collective-permute-start | bytes 393224 | tf_op jit(solution)/shard_map/ppermute | solution.py:704
